TPU v7x, 32 devices: a whole 2x2x4 slice. The times are simulated.
32 devices in a mesh: ctx: 16 (over z, y, core), ws: 2 (over x).
Axes of the slice: x: 2, y: 2, z: 4, core: 2. Of those that a mesh axis runs over, the one named last changes fastest.
Arguments:
- layer_input: bfloat16 [16, 2, 128, 2048], P('ctx', 'ws'), may hold values from -6 to 6
- out_grad: bfloat16 [16, 2, 128, 2048], P('ctx', 'ws'), may hold values from -6 to 6
- seq_lengths: int32 [2], replicated, may hold values from 512 to 2048, as said below
- block_deal: int32 [32], replicated, may hold values from 0 to 31, as said below
- expert_routes: int32 [16, 2, 128, 8], P('ctx', 'ws'), may hold values from 0 to 15, all different within a row; in each aligned block of 128 rows (0 to 127, 128 to 255, ..., all dimensions but the last counted through in order) at most 80 rows name the same one
- attn_gain: float32 [2048], replicated, may hold values from 0.5 to 1.5
- query_gain: float32 [2048], replicated, may hold values from 0.5 to 1.5
- key_gain: float32 [2048], replicated, may hold values from 0.5 to 1.5
- ffn_gain: float32 [2048], replicated, may hold values from 0.5 to 1.5
- w_query: float32 [2048, 2048], P(('ctx', 'ws')), may hold values from -0.125 to 0.125
- w_key: float32 [2048, 2048], P(('ctx', 'ws')), may hold values from -0.125 to 0.125
- w_value: float32 [2048, 2048], P(('ctx', 'ws')), may hold values from -0.125 to 0.125
- w_out: float32 [2048, 2048], P(('ctx', 'ws')), may hold values from -0.75 to 0.75
- w_router: float32 [2048, 16], P(('ctx', 'ws')), may hold values from -0.0625 to 0.0625
- w_gate: float32 [16, 2048, 1024], P('ctx', 'ws'), may hold values from -0.125 to 0.125
- w_up: float32 [16, 2048, 1024], P('ctx', 'ws'), may hold values from -0.125 to 0.125
- w_down: float32 [16, 1024, 2048], P('ctx', 'ws'), may hold values from -12 to 12
Outputs:
- layer_out: bfloat16 [16, 2, 128, 2048], P('ctx', 'ws')
- grad_input: float32 [16, 2, 128, 2048], P('ctx', 'ws')
- grad_attn_gain: float32 [2048], P(('ctx', 'ws'))
- grad_query_gain: float32 [2048], P(('ctx', 'ws'))
- grad_key_gain: float32 [2048], P(('ctx', 'ws'))
- grad_ffn_gain: float32 [2048], P(('ctx', 'ws'))
- grad_w_query: float32 [2048, 2048], P(('ctx', 'ws'))
- grad_w_key: float32 [2048, 2048], P(('ctx', 'ws'))
- grad_w_value: float32 [2048, 2048], P(('ctx', 'ws'))
- grad_w_out: float32 [2048, 2048], P(('ctx', 'ws'))
- grad_w_router: float32 [2048, 16], P(('ctx', 'ws'))
- grad_w_gate: float32 [16, 2048, 1024], P('ctx', 'ws')
- grad_w_up: float32 [16, 2048, 1024], P('ctx', 'ws')
- grad_w_down: float32 [16, 1024, 2048], P('ctx', 'ws')
Inputs may be any that keep to these rules, and one draw needn't show every extreme that they name: `seq_lengths`: one slot, which one drawn from the seed, is live over all 2048 positions; the other over at least 512. `block_deal`: each block number appears once; entries 2 k and 2 k + 1 sum to 31. `expert_routes`: each token names 8 different experts. Of the 128 tokens of one device, at most 80 name any one expert, and on some device one expert is named by exactly 80.
All inputs are finite; a program needn't handle non-finite values.
Results may differ from a plain program's by a relative error of at most 0.02.
Values may be sent and summed in bfloat16 or wider, within the bound.
No kernel may reach another device: no remote copies, remote signals or barrier semaphores. Data moves between devices by JAX's collectives and lax.ppermute only.
A program may use at most 896 MiB of HBM per device.

v0:
```python
import math

import jax
import jax.numpy as jnp
from jax import lax
from jax.sharding import PartitionSpec as P

HD = 128
TOP = 8
EXP_DEV = 1
SLOTS = 2
HB = 32


NORM_EPS = 1e-05
ROPE_BASE = 10000.0
MASK_FLOOR = -1e30


def rms_norm(field, norm_gain):
    return field * lax.rsqrt(jnp.mean(field * field, axis=-1, keepdims=True) + NORM_EPS) * norm_gain


def rotate(field, positions):
    row_count = field.shape[0]
    head_count = field.shape[1] // HD
    half_dim = HD // 2
    shaped = field.reshape(row_count, head_count, HD)
    inv_freq = jnp.exp(jnp.arange(half_dim, dtype=jnp.float32) * (-2.0 * math.log(ROPE_BASE) / HD))
    angles = positions.astype(jnp.float32)[:, None] * inv_freq[None, :]
    cosine = jnp.cos(angles)[:, None, :]
    sine_part = jnp.sin(angles)[:, None, :]
    lead_half = shaped[..., :half_dim]
    tail_half = shaped[..., half_dim:]
    turned = jnp.concatenate(
        [lead_half * cosine - tail_half * sine_part, tail_half * cosine + lead_half * sine_part],
        axis=-1,
    )
    return turned.reshape(row_count, head_count * HD)


def swiglu(gate_pre, up_pre):
    return jax.nn.silu(gate_pre) * up_pre


def round_trip(field):
    return lax.optimization_barrier(field.astype(jnp.bfloat16)).astype(jnp.float32)


def table_lookup(lookup, indices):
    matches = indices[:, None] == jnp.arange(lookup.shape[0], dtype=jnp.int32)[None, :]
    return jnp.sum(jnp.where(matches, lookup[None, :], 0), axis=1)


def place_rows(indices, block_deal, ws_count):
    per_device = 2 * HB
    device = indices // per_device
    inner_row = indices % per_device
    ctx_pos = device // ws_count
    ws_pos = device % ws_count
    block_pick = inner_row // HB
    row_in = inner_row % HB
    block_num = table_lookup(block_deal, 2 * ctx_pos + block_pick)
    return block_num * (HB * ws_count) + ws_pos * HB + row_in


def split_heads(field, slots):
    head_count = field.shape[1] // HD
    return field.reshape(slots, field.shape[0] // slots, head_count, HD).transpose(0, 2, 1, 3)


def join_heads(field):
    return field.transpose(1, 0, 2).reshape(field.shape[1], field.shape[0] * field.shape[2])


def masked_scores(q_heads, k_heads, pos_query, pos_key, live_key):
    raw_score = jnp.einsum(
        "hqd,hkd->hqk", q_heads, k_heads, preferred_element_type=jnp.float32
    ) * HD ** (-0.5)
    visible = (pos_key[None, :] <= pos_query[:, None]) & live_key[None, :]
    return jnp.where(visible[None], raw_score, MASK_FLOOR)


def score_grads(
    q_heads, k_heads, v_heads, do_heads, log_total, delta, pos_query, pos_key, live_key
):
    scores = masked_scores(q_heads, k_heads, pos_query, pos_key, live_key)
    soft_prob = jnp.exp(scores - log_total)
    prob_low = soft_prob.astype(jnp.bfloat16)
    d_prob = jnp.einsum("hqd,hkd->hqk", do_heads, v_heads, preferred_element_type=jnp.float32)
    d_score = (soft_prob * (d_prob - delta)).astype(jnp.bfloat16)
    return (prob_low, d_score)


def local(
    layer_input,
    out_grad,
    seq_lengths,
    block_deal,
    expert_routes,
    attn_gain,
    query_gain,
    key_gain,
    ffn_gain,
    w_query,
    w_key,
    w_value,
    w_out,
    w_router,
    w_gate,
    w_up,
    w_down,
):
    low_type = jnp.bfloat16
    high_type = jnp.float32
    ws_count = lax.axis_size("ws")
    ctx_count = lax.axis_size("ctx")
    tokens = layer_input.shape[2]
    model_width = layer_input.shape[3]
    slot_rows = 2 * HB
    device = lax.axis_index("ctx") * ws_count + lax.axis_index("ws")
    experts = ctx_count * EXP_DEV
    mean_load = tokens * TOP // experts
    capacity = mean_load + max(1, mean_load // 4)
    score_scale = HD ** (-0.5)
    local_rows = jnp.arange(tokens, dtype=jnp.int32)
    slot_of = local_rows // slot_rows
    pos_query = place_rows(device * slot_rows + local_rows % slot_rows, block_deal, ws_count)
    live_query = pos_query < table_lookup(seq_lengths, slot_of)
    dense_low = (
        lax.all_gather(w_query.astype(low_type), ("ctx", "ws"), axis=0, tiled=True),
        lax.all_gather(w_key.astype(low_type), ("ctx", "ws"), axis=0, tiled=True),
        lax.all_gather(w_value.astype(low_type), ("ctx", "ws"), axis=0, tiled=True),
        lax.all_gather(w_out.astype(low_type), ("ctx", "ws"), axis=0, tiled=True),
        lax.all_gather(w_router.astype(low_type), ("ctx", "ws"), axis=0, tiled=True),
    )
    q_weight, k_weight, v_weight, o_weight, r_weight = dense_low
    expert_low = (
        lax.all_gather(w_gate.astype(low_type), "ws", axis=1, tiled=True),
        lax.all_gather(w_up.astype(low_type), "ws", axis=1, tiled=True),
        lax.all_gather(w_down.astype(low_type), "ws", axis=1, tiled=True),
    )
    g_weight = expert_low[0][0]
    u_weight = expert_low[1][0]
    d_weight = expert_low[2][0]
    input_f = layer_input.reshape(tokens, model_width).astype(high_type)
    attn_norm, attn_pull = jax.vjp(rms_norm, input_f, attn_gain)
    attn_in = attn_norm.astype(low_type)
    q_pre = jnp.dot(attn_in, q_weight, preferred_element_type=high_type)
    k_pre = jnp.dot(attn_in, k_weight, preferred_element_type=high_type)
    v_low = jnp.dot(attn_in, v_weight, preferred_element_type=high_type).astype(low_type)

    def qk_post(q_field, k_field, q_gain, k_gain):
        return (
            rotate(rms_norm(q_field, q_gain), pos_query),
            rotate(rms_norm(k_field, k_gain), pos_query),
        )

    (q_rot, k_rot), qk_pull = jax.vjp(qk_post, q_pre, k_pre, query_gain, key_gain)
    q_low = q_rot.astype(low_type)
    k_low = k_rot.astype(low_type)
    q_major = split_heads(q_low, SLOTS)
    k_major = split_heads(k_low, SLOTS)
    v_major = split_heads(v_low, SLOTS)
    keys_all, values_all = (
        lax.all_gather(k_major, ("ctx", "ws"), axis=2, tiled=True),
        lax.all_gather(v_major, ("ctx", "ws"), axis=2, tiled=True),
    )
    key_span = keys_all.shape[2]
    pos_key = place_rows(jnp.arange(key_span, dtype=jnp.int32), block_deal, ws_count)
    attn_parts = []
    attn_major = []
    log_parts = []
    for slot_id in range(SLOTS):
        lo_row = slot_id * slot_rows
        hi_row = lo_row + slot_rows
        live_key = pos_key < seq_lengths[slot_id]
        scores = masked_scores(
            q_major[slot_id], keys_all[slot_id], pos_query[lo_row:hi_row], pos_key, live_key
        )
        row_max = jnp.max(scores, axis=-1, keepdims=True)
        expo_vals = jnp.exp(scores - row_max)
        row_sum = jnp.sum(expo_vals, axis=-1, keepdims=True)
        prob_low = (expo_vals / row_sum).astype(low_type)
        slot_out = jnp.einsum(
            "hqk,hkd->hqd", prob_low, values_all[slot_id], preferred_element_type=high_type
        )
        attn_major.append(slot_out)
        attn_parts.append(join_heads(slot_out))
        log_parts.append((row_max + jnp.log(row_sum))[:, :, 0])
    attn_full = jnp.concatenate(attn_parts, axis=0)
    attn_low = attn_full.astype(low_type)
    resid_mid = input_f + jnp.dot(attn_low, o_weight, preferred_element_type=high_type)
    ffn_norm, ffn_pull = jax.vjp(rms_norm, resid_mid, ffn_gain)
    ffn_in = ffn_norm.astype(low_type)
    logits = jnp.dot(ffn_in, r_weight, preferred_element_type=high_type)
    router_prob = jax.nn.softmax(logits, axis=-1)
    route_local = expert_routes.reshape(tokens, TOP)
    route_hot = (
        route_local[:, :, None] == jnp.arange(experts, dtype=jnp.int32)[None, None, :]
    ).astype(high_type)
    gate_vals = jnp.sum(route_hot * router_prob[:, None, :], axis=-1)
    flat_route = route_local.reshape(tokens * TOP)
    hot_flat = (flat_route[:, None] == jnp.arange(experts, dtype=jnp.int32)[None, :]).astype(
        jnp.int32
    )
    slot_rank = jnp.sum((jnp.cumsum(hot_flat, axis=0) - 1) * hot_flat, axis=1)
    target = flat_route * capacity + slot_rank
    source = (
        jnp.full((experts * capacity,), tokens * TOP, jnp.int32)
        .at[target]
        .set(jnp.arange(tokens * TOP, dtype=jnp.int32))
    )
    padded_in = jnp.concatenate([ffn_in, jnp.zeros((1, model_width), low_type)], axis=0)
    send_buf = padded_in[source // TOP].reshape(experts, capacity, model_width)
    received = lax.all_to_all(send_buf, "ctx", split_axis=0, concat_axis=0, tiled=True)
    sources = received.shape[0]
    slot_count = received.shape[1]
    flat_rows = received.reshape(sources * slot_count, model_width)
    gate_pre = jnp.dot(flat_rows, g_weight, preferred_element_type=high_type)
    up_pre = jnp.dot(flat_rows, u_weight, preferred_element_type=high_type)
    hidden_low = swiglu(gate_pre, up_pre).astype(low_type)
    produced = jnp.dot(hidden_low, d_weight, preferred_element_type=high_type).astype(low_type)
    received, gate_kept, up_kept, produced = (
        received,
        gate_pre.reshape(sources, slot_count, -1),
        up_pre.reshape(sources, slot_count, -1),
        produced.reshape(sources, slot_count, model_width),
    )
    masked_grad = out_grad.reshape(tokens, model_width).astype(high_type) * live_query[
        :, None
    ].astype(high_type)
    d_copy = (
        (gate_vals[:, :, None] * masked_grad[:, None, :])
        .astype(low_type)
        .reshape(tokens * TOP, model_width)
    )
    padded_grad = jnp.concatenate([d_copy, jnp.zeros((1, model_width), low_type)], axis=0)
    d_send = padded_grad[source].reshape(experts, capacity, model_width)
    back_buf, d_recv = (
        lax.all_to_all(produced, "ctx", split_axis=0, concat_axis=0, tiled=True),
        lax.all_to_all(d_send, "ctx", split_axis=0, concat_axis=0, tiled=True),
    )
    copy_out = (
        back_buf.reshape(experts * capacity, model_width)[target]
        .reshape(tokens, TOP, model_width)
        .astype(high_type)
    )
    mixture = jnp.sum(gate_vals[:, :, None] * copy_out, axis=1)
    layer_out = (resid_mid + mixture).astype(low_type)
    d_gates = jnp.sum(copy_out * masked_grad[:, None, :], axis=-1)
    row_total = received.shape[0] * received.shape[1]
    routed_rows = received.reshape(row_total, model_width)
    d_produced = d_recv.reshape(row_total, model_width)
    hidden_val, hidden_pull = jax.vjp(
        swiglu, gate_kept.reshape(row_total, -1), up_kept.reshape(row_total, -1)
    )
    hidden_low = hidden_val.astype(low_type)
    d_w_down = jnp.einsum("cf,cd->fd", hidden_low, d_produced, preferred_element_type=high_type)
    d_hidden = jnp.einsum("cd,fd->cf", d_produced, d_weight, preferred_element_type=high_type)
    d_gate_pre, d_up_pre = hidden_pull(d_hidden)
    d_gate_low = d_gate_pre.astype(low_type)
    d_up_low = d_up_pre.astype(low_type)
    d_w_gate = jnp.einsum("cd,cf->df", routed_rows, d_gate_low, preferred_element_type=high_type)
    d_w_up = jnp.einsum("cd,cf->df", routed_rows, d_up_low, preferred_element_type=high_type)
    d_routed = (
        jnp.einsum("cf,df->cd", d_gate_low, g_weight, preferred_element_type=high_type)
        + jnp.einsum("cf,df->cd", d_up_low, u_weight, preferred_element_type=high_type)
    ).astype(low_type)
    d_back = lax.all_to_all(
        d_routed.reshape(received.shape[0], received.shape[1], model_width),
        "ctx",
        split_axis=0,
        concat_axis=0,
        tiled=True,
    )
    d_ffn_expert = jnp.sum(
        d_back.reshape(experts * capacity, model_width)[target]
        .reshape(tokens, TOP, model_width)
        .astype(high_type),
        axis=1,
    )
    q_back, k_back, v_back, o_back, r_back = dense_low
    d_router_prob = jnp.sum(route_hot * d_gates[:, :, None], axis=1)
    d_logits = (
        router_prob * (d_router_prob - jnp.sum(router_prob * d_router_prob, axis=-1, keepdims=True))
    ).astype(low_type)
    d_w_router = jnp.einsum("td,te->de", ffn_in, d_logits, preferred_element_type=high_type)
    d_ffn = d_ffn_expert + jnp.einsum(
        "te,de->td", d_logits, r_back, preferred_element_type=high_type
    )
    d_mid_norm, d_ffn_gain = ffn_pull(d_ffn)
    d_mid = masked_grad + d_mid_norm
    d_mid_low = d_mid.astype(low_type)
    d_w_out = jnp.einsum("td,te->de", attn_low, d_mid_low, preferred_element_type=high_type)
    d_attn_o = jnp.einsum("te,de->td", d_mid_low, o_back, preferred_element_type=high_type).astype(
        low_type
    )
    do_major = split_heads(d_attn_o, SLOTS)
    dq_parts = []
    slot_delta = []
    for slot_id in range(SLOTS):
        lo_row = slot_id * slot_rows
        hi_row = lo_row + slot_rows
        live_key = pos_key < seq_lengths[slot_id]
        delta_heads = jnp.sum(do_major[slot_id].astype(high_type) * attn_major[slot_id], axis=-1)
        unused_prob, d_score = score_grads(
            q_major[slot_id],
            keys_all[slot_id],
            values_all[slot_id],
            do_major[slot_id],
            log_parts[slot_id][:, :, None],
            delta_heads[:, :, None],
            pos_query[lo_row:hi_row],
            pos_key,
            live_key,
        )
        dq_heads = (
            jnp.einsum("hqk,hkd->hqd", d_score, keys_all[slot_id], preferred_element_type=high_type)
            * score_scale
        )
        dq_parts.append(join_heads(dq_heads))
        slot_delta.append(delta_heads)
    lse_stack = jnp.stack(log_parts, axis=0)
    delta_stack = jnp.stack(slot_delta, axis=0)
    dk_parts = []
    dv_parts = []
    q_ctx, do_ctx = (
        lax.all_gather(q_major, "ctx", axis=2, tiled=True),
        lax.all_gather(do_major, "ctx", axis=2, tiled=True),
    )
    lse_ctx, delta_ctx = (
        lax.all_gather(lse_stack, "ctx", axis=2, tiled=True),
        lax.all_gather(delta_stack, "ctx", axis=2, tiled=True),
    )
    query_span = q_ctx.shape[2]
    span_index = jnp.arange(query_span, dtype=jnp.int32)
    pos_pair_query = place_rows(
        (span_index // slot_rows * ws_count + lax.axis_index("ws")) * slot_rows
        + span_index % slot_rows,
        block_deal,
        ws_count,
    )
    pair_rows = ws_count * slot_rows
    pair_first = lax.axis_index("ctx") * pair_rows
    pos_pair_key = lax.dynamic_slice_in_dim(pos_key, pair_first, pair_rows, 0)
    pair_dk = []
    pair_dv = []
    for slot_id in range(SLOTS):
        pair_keys = lax.dynamic_slice_in_dim(keys_all[slot_id], pair_first, pair_rows, 1)
        pair_values = lax.dynamic_slice_in_dim(values_all[slot_id], pair_first, pair_rows, 1)
        pair_live = pos_pair_key < seq_lengths[slot_id]
        prob_pair, d_score_pair = score_grads(
            q_ctx[slot_id],
            pair_keys,
            pair_values,
            do_ctx[slot_id],
            lse_ctx[slot_id][:, :, None],
            delta_ctx[slot_id][:, :, None],
            pos_pair_query,
            pos_pair_key,
            pair_live,
        )
        pair_dk.append(
            jnp.einsum(
                "hqk,hqd->hkd", d_score_pair, q_ctx[slot_id], preferred_element_type=high_type
            )
            * score_scale
        )
        pair_dv.append(
            jnp.einsum("hqk,hqd->hkd", prob_pair, do_ctx[slot_id], preferred_element_type=high_type)
        )
    dk_summed, dv_summed = (
        lax.psum_scatter(
            jnp.stack(pair_dk, axis=0).astype(jnp.bfloat16), "ws", scatter_dimension=2, tiled=True
        ).astype(jnp.float32),
        lax.psum_scatter(
            jnp.stack(pair_dv, axis=0).astype(jnp.bfloat16), "ws", scatter_dimension=2, tiled=True
        ).astype(jnp.float32),
    )
    for slot_id in range(SLOTS):
        dk_parts.append(join_heads(dk_summed[slot_id]))
        dv_parts.append(join_heads(dv_summed[slot_id]))
    dq_all = jnp.concatenate(dq_parts, axis=0)
    dk_all = jnp.concatenate(dk_parts, axis=0)
    dv_low = jnp.concatenate(dv_parts, axis=0).astype(low_type)
    d_q_pre, d_k_pre, d_query_gain, d_key_gain = qk_pull((round_trip(dq_all), round_trip(dk_all)))
    dq_low = d_q_pre.astype(low_type)
    dk_low = d_k_pre.astype(low_type)
    d_w_query = jnp.einsum("td,te->de", attn_in, dq_low, preferred_element_type=high_type)
    d_w_key = jnp.einsum("td,te->de", attn_in, dk_low, preferred_element_type=high_type)
    d_w_value = jnp.einsum("td,te->de", attn_in, dv_low, preferred_element_type=high_type)
    d_attn_in = (
        jnp.einsum("te,de->td", dq_low, q_back, preferred_element_type=high_type)
        + jnp.einsum("te,de->td", dk_low, k_back, preferred_element_type=high_type)
        + jnp.einsum("te,de->td", dv_low, v_back, preferred_element_type=high_type)
    )
    d_input_norm, d_attn_gain = attn_pull(d_attn_in)
    grad_input = d_mid + d_input_norm
    dense_sums = (
        lax.psum_scatter(d_w_query, ("ctx", "ws"), scatter_dimension=0, tiled=True),
        lax.psum_scatter(d_w_key, ("ctx", "ws"), scatter_dimension=0, tiled=True),
        lax.psum_scatter(d_w_value, ("ctx", "ws"), scatter_dimension=0, tiled=True),
        lax.psum_scatter(d_w_out, ("ctx", "ws"), scatter_dimension=0, tiled=True),
        lax.psum_scatter(d_w_router, ("ctx", "ws"), scatter_dimension=0, tiled=True),
        lax.psum_scatter(d_attn_gain, ("ctx", "ws"), scatter_dimension=0, tiled=True),
        lax.psum_scatter(d_query_gain, ("ctx", "ws"), scatter_dimension=0, tiled=True),
        lax.psum_scatter(d_key_gain, ("ctx", "ws"), scatter_dimension=0, tiled=True),
        lax.psum_scatter(d_ffn_gain, ("ctx", "ws"), scatter_dimension=0, tiled=True),
    )
    expert_sums = (
        lax.psum_scatter(
            d_w_gate[None].astype(jnp.bfloat16), "ws", scatter_dimension=1, tiled=True
        ).astype(jnp.float32),
        lax.psum_scatter(
            d_w_up[None].astype(jnp.bfloat16), "ws", scatter_dimension=1, tiled=True
        ).astype(jnp.float32),
        lax.psum_scatter(
            d_w_down[None].astype(jnp.bfloat16), "ws", scatter_dimension=1, tiled=True
        ).astype(jnp.float32),
    )
    return (
        layer_out.reshape(1, 1, tokens, model_width),
        grad_input.reshape(1, 1, tokens, model_width),
        dense_sums[5],
        dense_sums[6],
        dense_sums[7],
        dense_sums[8],
        dense_sums[0],
        dense_sums[1],
        dense_sums[2],
        dense_sums[3],
        dense_sums[4],
        expert_sums[0],
        expert_sums[1],
        expert_sums[2],
    )


def solution(mesh):
    placed = (
        P("ctx", "ws", None, None),
        P("ctx", "ws", None, None),
        P(),
        P(),
        P("ctx", "ws", None, None),
        P(),
        P(),
        P(),
        P(),
        P(("ctx", "ws"), None),
        P(("ctx", "ws"), None),
        P(("ctx", "ws"), None),
        P(("ctx", "ws"), None),
        P(("ctx", "ws"), None),
        P("ctx", "ws", None),
        P("ctx", "ws", None),
        P("ctx", "ws", None),
    )
    return jax.shard_map(
        local,
        mesh=mesh,
        in_specs=placed,
        out_specs=(
            P("ctx", "ws", None, None),
            P("ctx", "ws", None, None),
            P(("ctx", "ws")),
            P(("ctx", "ws")),
            P(("ctx", "ws")),
            P(("ctx", "ws")),
            P(("ctx", "ws"), None),
            P(("ctx", "ws"), None),
            P(("ctx", "ws"), None),
            P(("ctx", "ws"), None),
            P(("ctx", "ws"), None),
            P("ctx", "ws", None),
            P("ctx", "ws", None),
            P("ctx", "ws", None),
        ),
        check_vma=False,
    )
```

profile of v0, /device:TPU:0, one launch (start us, length us, event | category | flops | bytes accessed | tf_op | source)
XLA Modules:
  0.0 3139.4 jit_solution(10190864478156714120)
XLA Ops:
  16.8 75.6 %all-gather.15.cloned.1.call-done = bf16[2048,2048]{1,0:T(8,128)(2,1)} async-done(((bf16[64,2048]{1,0:T(8,128)(2,1)}), bf16[2048,2048]{1,0:T(8,128)(2,1)}) %all-gather.15.cloned.1.call-update) | async-done | bytes 8388624 | tf_op jit(solution)/shard_map/all_gather | solution.py:132
  98.8 73.1 %all-gather.13.cloned.1.call-done = bf16[2048,2048]{1,0:T(8,128)(2,1)} async-done(((bf16[64,2048]{1,0:T(8,128)(2,1)}), bf16[2048,2048]{1,0:T(8,128)(2,1)}) %all-gather.13.cloned.1.call-update) | async-done | bytes 8388624 | tf_op jit(solution)/shard_map/all_gather | solution.py:131
  180.2 71.1 %all-gather.19.cloned.1.call-done = bf16[2048,2048]{1,0:T(8,128)(2,1)} async-done(((bf16[64,2048]{1,0:T(8,128)(2,1)}), bf16[2048,2048]{1,0:T(8,128)(2,1)}) %all-gather.19.cloned.1.call-update) | async-done | bytes 8388624 | tf_op jit(solution)/shard_map/all_gather | solution.py:133
  270.9 99.0 %all-gather.17.cloned.1.call-done = bf16[2,16,2048,128]{3,2,1,0:T(8,128)(2,1)} async-done(((bf16[2,16,64,128]{3,2,1,0:T(8,128)(2,1)}), bf16[2,16,2048,128]{3,2,1,0:T(8,128)(2,1)}) %all-gather.17.cloned.1.call-update) | async-done | bytes 16777232 | tf_op jit(solution)/shard_map/all_gather | solution.py:166
  381.0 107.8 %all-gather.21.cloned.1.call-done = bf16[2,16,2048,128]{3,2,1,0:T(8,128)(2,1)} async-done(((bf16[2,16,64,128]{3,2,1,0:T(8,128)(2,1)}), bf16[2,16,2048,128]{3,2,1,0:T(8,128)(2,1)}) %all-gather.21.cloned.1.call-update) | async-done | bytes 16777232 | tf_op jit(solution)/shard_map/all_gather | solution.py:167
  510.6 58.0 %all-gather.23.cloned.1.call-done = bf16[2048,2048]{1,0:T(8,128)(2,1)} async-done(((bf16[64,2048]{1,0:T(8,128)(2,1)}), bf16[2048,2048]{1,0:T(8,128)(2,1)}) %all-gather.23.cloned.1.call-update) | async-done | bytes 8388624 | tf_op jit(solution)/shard_map/all_gather | solution.py:134
  589.4 144.5 %all-gather = bf16[32,64,16]{1,2,0:T(8,128)(2,1)S(1)} all-gather(bf16[1,64,16]{1,2,0:T(8,128)(2,1)S(1)} %convert_bitcast_fusion.7), channel_id=1, replica_groups=mesh['ctx'=16,'ws'=2] {'ctx','ws'}, dimensions={0}, use_global_device_ids=true | all-gather | bytes 67584 | tf_op jit(solution)/shard_map/all_gather | solution.py:135
  751.7 16.8 all-to-all-start.2
  786.9 43.0 %all-gather.25.cloned.1.call-done = bf16[1,2048,1024]{2,1,0:T(8,128)(2,1)} async-done(((bf16[1,1024,1024]{2,1,0:T(8,128)(2,1)}), bf16[1,2048,1024]{2,1,0:T(8,128)(2,1)}) %all-gather.25.cloned.1.call-update) | async-done | bytes 4194320 | tf_op jit(solution)/shard_map/all_gather | solution.py:139
  840.0 48.4 %all-gather.29.cloned.1.call-done = bf16[1,1024,2048]{2,1,0:T(8,128)(2,1)} async-done(((bf16[1,512,2048]{2,1,0:T(8,128)(2,1)}), bf16[1,1024,2048]{2,1,0:T(8,128)(2,1)}) %all-gather.29.cloned.1.call-update) | async-done | bytes 4194320 | tf_op jit(solution)/shard_map/all_gather | solution.py:141
  888.4 15.2 multiply_convert_fusion.4
  933.6 129.5 %all-to-all-done.1 = bf16[16,80,2048]{2,1,0:T(8,128)(2,1)} async-done(((bf16[16,80,2048]{2,1,0:T(8,128)(2,1)}), bf16[16,80,2048]{2,1,0:T(8,128)(2,1)}, u32[]{:S(2)}, u32[]{:S(2)}) %all-to-all-start.1) | async-done | bytes 5242912 | tf_op jit(solution)/shard_map/all_to_all | solution.py:241
  1063.2 23.9 all-to-all-start.3
  1104.1 79.0 %all-to-all-done.3 = bf16[16,80,2048]{2,1,0:T(8,128)(2,1)} async-done(((bf16[16,80,2048]{2,1,0:T(8,128)(2,1)}), bf16[16,80,2048]{2,1,0:T(8,128)(2,1)}, u32[]{:S(2)}, u32[]{:S(2)}) %all-to-all-start.3) | async-done | bytes 5242912 | tf_op jit(solution)/shard_map/all_to_all | solution.py:270
  1212.7 48.9 %all_gather.53 = f32[2,16,1024]{1,0,2:T(2,128)S(1)} all-gather(f32[2,16,64]{1,0,2:T(2,128)S(1)} %copy.177), channel_id=1, replica_groups=mesh['ctx'=16,'ws'=2] {'ctx'}, dimensions={2}, use_global_device_ids=true | all-gather | bytes 139264 | tf_op jit(solution)/shard_map/all_gather | solution.py:333
  1299.3 22.0 all_gather.55
  1463.6 31.9 %reduce-scatter.27.cloned.1.call-done = bf16[1,1024,1024]{2,1,0:T(8,128)(2,1)} async-done(((bf16[1,2048,1024]{2,1,0:T(8,128)(2,1)}), bf16[1,1024,1024]{2,1,0:T(8,128)(2,1)}) %reduce-scatter.27.cloned.1.call-update) | async-done | bytes 2097168 | tf_op jit(solution)/shard_map/reduce_scatter | solution.py:415
  1499.5 52.9 %reduce-scatter.25.cloned.1.call-done = bf16[1,1024,1024]{2,1,0:T(8,128)(2,1)} async-done(((bf16[1,2048,1024]{2,1,0:T(8,128)(2,1)}), bf16[1,1024,1024]{2,1,0:T(8,128)(2,1)}) %reduce-scatter.25.cloned.1.call-update) | async-done | bytes 2097168 | tf_op jit(solution)/shard_map/reduce_scatter | solution.py:412
  1556.5 133.1 %reduce-scatter.31.cloned.1.call-done = f32[64,16]{1,0:T(8,128)} async-done(((f32[2048,16]{1,0:T(8,128)}), f32[64,16]{1,0:T(8,128)}) %reduce-scatter.31.cloned.1.call-update) | async-done | bytes 4112
  1707.2 38.6 %all-reduce.10 = (f32[2048]{0:T(1024)S(1)}, f32[2048]{0:T(1024)S(1)}, f32[2048]{0:T(1024)S(1)}, f32[2048]{0:T(1024)S(1)}) all-reduce(f32[2048]{0:T(1024)S(1)} %get-tuple-element.22, f32[2048]{0:T(1024)S(1)} %get-tuple-element.20, f32[2048]{0:T(1024)S(1)} %get-tuple-element.18, ...), channel_id=4, replica_groups=mesh['ctx'=16,'ws'=2] {'ctx','ws'}, use_global_device_ids=true, to_apply=%region_33.34.clone | all-reduce | flops 8192 | bytes 65536
  1749.4 297.7 %reduce-scatter.23.cloned.1.call-done = f32[64,2048]{1,0:T(8,128)} async-done(((f32[2048,2048]{1,0:T(8,128)}), f32[64,2048]{1,0:T(8,128)}) %reduce-scatter.23.cloned.1.call-update) | async-done | bytes 524304 | tf_op jit(solution)/shard_map/reduce_scatter | solution.py:404
  2047.0 361.9 %reduce-scatter.21.cloned.1.call-done = f32[64,2048]{1,0:T(8,128)} async-done(((f32[2048,2048]{1,0:T(8,128)}), f32[64,2048]{1,0:T(8,128)}) %reduce-scatter.21.cloned.1.call-update) | async-done | bytes 524304 | tf_op jit(solution)/shard_map/reduce_scatter | solution.py:403
  2409.0 361.4 %reduce-scatter.19.cloned.1.call-done = f32[64,2048]{1,0:T(8,128)} async-done(((f32[2048,2048]{1,0:T(8,128)}), f32[64,2048]{1,0:T(8,128)}) %reduce-scatter.19.cloned.1.call-update) | async-done | bytes 524304 | tf_op jit(solution)/shard_map/reduce_scatter | solution.py:402
  2770.4 361.2 %reduce-scatter.17.cloned.1.call-done = f32[64,2048]{1,0:T(8,128)} async-done(((f32[2048,2048]{1,0:T(8,128)}), f32[64,2048]{1,0:T(8,128)}) %reduce-scatter.17.cloned.1.call-update) | async-done | bytes 524304 | tf_op jit(solution)/shard_map/reduce_scatter | solution.py:401
  (401 shorter events, 427.0 us)
Async XLA Ops:
  8.0 84.4 %all-gather.15.cloned.1.call-start = ((), (), s32[]{:S(2)}) async-start(), calls=%async_computation.15 | async-start | bytes 8650752 | tf_op jit(solution)/shard_map/all_gather | solution.py:132
  9.9 162.0 %all-gather.13.cloned.1.call-start = ((), (), s32[]{:S(2)}) async-start(), calls=%async_computation.14 | async-start | bytes 8650752 | tf_op jit(solution)/shard_map/all_gather | solution.py:131
  11.7 239.7 %all-gather.19.cloned.1.call-start = ((), (), s32[]{:S(2)}) async-start(), calls=%async_computation.17 | async-start | bytes 8650752 | tf_op jit(solution)/shard_map/all_gather | solution.py:133
  13.6 356.3 %all-gather.17.cloned.1.call-start = ((), (), s32[]{:S(2)}) async-start(), calls=%async_computation.16 | async-start | bytes 17301504 | tf_op jit(solution)/shard_map/all_gather | solution.py:166
  180.2 308.6 %all-gather.21.cloned.1.call-start = ((), (), s32[]{:S(2)}) async-start(), calls=%async_computation.18 | async-start | bytes 17301504 | tf_op jit(solution)/shard_map/all_gather | solution.py:167
  257.2 311.5 %all-gather.23.cloned.1.call-start = ((), (), s32[]{:S(2)}) async-start(), calls=%async_computation.19 | async-start | bytes 8650752 | tf_op jit(solution)/shard_map/all_gather | solution.py:134
  580.8 171.0 %all-to-all-start = ((bf16[16,80,2048]{2,1,0:T(8,128)(2,1)}), bf16[16,80,2048]{2,1,0:T(8,128)(2,1)}, u32[]{:S(2)}, u32[]{:S(2)}) async-start(bf16[16,80,2048]{2,1,0:T(8,128)(2,1)} %bitcast.409), calls=%async_computation | async-start | bytes 10485760 | tf_op jit(solution)/shard_map/all_to_all | solution.py:216
  585.5 190.9 %all-gather.27.cloned.1.call-start = ((), (), s32[]{:S(2)}) async-start(), calls=%async_computation.21 | async-start | bytes 6291456 | tf_op jit(solution)/shard_map/all_gather | solution.py:140
  751.7 136.7 %all-to-all-start.2 = ((bf16[16,80,2048]{2,1,0:T(8,128)(2,1)}), bf16[16,80,2048]{2,1,0:T(8,128)(2,1)}, u32[]{:S(2)}, u32[]{:S(2)}) async-start(bf16[16,80,2048]{2,1,0:T(8,128)(2,1)} %bitcast.408), calls=%async_computation.2 | async-start | bytes 10485760 | tf_op jit(solution)/shard_map/all_to_all | solution.py:242
  772.5 115.9 %all-gather.29.cloned.1.call-start = ((), (), s32[]{:S(2)}) async-start(), calls=%async_computation.22 | async-start | bytes 6291456 | tf_op jit(solution)/shard_map/all_gather | solution.py:141
  911.0 152.1 %all-to-all-start.1 = ((bf16[16,80,2048]{2,1,0:T(8,128)(2,1)}), bf16[16,80,2048]{2,1,0:T(8,128)(2,1)}, u32[]{:S(2)}, u32[]{:S(2)}) async-start(bf16[16,80,2048]{2,1,0:T(8,128)(2,1)} %bitcast.419), calls=%async_computation.1 | async-start | bytes 10485760 | tf_op jit(solution)/shard_map/all_to_all | solution.py:241
  916.7 357.6 %all-gather.31.cloned.1.call-start = ((), (), s32[]{:S(2)}) async-start(), calls=%async_computation.23 | async-start | bytes 8912896 | tf_op jit(solution)/shard_map/all_gather | solution.py:329
  1063.2 119.9 %all-to-all-start.3 = ((bf16[16,80,2048]{2,1,0:T(8,128)(2,1)}), bf16[16,80,2048]{2,1,0:T(8,128)(2,1)}, u32[]{:S(2)}, u32[]{:S(2)}) async-start(bf16[16,80,2048]{2,1,0:T(8,128)(2,1)} %bitcast.418), calls=%async_computation.3 | async-start | bytes 10485760 | tf_op jit(solution)/shard_map/all_to_all | solution.py:270
  1087.1 235.4 %all-gather.33.cloned.1.call-start = ((), (), s32[]{:S(2)}) async-start(), calls=%async_computation.24 | async-start | bytes 8912896 | tf_op jit(solution)/shard_map/all_gather | solution.py:330
  1210.1 191.2 %reduce-scatter.15.cloned.1.call-start = ((), (), s32[]{:S(2)}) async-start(), calls=%async_computation.26 | async-start | bytes 1572864 | tf_op jit(solution)/shard_map/reduce_scatter | solution.py:377
  1340.3 93.7 %reduce-scatter.13.cloned.1.call-start = ((), (), s32[]{:S(2)}) async-start(), calls=%async_computation.25 | async-start | bytes 1572864 | tf_op jit(solution)/shard_map/reduce_scatter | solution.py:374
  1360.7 98.8 %reduce-scatter.29.cloned.1.call-start = ((), (), s32[]{:S(2)}) async-start(), calls=%async_computation.33 | async-start | bytes 6291456 | tf_op jit(solution)/shard_map/reduce_scatter | solution.py:418
  1370.9 124.6 %reduce-scatter.27.cloned.1.call-start = ((), (), s32[]{:S(2)}) async-start(), calls=%async_computation.32 | async-start | bytes 6291456 | tf_op jit(solution)/shard_map/reduce_scatter | solution.py:415
  1381.1 171.3 %reduce-scatter.25.cloned.1.call-start = ((), (), s32[]{:S(2)}) async-start(), calls=%async_computation.31 | async-start | bytes 6291456 | tf_op jit(solution)/shard_map/reduce_scatter | solution.py:412
  1391.5 298.1 %reduce-scatter.31.cloned.1.call-start = ((), (), s32[]{:S(2)}) async-start(), calls=%async_computation.34 | async-start | bytes 1081344
  1392.9 654.1 %reduce-scatter.23.cloned.1.call-start = ((), (), s32[]{:S(2)}) async-start(), calls=%async_computation.30 | async-start | bytes 17301504 | tf_op jit(solution)/shard_map/reduce_scatter | solution.py:404
  1401.2 1007.7 %reduce-scatter.21.cloned.1.call-start = ((), (), s32[]{:S(2)}) async-start(), calls=%async_computation.29 | async-start | bytes 17301504 | tf_op jit(solution)/shard_map/reduce_scatter | solution.py:403
  1410.9 1359.5 %reduce-scatter.19.cloned.1.call-start = ((), (), s32[]{:S(2)}) async-start(), calls=%async_computation.28 | async-start | bytes 17301504 | tf_op jit(solution)/shard_map/reduce_scatter | solution.py:402
  1447.7 1683.9 %reduce-scatter.17.cloned.1.call-start = ((), (), s32[]{:S(2)}) async-start(), calls=%async_computation.27 | async-start | bytes 17301504 | tf_op jit(solution)/shard_map/reduce_scatter | solution.py:401
  (85 other events, 3804.8 us)
Sparse Core Ops, SparseCore 0:
  12.4 79.9 all-gather.14
  96.0 75.8 all-gather.12
  175.5 75.8 all-gather.18
  254.8 114.9 all-gather.16
  373.3 115.3 all-gather.20
  492.2 76.4 all-gather.22
  920.3 137.1 all-gather.30
  1210.2 98.7 all-gather.32
Sparse Core Ops, SparseCore 1:
  589.5 57.8 all-gather.26
  772.6 57.2 all-gather.24
  831.8 56.6 all-gather.28
  1340.4 17.7 reduce-scatter.14
  1361.0 20.2 reduce-scatter.12
  1384.2 54.2 reduce-scatter.28
  1441.3 54.2 reduce-scatter.26
  1498.2 54.2 reduce-scatter.24
  1554.7 134.9 reduce-scatter.30
  1692.5 354.5 reduce-scatter.22
  2049.8 359.1 reduce-scatter.20
  2411.9 358.5 reduce-scatter.18
  2773.1 358.5 reduce-scatter.16
where the time goes:
time: 3150 us; the launch traced here: 3140 us
  waiting for transfers between devices  2390 us (76%)
  matrix products  261 us (8%)
  blocking collectives  254 us (8%)
  local copies, waits for them, and re-layouts  96.2 us (3%)
  other arithmetic  71.2 us (2%)
  starting transfers between devices  53.2 us (2%)
    reduce_scatter x1, waiting for transfers between devices, local(): lax.psum_scatter(d_w_value, ('ctx', 'ws'), scatter_dimension=0, tiled=True)  362 us
    reduce_scatter x1, waiting for transfers between devices, local(): lax.psum_scatter(d_w_key, ('ctx', 'ws'), scatter_dimension=0, tiled=True)  361 us
    reduce_scatter x1, waiting for transfers between devices, local(): lax.psum_scatter(d_w_query, ('ctx', 'ws'), scatter_dimension=0, tiled=True)  361 us
    reduce_scatter x1, waiting for transfers between devices, local(): lax.psum_scatter(d_w_out, ('ctx', 'ws'), scatter_dimension=0, tiled=True)  298 us
    all_gather x1, blocking collectives, local(): lax.all_gather(w_router.astype(low_type), ('ctx', 'ws'), axis=0, tiled=True)  145 us
    unnamed x22, waiting for transfers between devices  134 us
    all_to_all x1, waiting for transfers between devices, local(): lax.all_to_all(produced, 'ctx', split_axis=0, concat_axis=0, tiled=True)  130 us
    all_gather x1, waiting for transfers between devices, local(): lax.all_gather(v_major, ('ctx', 'ws'), axis=2, tiled=True)  108 us
  transfers between devices with their start and end apart: 25, of which 17 were waited for; matrix products, arithmetic and copies ran while one was open for 12% of the time, Pallas kernels for 0%

commit v1 on v0

v1 whole, which is shorter than its diff:
```python
import math

import jax
import jax.numpy as jnp
from jax import lax
from jax.sharding import PartitionSpec as P

HD = 128
SLOTS = 2

NORM_EPS = 1e-05
ROPE_BASE = 10000.0
MASK_FLOOR = -1e30

LOW = jnp.bfloat16
HIGH = jnp.float32


def dot(left, right, dims=((1,), (0,))):
    return lax.dot_general(left, right, (dims, ((), ())), preferred_element_type=HIGH)


def inv_rms(field):
    return lax.rsqrt(jnp.mean(field * field, axis=-1, keepdims=True) + NORM_EPS)


def rms_back(field, scale, d_hat):
    hat = field * scale
    return scale * (d_hat - hat * jnp.mean(d_hat * hat, axis=-1, keepdims=True))


def rope_tables(positions):
    half_dim = HD // 2
    inv_freq = jnp.exp(jnp.arange(half_dim, dtype=HIGH) * (-2.0 * math.log(ROPE_BASE) / HD))
    angles = positions.astype(HIGH)[:, None] * inv_freq[None, :]
    return jnp.cos(angles), jnp.sin(angles)


def rotate(field, cosine, sine):
    lead, tail = field[:, : HD // 2], field[:, HD // 2 :]
    return jnp.concatenate([lead * cosine - tail * sine, tail * cosine + lead * sine], axis=1)


def swap_ws(field):
    mine = lax.axis_index("ws")
    count = lax.axis_size("ws")
    if count != 2:
        return lax.all_to_all(field, "ws", 0, 0, tiled=True)
    own = lax.dynamic_index_in_dim(field, mine, 0, keepdims=False)
    away = lax.dynamic_index_in_dim(field, 1 - mine, 0, keepdims=False)
    came = lax.ppermute(away, "ws", [(0, 1), (1, 0)])
    first = mine == 0
    return jnp.stack([jnp.where(first, own, came), jnp.where(first, came, own)], axis=0)


def sum_ctx(field):
    count = lax.axis_size("ctx")
    if count & (count - 1):
        return lax.psum(field, "ctx")
    step = 1
    while step < count:
        field = field + lax.ppermute(field, "ctx", [(i, i ^ step) for i in range(count)])
        step *= 2
    return field


def gather_ctx(block):
    return lax.all_gather(block, "ctx", axis=0, tiled=True)


def scatter_ctx(field):
    return lax.psum_scatter(field, "ctx", scatter_dimension=0, tiled=True)


def local(
    layer_input,
    out_grad,
    seq_lengths,
    block_deal,
    expert_routes,
    attn_gain,
    query_gain,
    key_gain,
    ffn_gain,
    w_query,
    w_key,
    w_value,
    w_out,
    w_router,
    w_gate,
    w_up,
    w_down,
):
    ws_count = lax.axis_size("ws")
    ctx_count = lax.axis_size("ctx")
    c = lax.axis_index("ctx")
    w = lax.axis_index("ws")
    tokens, width = layer_input.shape[2:]
    heads = width // HD
    parts = ctx_count // heads
    head = c // parts
    part = c % parts
    own_part = c // heads
    slot_rows = tokens // SLOTS
    half_block = slot_rows // 2
    rows = w_query.shape[0]
    experts = w_router.shape[1]
    span = ctx_count * tokens
    part_span = span // parts

    starts = block_deal.reshape(ctx_count, 1, 2, 1) * (half_block * ws_count)
    in_block = jnp.arange(half_block, dtype=jnp.int32)
    pair_pos = starts + (
        jnp.arange(ws_count, dtype=jnp.int32)[None, :, None, None] * half_block + in_block
    )
    pos_slot = pair_pos.reshape(span)
    live_slot = pos_slot < seq_lengths[w]
    own_pos = lax.dynamic_index_in_dim(
        (starts + w * half_block + in_block)[:, 0], c, 0, keepdims=False
    ).reshape(1, slot_rows)
    live_own = (own_pos < seq_lengths[:, None]).reshape(tokens, 1)

    x = layer_input.reshape(tokens, width).astype(HIGH)
    x_scale = inv_rms(x)
    attn_in = (x * x_scale * attn_gain).astype(LOW)
    slot_in = gather_ctx(swap_ws(attn_in.reshape(SLOTS, slot_rows, width)).reshape(tokens, width))

    own_qkv = jnp.stack([w_query, w_key, w_value]).astype(LOW)
    by_head = own_qkv.reshape(3, rows, heads, HD).transpose(2, 1, 0, 3).reshape(heads, rows, 3 * HD)
    if parts > 1:
        by_head = jnp.repeat(by_head, parts, axis=0)
    head_rows = lax.all_to_all(by_head, "ctx", 0, 0, tiled=True)
    head_rows = lax.all_gather(head_rows, "ws", axis=1)
    w_head = head_rows.reshape(width, 3 * HD)

    o_weight = lax.all_gather(w_out.astype(LOW), ("ctx", "ws"), axis=0, tiled=True)
    r_weight = lax.all_gather(w_router.astype(LOW), ("ctx", "ws"), axis=0, tiled=True)
    g_weight = lax.all_gather(w_gate[0].astype(LOW), "ws", axis=0, tiled=True)
    u_weight = lax.all_gather(w_up[0].astype(LOW), "ws", axis=0, tiled=True)
    d_weight = lax.all_gather(w_down[0].astype(LOW), "ws", axis=0, tiled=True)
    grad_own = jnp.where(live_own, out_grad.reshape(tokens, width), 0).astype(LOW)
    grad_plane = gather_ctx(grad_own)
    routes = lax.all_gather(expert_routes.reshape(tokens, -1), "ctx", axis=0, tiled=True)

    qkv = dot(slot_in, w_head)
    q_pre, k_pre = qkv[:, :HD], qkv[:, HD : 2 * HD]
    v_low = qkv[:, 2 * HD :].astype(LOW)
    squares = sum_ctx(jnp.stack([jnp.sum(q_pre * q_pre, axis=1), jnp.sum(k_pre * k_pre, axis=1)]))
    qk_scale = lax.rsqrt(squares * (1.0 / (parts * width)) + NORM_EPS)
    q_hat = q_pre * qk_scale[0][:, None]
    k_hat = k_pre * qk_scale[1][:, None]
    q_gain = lax.dynamic_slice_in_dim(query_gain, head * HD, HD, 0)
    k_gain = lax.dynamic_slice_in_dim(key_gain, head * HD, HD, 0)
    cosine, sine = rope_tables(pos_slot)
    q_low = rotate(q_hat * q_gain, cosine, sine).astype(LOW)
    k_low = rotate(k_hat * k_gain, cosine, sine).astype(LOW)

    def of_part(field):
        if parts == 1:
            return field
        return lax.dynamic_slice_in_dim(field, part * part_span, part_span, 0)

    q_part = of_part(q_low)
    pos_query = of_part(pos_slot)
    score_scale = HD ** (-0.5)
    visible = (pos_slot[None, :] <= pos_query[:, None]) & live_slot[None, :]
    scores = jnp.where(visible, dot(q_part, k_low, ((1,), (1,))) * score_scale, MASK_FLOOR)
    row_max = jnp.max(scores, axis=1, keepdims=True)
    expo = jnp.exp(scores - row_max)
    row_sum = jnp.sum(expo, axis=1, keepdims=True)
    attn_head = dot((expo / row_sum).astype(LOW), v_low)
    log_total = row_max + jnp.log(row_sum)
    attn_head_low = attn_head.astype(LOW)

    out_chunks = attn_head_low.reshape(heads, tokens, HD)
    if parts > 1:
        out_chunks = lax.dynamic_update_slice_in_dim(
            jnp.zeros((ctx_count, tokens, HD), LOW), out_chunks, part * heads, 0
        )
    came = lax.all_to_all(out_chunks, "ctx", 0, 0, tiled=True)
    if parts > 1:
        came = lax.dynamic_index_in_dim(
            came.reshape(heads, parts, tokens, HD), own_part, 1, keepdims=False
        )
    attn_rows = came.transpose(1, 0, 2).reshape(ws_count, slot_rows, width)
    attn_low = swap_ws(attn_rows).reshape(tokens, width)

    mid = x + dot(attn_low, o_weight)
    mid_scale = inv_rms(mid)
    ffn_in = (mid * mid_scale * ffn_gain).astype(LOW)
    plane_in = gather_ctx(ffn_in)

    router_prob = jax.nn.softmax(dot(plane_in, r_weight), axis=-1)
    prob_own = lax.dynamic_slice_in_dim(router_prob, c, 1, 1)
    routed = jnp.any(routes == c, axis=1, keepdims=True)
    gate = jnp.where(routed, prob_own, 0.0)
    d_hidden_raw = dot(grad_plane, d_weight, ((1,), (1,)))
    gate_pre = dot(plane_in, g_weight)
    up_pre = dot(plane_in, u_weight)
    sigma = jax.nn.sigmoid(gate_pre)
    act = gate_pre * sigma
    hidden = (act * up_pre).astype(LOW)
    d_gate = jnp.where(
        routed, jnp.sum(hidden.astype(HIGH) * d_hidden_raw, axis=1, keepdims=True), 0.0
    )
    prob_sum = sum_ctx((prob_own * d_gate).reshape(-1, 128)).reshape(-1, 1)
    d_log = (prob_own * (d_gate - prob_sum)).astype(LOW)
    d_hidden = gate * d_hidden_raw
    d_gate_low = (d_hidden * up_pre * (sigma * (1.0 + gate_pre * (1.0 - sigma)))).astype(LOW)
    d_up_low = (d_hidden * act).astype(LOW)
    r_column = lax.dynamic_slice_in_dim(r_weight, c, 1, 1).reshape(1, width)
    d_copy = (
        dot(d_gate_low, g_weight, ((1,), (1,)))
        + dot(d_up_low, u_weight, ((1,), (1,)))
        + d_log.astype(HIGH) * r_column.astype(HIGH)
    ).astype(LOW)
    d_ffn = scatter_ctx(d_copy).astype(HIGH)

    produced = dot(hidden, d_weight).astype(LOW).astype(HIGH)
    mixture = scatter_ctx((gate * produced).astype(LOW)).astype(HIGH)
    layer_out = (mid + mixture).astype(LOW)

    hidden_gated = (gate * hidden.astype(HIGH)).astype(LOW)

    def expert_grad(left, right):
        total = dot(left, right, ((0,), (0,)))
        return lax.psum_scatter(
            total.astype(LOW), "ws", scatter_dimension=0, tiled=True
        ).astype(HIGH)[None]

    grad_w_down = expert_grad(hidden_gated, grad_plane)
    grad_w_gate = expert_grad(plane_in, d_gate_low)
    grad_w_up = expert_grad(plane_in, d_up_low)
    router_column = jnp.sum(plane_in.astype(HIGH) * d_log.astype(HIGH), axis=0)

    mid_hat = mid * mid_scale
    ffn_gain_part = jnp.sum(d_ffn * mid_hat, axis=0)
    d_mid = grad_own.astype(HIGH) + rms_back(mid, mid_scale, d_ffn * ffn_gain)
    d_mid_low = d_mid.astype(LOW)

    small = lax.all_gather(jnp.stack([ffn_gain_part, router_column]), ("ctx", "ws"), axis=0)
    small = lax.dynamic_slice_in_dim(small, (c * ws_count + w) * rows, rows, 2)
    grad_ffn_gain = jnp.sum(small[:, 0], axis=0)
    grad_w_router = jnp.sum(small[:, 1].reshape(experts, ws_count, rows), axis=1).T

    d_attn = dot(d_mid_low, o_weight, ((1,), (1,))).astype(LOW)
    d_attn_rows = swap_ws(d_attn.reshape(SLOTS, slot_rows, width)).reshape(tokens, heads, HD)
    in_chunks = d_attn_rows.transpose(1, 0, 2)
    if parts > 1:
        in_chunks = lax.dynamic_update_slice(
            jnp.zeros((heads, parts, tokens, HD), LOW), in_chunks[:, None], (0, own_part, 0, 0)
        ).reshape(ctx_count, tokens, HD)
    d_attn_head = lax.all_to_all(in_chunks, "ctx", 0, 0, tiled=True)
    if parts > 1:
        d_attn_head = lax.dynamic_slice_in_dim(d_attn_head, part * heads, heads, 0)
    d_attn_head = d_attn_head.reshape(part_span, HD)

    slot_d_mid = gather_ctx(
        swap_ws(d_mid_low.reshape(SLOTS, slot_rows, width)).reshape(tokens, width)
    )
    out_rows = dot(attn_head_low, of_part(slot_d_mid), ((0,), (0,)))
    if parts > 1:
        groups = [[h * parts + i for i in range(parts)] for h in range(heads)]
        out_rows = lax.psum_scatter(
            out_rows, "ctx", scatter_dimension=0, axis_index_groups=groups, tiled=True
        )
    grad_w_out = jnp.sum(swap_ws(out_rows.reshape(ws_count, rows, width)), axis=0)

    delta = jnp.sum(d_attn_head.astype(HIGH) * attn_head, axis=1, keepdims=True)
    prob = jnp.exp(
        jnp.where(visible, dot(q_part, k_low, ((1,), (1,))) * score_scale, MASK_FLOOR) - log_total
    )
    d_prob = dot(d_attn_head, v_low, ((1,), (1,)))
    d_score = (prob * (d_prob - delta)).astype(LOW)
    d_q_part = (dot(d_score, k_low) * score_scale).astype(LOW)
    d_k_rot = (dot(d_score, q_part, ((0,), (0,))) * score_scale).astype(LOW)
    d_v_low = dot(prob.astype(LOW), d_attn_head, ((0,), (0,))).astype(LOW)
    d_q_rot = d_q_part
    if parts > 1:
        d_q_rot = lax.dynamic_update_slice_in_dim(
            jnp.zeros((span, HD), LOW), d_q_part, part * part_span, 0
        )
    d_q_norm = rotate(d_q_rot.astype(HIGH), cosine, -sine)
    d_k_norm = rotate(d_k_rot.astype(HIGH), cosine, -sine)
    gain_parts = jnp.stack([jnp.sum(d_q_norm * q_hat, axis=0), jnp.sum(d_k_norm * k_hat, axis=0)])
    d_q_hat = d_q_norm * q_gain
    d_k_hat = d_k_norm * k_gain
    dots = sum_ctx(jnp.stack([jnp.sum(d_q_hat * q_hat, axis=1), jnp.sum(d_k_hat * k_hat, axis=1)]))
    dots = dots * (1.0 / (parts * width))
    d_q_low = (qk_scale[0][:, None] * (d_q_hat - q_hat * dots[0][:, None])).astype(LOW)
    d_k_low = (qk_scale[1][:, None] * (d_k_hat - k_hat * dots[1][:, None])).astype(LOW)
    d_qkv = jnp.concatenate([d_q_low, d_k_low, d_v_low], axis=1)

    d_in_sum = scatter_ctx(dot(d_qkv, w_head, ((1,), (1,))).astype(LOW))
    d_in = swap_ws(d_in_sum.reshape(ws_count, slot_rows, width)).reshape(tokens, width)
    grad_input = d_mid + rms_back(x, x_scale, d_in.astype(HIGH) * attn_gain)

    head_grad = dot(slot_in, d_qkv, ((0,), (0,))).astype(LOW)
    head_grad = head_grad.reshape(ctx_count, ws_count, rows, 3 * HD).transpose(1, 0, 2, 3)
    head_grad = jnp.sum(swap_ws(head_grad).astype(HIGH), axis=0).astype(LOW)
    col_grad = lax.all_to_all(head_grad, "ctx", 0, 0, tiled=True).astype(HIGH)
    if parts > 1:
        col_grad = jnp.sum(col_grad.reshape(heads, parts, rows, 3 * HD), axis=1)
    grads_qkv = col_grad.reshape(heads, rows, 3, HD).transpose(2, 1, 0, 3).reshape(3, rows, width)
    own_gain = lax.dynamic_slice_in_dim(attn_gain, (c * ws_count + w) * rows, rows, 0)
    grad_attn_gain = jnp.sum(grads_qkv * own_qkv.astype(HIGH), axis=(0, 2)) / own_gain

    if parts > 1:
        gain_parts = lax.psum_scatter(
            gain_parts, "ctx", scatter_dimension=1, axis_index_groups=groups, tiled=True
        )
    gain_rows = gain_parts.reshape(2, ws_count, rows).transpose(1, 0, 2)
    grad_qk_gain = jnp.sum(swap_ws(gain_rows), axis=0)

    return (
        layer_out.reshape(1, 1, tokens, width),
        grad_input.reshape(1, 1, tokens, width),
        grad_attn_gain,
        grad_qk_gain[0],
        grad_qk_gain[1],
        grad_ffn_gain,
        grads_qkv[0],
        grads_qkv[1],
        grads_qkv[2],
        grad_w_out,
        grad_w_router,
        grad_w_gate,
        grad_w_up,
        grad_w_down,
    )


def solution(mesh):
    rows = P("ctx", "ws", None, None)
    master = P(("ctx", "ws"), None)
    expert = P("ctx", "ws", None)
    gain = P(("ctx", "ws"))
    return jax.shard_map(
        local,
        mesh=mesh,
        in_specs=(rows, rows, P(), P(), rows) + (P(),) * 4 + (master,) * 5 + (expert,) * 3,
        out_specs=(rows, rows) + (gain,) * 4 + (master,) * 5 + (expert,) * 3,
        check_vma=False,
    )
```

time: 3150 us -> 1260 us (0.40)
  waiting for transfers between devices: 2390 us -> 679 us
  local copies, waits for them, and re-layouts: 96.2 us -> 24.4 us
  blocking collectives: 254 us -> 189 us
  matrix products: 261 us -> 225 us
    reduce_scatter x9 -> x6, waiting for transfers between devices: 1470 us -> 206 us  [the longest x3 195 us: scatter_ctx(): return lax.psum_scatter(field, 'ctx', scatter_dimension=0, tiled=True)]
    all_gather x11 -> x9, waiting for transfers between devices: 576 us -> 357 us  [the longest x4 222 us: gather_ctx(): return lax.all_gather(block, 'ctx', axis=0, tiled=True)]
    all_to_all x4 -> x3, waiting for transfers between devices: 208 us -> 32.7 us  [the longest x1 18.4 us: local(): head_rows = lax.all_to_all(by_head, 'ctx', 0, 0, tiled=True)]
    unnamed x22 -> x15, waiting for transfers between devices: 134 us -> 0.25 us
    ppermute x0 -> x20, waiting for transfers between devices: none -> 82.8 us  [the longest x8 59 us: swap_ws(): came = lax.ppermute(away, 'ws', [(0, 1), (1, 0)])]
    all_gather x3, blocking collectives: 215 us -> 163 us  [the longest x1 73.7 us: local(): lax.all_gather(jnp.stack([ffn_gain_part, router_column]), ('ctx', 'ws'),...]
    gather x4 -> x0, local copies, waits for them, and re-layouts: 43.7 us -> none  [the longest x1 13.6 us: local(): d_send = padded_grad[source].reshape(experts, capacity, model_width)]
    unnamed x1 -> x0, blocking collectives: 38.6 us -> none
  transfers between devices with their start and end apart: 25 -> 38, of which waited for: 17 -> 32; matrix products, arithmetic and copies ran while one was open for 12% -> 20% of each run, Pallas kernels for 0% -> 0%
where the time goes in v1:
time: 1260 us
  waiting for transfers between devices  679 us (54%)
  matrix products  225 us (18%)
  blocking collectives  189 us (15%)
  other arithmetic  86.3 us (7%)
  starting transfers between devices  38.4 us (3%)
  local copies, waits for them, and re-layouts  24.4 us (2%)
  between operations  15.6 us (1%)
    dot_general x22, matrix products, dot(): lax.dot_general(left, right, (dims, ((), ())), preferred_element_type=HIGH)  225 us
    all_gather x4, waiting for transfers between devices, gather_ctx(): return lax.all_gather(block, 'ctx', axis=0, tiled=True)  222 us
    reduce_scatter x3, waiting for transfers between devices, scatter_ctx(): return lax.psum_scatter(field, 'ctx', scatter_dimension=0, tiled=True)  195 us
    all_gather x1, blocking collectives, local(): lax.all_gather(jnp.stack([ffn_gain_part, router_column]), ('ctx', 'ws'),...  73.7 us
    all_gather x1, blocking collectives, local(): lax.all_gather(w_router.astype(LOW), ('ctx', 'ws'), axis=0, tiled=True)  72 us
    ppermute x8, waiting for transfers between devices, swap_ws(): came = lax.ppermute(away, 'ws', [(0, 1), (1, 0)])  59 us
    all_gather x1, waiting for transfers between devices, local(): d_weight = lax.all_gather(w_down[0].astype(LOW), 'ws', axis=0, tiled=True)  44.3 us
    all_gather x1, waiting for transfers between devices, local(): g_weight = lax.all_gather(w_gate[0].astype(LOW), 'ws', axis=0, tiled=True)  44.1 us
  transfers between devices with their start and end apart: 38, of which 32 were waited for; matrix products, arithmetic and copies ran while one was open for 20% of the time, Pallas kernels for 0%

profile of v1, /device:TPU:0, one launch (start us, length us, event | category | flops | bytes accessed | tf_op | source)
XLA Modules:
  0.0 1258.4 jit_solution(16519450044523968496)
XLA Ops:
  21.6 18.4 %all-to-all-done = bf16[16,64,384]{2,1,0:T(8,128)(2,1)S(1)} async-done(((bf16[16,64,384]{2,1,0:T(8,128)(2,1)}), bf16[16,64,384]{2,1,0:T(8,128)(2,1)S(1)}, u32[]{:S(2)}, u32[]{:S(2)}) %all-to-all-start) | async-done | bytes 786464 | tf_op jit(solution)/shard_map/all_to_all | solution.py:132
  51.7 17.3 %all-gather.28.cloned.1.call-done = bf16[16,128,384]{2,1,0:T(8,128)(2,1)} async-done(((bf16[16,64,384]{2,1,0:T(8,128)(2,1)}), bf16[16,128,384]{2,1,0:T(8,128)(2,1)}) %all-gather.28.cloned.1.call-update) | async-done | bytes 1572880 | tf_op jit(solution)/shard_map/all_gather | solution.py:133
  69.0 77.7 %all-gather.18.cloned.1.call-done = bf16[2048,2048]{1,0:T(8,128)(2,1)} async-done(((bf16[128,2048]{1,0:T(8,128)(2,1)}), bf16[2048,2048]{1,0:T(8,128)(2,1)}) %all-gather.18.cloned.1.call-update) | async-done | bytes 8388624 | tf_op jit(solution)/shard_map/all_gather | solution.py:68
  197.1 26.3 %all_to_all.20 = bf16[16,128,128]{2,1,0:T(8,128)(2,1)S(1)} all-to-all(bf16[16,128,128]{2,1,0:T(8,128)(2,1)S(1)} %bitcast.263), channel_id=1, replica_groups=mesh['ctx'=16,'ws'=2] {'ctx'}, dimensions={0} | all-to-all | bytes 1048576 | tf_op jit(solution)/shard_map/all_to_all | solution.py:180
  255.8 72.0 %all-gather.6 = bf16[32,64,16]{1,2,0:T(8,128)(2,1)S(1)} all-gather(bf16[1,64,16]{1,2,0:T(8,128)(2,1)S(1)} %convert_bitcast_fusion.3), channel_id=1, replica_groups=mesh['ctx'=16,'ws'=2] {'ctx','ws'}, dimensions={0}, use_global_device_ids=true | all-gather | bytes 67584 | tf_op jit(solution)/shard_map/all_gather | solution.py:137
  328.0 17.3 %all-gather.1 = s32[1,1,2048,8]{2,3,1,0:T(8,128)S(1)} all-gather(s32[1,1,128,8]{2,3,1,0:T(8,128)S(1)} %copy-done.67), channel_id=3, replica_groups=mesh['ctx'=16,'ws'=2] {'ctx'}, dimensions={2}, use_global_device_ids=true | all-gather | bytes 69632 | tf_op jit(solution)/shard_map/all_gather | solution.py:143
  351.1 26.2 %all-gather.32.cloned.1.call-done = bf16[1,2048,1024]{2,1,0:T(8,128)(2,1)} async-done(((bf16[1,1024,1024]{2,1,0:T(8,128)(2,1)}), bf16[1,2048,1024]{2,1,0:T(8,128)(2,1)}) %all-gather.32.cloned.1.call-update) | async-done | bytes 4194320 | tf_op jit(solution)/shard_map/all_gather | solution.py:139
  377.2 14.6 %fusion.15 = f32[2048,1024]{0,1:T(8,128)} fusion(bf16[2048,2048]{1,0:T(8,128)(2,1)} %all-gather.22.cloned.1.call-done, bf16[1,2048,1024]{2,1,0:T(8,128)(2,1)} %all-gather.32.cloned.1.call-done), kind=kOutput, calls=%fused_computation.28 | convolution fusion | flops 8589934592 | bytes 20971520 | tf_op jit(solution)/shard_map/dot_general | solution.py:20
  391.9 44.1 %all-gather.30.cloned.1.call-done = bf16[1,2048,1024]{2,1,0:T(8,128)(2,1)} async-done(((bf16[1,1024,1024]{2,1,0:T(8,128)(2,1)}), bf16[1,2048,1024]{2,1,0:T(8,128)(2,1)}) %all-gather.30.cloned.1.call-update) | async-done | bytes 4194320 | tf_op jit(solution)/shard_map/all_gather | solution.py:138
  436.0 14.6 %fusion.19 = f32[2048,1024]{0,1:T(8,128)} fusion(bf16[2048,2048]{1,0:T(8,128)(2,1)} %all-gather.22.cloned.1.call-done, bf16[1,2048,1024]{2,1,0:T(8,128)(2,1)} %all-gather.30.cloned.1.call-done), kind=kOutput, calls=%fused_computation.32 | convolution fusion | flops 8589934592 | bytes 20971520 | tf_op jit(solution)/shard_map/dot_general | solution.py:20
  450.6 44.3 %all-gather.34.cloned.1.call-done = bf16[1,1024,2048]{2,1,0:T(8,128)(2,1)} async-done(((bf16[1,512,2048]{2,1,0:T(8,128)(2,1)}), bf16[1,1024,2048]{2,1,0:T(8,128)(2,1)}) %all-gather.34.cloned.1.call-update) | async-done | bytes 4194320 | tf_op jit(solution)/shard_map/all_gather | solution.py:140
  494.9 77.7 %all-gather.24.cloned.1.call-done = bf16[2048,2048]{1,0:T(8,128)(2,1)} async-done(((bf16[128,2048]{1,0:T(8,128)(2,1)}), bf16[2048,2048]{1,0:T(8,128)(2,1)}) %all-gather.24.cloned.1.call-update) | async-done | bytes 8388624 | tf_op jit(solution)/shard_map/all_gather | solution.py:68
  572.6 21.6 %fusion.2 = (f32[2048]{0:T(1024)S(1)}, bf16[2048,1024]{0,1:T(8,128)(2,1)}, f32[2048,1024]{0,1:T(8,128)}) fusion(f32[2048,1024]{0,1:T(8,128)} %fusion.15, f32[2048,1024]{0,1:T(8,128)} %fusion.19, bf16[2048,2048]{1,0:T(8,128)(2,1)} %all-gather.24.cloned.1.call-done, bf16[1,1024,2048]{2,1,0:T(8,128)(2,1)} %all-gather.34.cloned.1.call-done), kind=kOutput, calls=%fused_computation.12 | convolution fusion | flops 8608806912 | bytes 41951232 | tf_op jit(solution)/shard_map/dot_general | solution.py:20
  617.2 15.7 %fusion.17 = f32[2048,2048]{1,0:T(8,128)} fusion(bf16[2048,1024]{0,1:T(8,128)(2,1)S(1)} %get-tuple-element.33, bf16[1,2048,1024]{2,1,0:T(8,128)(2,1)} %all-gather.30.cloned.1.call-done), kind=kOutput, calls=%fused_computation.30 | convolution fusion | flops 8589934592 | bytes 25165824 | tf_op jit(solution)/shard_map/dot_general | solution.py:20
  632.9 18.4 %add_convert_fusion = bf16[2048,2048]{1,0:T(8,128)(2,1)} fusion(f32[2048,2048]{1,0:T(8,128)} %fusion.17, f32[2048]{0:T(1024)S(1)} %bitcast.317, f32[2048]{0:T(1024)S(1)} %bitcast.313, bf16[2048,1024]{0,1:T(8,128)(2,1)S(1)} %copy-done.18, bf16[1,2048,1024]{2,1,0:T(8,128)(2,1)} %all-gather.32.cloned.1.call-done), kind=kOutput, calls=%fused_computation.3 | convolution fusion | flops 8606711808 | bytes 33570816 | tf_op jit(solution)/shard_map/dot_general | solution.py:20
  665.5 15.2 %fusion.22 = bf16[1024,2048]{1,0:T(8,128)(2,1)} fusion(bf16[2048,2048]{1,0:T(8,128)(2,1)} %all-gather.24.cloned.1.call-done, bf16[2048,1024]{0,1:T(8,128)(2,1)} %get-tuple-element.29, f32[2048]{0:T(1024)S(1)} %bitcast.304), kind=kOutput, calls=%fused_computation.35 | convolution fusion | flops 8598323200 | bytes 16785408 | tf_op jit(solution)/shard_map/dot_general | solution.py:20
  680.8 73.6 %reduce-scatter.9.cloned.1.call-done = bf16[128,2048]{1,0:T(8,128)(2,1)} async-done(((bf16[2048,2048]{1,0:T(8,128)(2,1)}), bf16[128,2048]{1,0:T(8,128)(2,1)}) %reduce-scatter.9.cloned.1.call-update) | async-done | bytes 524304 | tf_op jit(solution)/shard_map/reduce_scatter | solution.py:72
  784.6 14.4 %all-to-all-done.2 = bf16[16,128,128]{2,1,0:T(8,128)(2,1)S(1)} async-done(((bf16[16,128,128]{2,1,0:T(8,128)(2,1)}), bf16[16,128,128]{2,1,0:T(8,128)(2,1)S(1)}, u32[]{:S(2)}, u32[]{:S(2)}) %all-to-all-start.2) | async-done | bytes 524320 | tf_op jit(solution)/shard_map/all_to_all | solution.py:253
  869.3 14.4 %multiply_convert_fusion.1 = bf16[2048,2048]{1,0:T(8,128)(2,1)} fusion(f32[2048]{0:T(1024)S(1)} %bitcast.305, bf16[2048,1024]{0,1:T(8,128)(2,1)} %get-tuple-element.29, bf16[1,1024,2048]{2,1,0:T(8,128)(2,1)} %all-gather.34.cloned.1.call-done), kind=kOutput, calls=%fused_computation.4 | convolution fusion | flops 8606711808 | bytes 16785408 | tf_op jit(solution)/shard_map/dot_general | solution.py:20
  908.6 26.7 %collective-permute-done.16 = bf16[16,64,384]{2,1,0:T(8,128)(2,1)S(1)} collective-permute-done((bf16[16,64,384]{2,1,0:T(8,128)(2,1)S(1)}, bf16[16,64,384]{2,1,0:T(8,128)(2,1)S(1)}, u32[]{:S(2)}, u32[]{:S(2)}) %collective-permute-start.16) | collective-permute-done | bytes 786464 | tf_op jit(solution)/shard_map/ppermute | solution.py:51
  956.7 73.7 %all-gather.7 = f32[32,2,2048]{2,1,0:T(2,128)S(1)} all-gather(f32[1,2,2048]{2,1,0:T(2,128)S(1)} %maximum_bitcast_fusion), channel_id=7, replica_groups=mesh['ctx'=16,'ws'=2] {'ctx','ws'}, dimensions={0}, use_global_device_ids=true | all-gather | bytes 540672 | tf_op jit(solution)/shard_map/all_gather | solution.py:241
  1039.7 22.2 %reduce-scatter.11.cloned.1.call-done = bf16[128,2048]{1,0:T(8,128)(2,1)} async-done(((bf16[2048,2048]{1,0:T(8,128)(2,1)}), bf16[128,2048]{1,0:T(8,128)(2,1)}) %reduce-scatter.11.cloned.1.call-update) | async-done | bytes 524304 | tf_op jit(solution)/shard_map/reduce_scatter | solution.py:72
  1072.6 66.3 %all-gather.26.cloned.1.call-done = bf16[2048,2048]{1,0:T(8,128)(2,1)} async-done(((bf16[128,2048]{1,0:T(8,128)(2,1)}), bf16[2048,2048]{1,0:T(8,128)(2,1)}) %all-gather.26.cloned.1.call-update) | async-done | bytes 8388624 | tf_op jit(solution)/shard_map/all_gather | solution.py:68
  1147.0 99.2 %reduce-scatter.7.cloned.1.call-done = bf16[128,2048]{1,0:T(8,128)(2,1)} async-done(((bf16[2048,2048]{1,0:T(8,128)(2,1)}), bf16[128,2048]{1,0:T(8,128)(2,1)}) %reduce-scatter.7.cloned.1.call-update) | async-done | bytes 524304 | tf_op jit(solution)/shard_map/reduce_scatter | solution.py:72
  (381 shorter events, 330.9 us)
Async XLA Ops:
  13.8 26.1 %all-to-all-start = ((bf16[16,64,384]{2,1,0:T(8,128)(2,1)}), bf16[16,64,384]{2,1,0:T(8,128)(2,1)S(1)}, u32[]{:S(2)}, u32[]{:S(2)}) async-start(bf16[16,64,384]{2,1,0:T(8,128)(2,1)} %reshape.416), calls=%async_computation | async-start | bytes 1572864 | tf_op jit(solution)/shard_map/all_to_all | solution.py:132
  21.2 47.8 %all-gather.28.cloned.1.call-start = ((), (), s32[]{:S(2)}) async-start(), calls=%async_computation.21 | async-start | bytes 2359296 | tf_op jit(solution)/shard_map/all_gather | solution.py:133
  40.8 105.8 %all-gather.18.cloned.1.call-start = ((), (), s32[]{:S(2)}) async-start(), calls=%async_computation.10 | async-start | bytes 8912896 | tf_op jit(solution)/shard_map/all_gather | solution.py:68
  41.1 8.5 collective-permute-start
  50.6 185.0 %all-gather.20.cloned.1.call-start = ((), (), s32[]{:S(2)}) async-start(), calls=%async_computation.11 | async-start | bytes 8650752 | tf_op jit(solution)/shard_map/all_gather | solution.py:136
  51.4 293.9 %all-gather.22.cloned.1.call-start = ((), (), s32[]{:S(2)}) async-start(), calls=%async_computation.12 | async-start | bytes 8912896 | tf_op jit(solution)/shard_map/all_gather | solution.py:68
  242.4 134.9 %all-gather.32.cloned.1.call-start = ((), (), s32[]{:S(2)}) async-start(), calls=%async_computation.23 | async-start | bytes 6291456 | tf_op jit(solution)/shard_map/all_gather | solution.py:139
  246.3 189.7 %all-gather.30.cloned.1.call-start = ((), (), s32[]{:S(2)}) async-start(), calls=%async_computation.22 | async-start | bytes 6291456 | tf_op jit(solution)/shard_map/all_gather | solution.py:138
  250.3 244.6 %all-gather.34.cloned.1.call-start = ((), (), s32[]{:S(2)}) async-start(), calls=%async_computation.24 | async-start | bytes 6291456 | tf_op jit(solution)/shard_map/all_gather | solution.py:140
  254.4 318.2 %all-gather.24.cloned.1.call-start = ((), (), s32[]{:S(2)}) async-start(), calls=%async_computation.14 | async-start | bytes 8912896 | tf_op jit(solution)/shard_map/all_gather | solution.py:68
  255.7 498.7 %reduce-scatter.9.cloned.1.call-start = ((), (), s32[]{:S(2)}) async-start(), calls=%async_computation.15 | async-start | bytes 8912896 | tf_op jit(solution)/shard_map/reduce_scatter | solution.py:72
  651.4 249.0 %reduce-scatter.15.cloned.1.call-start = ((), (), s32[]{:S(2)}) async-start(), calls=%async_computation.19 | async-start | bytes 6291456 | tf_op jit(solution)/shard_map/reduce_scatter | solution.py:227
  665.4 239.1 %reduce-scatter.17.cloned.1.call-start = ((), (), s32[]{:S(2)}) async-start(), calls=%async_computation.20 | async-start | bytes 6291456 | tf_op jit(solution)/shard_map/reduce_scatter | solution.py:227
  680.8 271.8 %reduce-scatter.13.cloned.1.call-start = ((), (), s32[]{:S(2)}) async-start(), calls=%async_computation.18 | async-start | bytes 6291456 | tf_op jit(solution)/shard_map/reduce_scatter | solution.py:227
  764.4 14.5 %collective-permute-start.10 = (bf16[64,2048]{1,0:T(8,128)(2,1)S(1)}, bf16[64,2048]{1,0:T(8,128)(2,1)S(1)}, u32[]{:S(2)}, u32[]{:S(2)}) collective-permute-start(bf16[64,2048]{1,0:T(8,128)(2,1)S(1)} %dynamic-slice_bitcast_fusion.4), channel_id=1, source_target_pairs={{0,1},{1,0},{2,3},{3,2},{4,5},{5,4},{6,7},{7,6},{8,9},{9,8},{10,11... | collective-permute-start | bytes 786440 | tf_op jit(solution)/shard_map/ppermute | solution.py:51
  780.0 19.0 %all-to-all-start.2 = ((bf16[16,128,128]{2,1,0:T(8,128)(2,1)}), bf16[16,128,128]{2,1,0:T(8,128)(2,1)S(1)}, u32[]{:S(2)}, u32[]{:S(2)}) async-start(bf16[16,128,128]{2,1,0:T(8,128)(2,1)} %bitcast.247), calls=%async_computation.4 | async-start | bytes 1048576 | tf_op jit(solution)/shard_map/all_to_all | solution.py:253
  784.5 277.4 %reduce-scatter.11.cloned.1.call-start = ((), (), s32[]{:S(2)}) async-start(), calls=%async_computation.16 | async-start | bytes 8912896 | tf_op jit(solution)/shard_map/reduce_scatter | solution.py:72
  854.4 284.5 %all-gather.26.cloned.1.call-start = ((), (), s32[]{:S(2)}) async-start(), calls=%async_computation.17 | async-start | bytes 8912896 | tf_op jit(solution)/shard_map/all_gather | solution.py:68
  854.5 13.9 %collective-permute-start.18 = (bf16[64,2048]{1,0:T(8,128)(2,1)S(1)}, bf16[64,2048]{1,0:T(8,128)(2,1)S(1)}, u32[]{:S(2)}, u32[]{:S(2)}) collective-permute-start(bf16[64,2048]{1,0:T(8,128)(2,1)S(1)} %dynamic-slice_bitcast_fusion.2), channel_id=1, source_target_pairs={{0,1},{1,0},{2,3},{3,2},{4,5},{5,4},{6,7},{7,6},{8,9},{9,8},{10,11... | collective-permute-start | bytes 786440 | tf_op jit(solution)/shard_map/ppermute | solution.py:51
  869.3 376.9 %reduce-scatter.7.cloned.1.call-start = ((), (), s32[]{:S(2)}) async-start(), calls=%async_computation.13 | async-start | bytes 8912896 | tf_op jit(solution)/shard_map/reduce_scatter | solution.py:72
  899.2 36.2 %collective-permute-start.16 = (bf16[16,64,384]{2,1,0:T(8,128)(2,1)S(1)}, bf16[16,64,384]{2,1,0:T(8,128)(2,1)S(1)}, u32[]{:S(2)}, u32[]{:S(2)}) collective-permute-start(bf16[16,64,384]{2,1,0:T(8,128)(2,1)S(1)} %dynamic-slice_bitcast_fusion), channel_id=1, source_target_pairs={{0,1},{1,0},{2,3},{3,2},{4,5},{5,4},{6,7},{7,6},{8,9},{9,8},{10,11... | collective-permute-start | bytes 2359304 | tf_op jit(solution)/shard_map/ppermute | solution.py:51
  937.6 97.1 %all-to-all-start.3 = ((bf16[16,64,384]{2,1,0:T(8,128)(2,1)}), bf16[16,64,384]{2,1,0:T(8,128)(2,1)S(1)}, u32[]{:S(2)}, u32[]{:S(2)}) async-start(bf16[16,64,384]{2,1,0:T(8,128)(2,1)} %fusion.45), calls=%async_computation.6 | async-start | bytes 1572864 | tf_op jit(solution)/shard_map/all_to_all | solution.py:301
  1062.9 8.2 collective-permute-start.15
  1145.6 103.9 %collective-permute-start.19 = (f32[64,2048]{1,0:T(8,128)}, f32[64,2048]{1,0:T(8,128)}, u32[]{:S(2)}, u32[]{:S(2)}) collective-permute-start(f32[64,2048]{1,0:T(8,128)} %dynamic-slice_bitcast_fusion.1), channel_id=1, source_target_pairs={{0,1},{1,0},{2,3},{3,2},{4,5},{5,4},{6,7},{7,6},{8,9},{9,8},{10,11... | collective-permute-start | bytes 1572872 | tf_op jit(solution)/shard_map/ppermute | solution.py:51
  (96 other events, 2832.4 us)
Sparse Core Ops, SparseCore 0:
  41.0 27.9 all-gather.27
  71.7 74.8 all-gather.17
  150.2 85.2 all-gather.19
  242.5 77.8 all-gather.21
  322.4 54.8 all-gather.31
  379.2 56.7 all-gather.29
  438.1 56.7 all-gather.33
  497.6 74.8 all-gather.23
  651.5 102.9 reduce-scatter.8
  756.6 59.6 reduce-scatter.14
  818.7 59.9 reduce-scatter.16
  881.4 71.1 reduce-scatter.12
  957.2 104.7 reduce-scatter.10
  1064.2 74.6 all-gather.25
  1143.4 102.8 reduce-scatter.6

commit v2 on v1

v2 whole, which is shorter than its diff:
```python
import math

import jax
import jax.numpy as jnp
from jax import lax
from jax.experimental import pallas as pl
from jax.experimental.pallas import tpu as pltpu
from jax.sharding import PartitionSpec as P

HD = 128
SLOTS = 2

NORM_EPS = 1e-05
ROPE_BASE = 10000.0
MASK_FLOOR = -1e30

LOW = jnp.bfloat16
HIGH = jnp.float32


def dot(left, right, dims=((1,), (0,))):
    return lax.dot_general(left, right, (dims, ((), ())), preferred_element_type=HIGH)


def inv_rms(field):
    return lax.rsqrt(jnp.mean(field * field, axis=-1, keepdims=True) + NORM_EPS)


def rms_back(field, scale, d_hat):
    hat = field * scale
    return scale * (d_hat - hat * jnp.mean(d_hat * hat, axis=-1, keepdims=True))


def rope_tables(positions):
    half_dim = HD // 2
    inv_freq = jnp.exp(jnp.arange(half_dim, dtype=HIGH) * (-2.0 * math.log(ROPE_BASE) / HD))
    angles = positions.astype(HIGH)[:, None] * inv_freq[None, :]
    return jnp.cos(angles), jnp.sin(angles)


def rotate(field, cosine, sine):
    lead, tail = field[:, : HD // 2], field[:, HD // 2 :]
    return jnp.concatenate([lead * cosine - tail * sine, tail * cosine + lead * sine], axis=1)


def pair_ws(own, away):
    came = lax.ppermute(away, "ws", [(0, 1), (1, 0)])
    first = lax.axis_index("ws") == 0
    return jnp.where(first, own, came), jnp.where(first, came, own)


def swap_ws(field):
    mine = lax.axis_index("ws")
    own = lax.dynamic_index_in_dim(field, mine, 0, keepdims=False)
    away = lax.dynamic_index_in_dim(field, 1 - mine, 0, keepdims=False)
    return jnp.stack(pair_ws(own, away), axis=0)


def other_ws(field):
    return lax.ppermute(field, "ws", [(0, 1), (1, 0)])


def whole_ws(half, came):
    first = lax.axis_index("ws") == 0
    return jnp.concatenate([jnp.where(first, half, came), jnp.where(first, came, half)], axis=0)


def sum_ctx(field):
    count = lax.axis_size("ctx")
    if count & (count - 1):
        return lax.psum(field, "ctx")
    step = 1
    while step < count:
        field = field + lax.ppermute(field, "ctx", [(i, i ^ step) for i in range(count)])
        step *= 2
    return field


class Line:
    groups = 4

    def __init__(self):
        c = lax.axis_index("ctx")
        self.z, y, core = c // 4, c // 2 % 2, c % 2
        near = jnp.array([[0, 1, 2, 3], [1, 0, 2, 3], [2, 1, 3, 0], [3, 2, 1, 0]], jnp.int32)[self.z]
        flip = jnp.arange(2, dtype=jnp.int32)
        self.order = (
            near[:, None, None] * 4
            + (y ^ flip)[None, None, :] * 2
            + (core ^ flip)[None, :, None]
        ).reshape(16)
        number = jnp.arange(16, dtype=jnp.int32)
        here = self.order[None, :] == number[:, None]
        self.inverse = jnp.sum(jnp.where(here, number[None, :], 0), axis=1)

    @staticmethod
    def send(field, dz=0, dy=0, dk=0, least=0, most=3):
        pairs = []
        for c in range(16):
            z, y, core = c // 4, c // 2 % 2, c % 2
            if least <= z <= most and 0 <= z + dz <= 3:
                pairs.append((c, (z + dz) * 4 + (y ^ dy) * 2 + (core ^ dk)))
        return lax.ppermute(field, "ctx", pairs)

    def gather(self, block, fills, use):
        send, z = self.send, self.z
        bar = lax.optimization_barrier
        side0, up1, down1, filled0 = bar(
            (send(block, dy=1), send(block, 1), send(block, -1), fills[0]())
        )
        near1 = jnp.where(z == 0, down1, up1)
        pair0 = jnp.concatenate([block, side0], axis=0)
        side1, up2, down2, core0, filled1 = bar(
            (
                send(near1, dy=1),
                send(up1, 1, least=1),
                send(down1, -1, most=2),
                send(pair0, dk=1),
                fills[1](),
            )
        )
        near2 = jnp.where(z == 0, down2, jnp.where(z == 3, up2, down1))
        pair1 = jnp.concatenate([near1, side1], axis=0)
        group0 = jnp.concatenate([pair0, core0], axis=0)
        side2, up3, down3, core1, used0 = bar(
            (
                send(near2, dy=1),
                send(up2, 1, least=2),
                send(down2, -1, most=1),
                send(pair1, dk=1),
                use(0, group0),
            )
        )
        near3 = jnp.where(z == 0, down3, jnp.where(z == 1, down2, jnp.where(z == 2, up2, up3)))
        pair2 = jnp.concatenate([near2, side2], axis=0)
        group1 = jnp.concatenate([pair1, core1], axis=0)
        side3, core2, used1 = bar((send(near3, dy=1), send(pair2, dk=1), use(1, group1)))
        pair3 = jnp.concatenate([near3, side3], axis=0)
        group2 = jnp.concatenate([pair2, core2], axis=0)
        core3, used2 = bar((send(pair3, dk=1), use(2, group2)))
        group3 = jnp.concatenate([pair3, core3], axis=0)
        used3 = use(3, group3)
        return [group0, group1, group2, group3], [filled0, filled1], [used0, used1, used2, used3]

    def scatter(self, make, fills):
        send, z = self.send, self.z
        bar = lax.optimization_barrier

        def add(*fields):
            total = fields[0].astype(HIGH)
            for field in fields[1:]:
                total = total + field.astype(HIGH)
            return total.astype(LOW)

        made3 = make(3)
        rows = made3.shape[0] // 4

        def to_core(made):
            return send(made[2 * rows :], dk=1)

        def side_pair(made, core):
            both = add(made[: 2 * rows], core)
            return both[:rows], send(both[rows:], dy=1)

        core3, made2 = bar((to_core(made3), make(2)))
        own3, side3 = side_pair(made3, core3)
        side3, core2, made1 = bar((side3, to_core(made2), make(1)))
        near3 = add(own3, side3)
        own2, side2 = side_pair(made2, core2)
        up, down = send(near3, 1, most=0), send(near3, -1, least=3)
        up, down, side2, core1, made0 = bar((up, down, side2, to_core(made1), make(0)))
        near2 = add(own2, side2)
        own1, side1 = side_pair(made1, core1)
        up = send(add(jnp.where(z == 0, near2, near3), up), 1, most=1)
        down = send(add(jnp.where(z == 2, near3, near2), down), -1, least=2)
        up, down, side1, core0, filled0 = bar((up, down, side1, to_core(made0), fills[0]()))
        near1 = add(own1, side1)
        own0, side0 = side_pair(made0, core0)
        up = send(add(jnp.where(z == 0, near1, near2), up), 1)
        down = send(add(near1, down), -1)
        up, down, side0, filled1 = bar((up, down, side0, fills[1]()))
        return add(own0, side0, up, down), [filled0, filled1]

    def to_whole(self, small):
        here = self.order[None, :] == jnp.arange(16, dtype=jnp.int32)[:, None]
        return jnp.sum(jnp.where(here[:, :, None], small[None], 0), axis=1)

    def from_whole(self, small):
        here = self.order[:, None] == jnp.arange(16, dtype=jnp.int32)[None, :]
        return jnp.sum(jnp.where(here[:, :, None], small[None], 0), axis=1)

    def move(self, field, back):
        order = self.inverse if back else self.order
        rows, width = field.shape[0] // 16, field.shape[1]
        out = jax.ShapeDtypeStruct(field.shape, field.dtype)
        if width < 1024:

            def small(order_ref, in_ref, out_ref):
                for i in range(16):
                    place = pl.ds(pl.multiple_of(order_ref[i] * rows, rows), rows)
                    out_ref[i * rows : (i + 1) * rows, :] = in_ref[place, :]

            return pl.pallas_call(
                small,
                in_specs=[
                    pl.BlockSpec(memory_space=pltpu.SMEM),
                    pl.BlockSpec(memory_space=pltpu.VMEM),
                ],
                out_specs=pl.BlockSpec(memory_space=pltpu.VMEM),
                out_shape=out,
                name="move_small",
            )(order, field)

        def large(order_ref, in0, in1, in2, in3, out_ref):
            for i, in_ref in enumerate((in0, in1, in2, in3)):
                out_ref[i * rows : (i + 1) * rows, :] = in_ref[...]

        return pl.pallas_call(
            large,
            grid_spec=pltpu.PrefetchScalarGridSpec(
                num_scalar_prefetch=1,
                grid=(4,),
                in_specs=[
                    pl.BlockSpec((rows, width), lambda g, order, i=i: (order[4 * g + i], 0))
                    for i in range(4)
                ],
                out_specs=pl.BlockSpec((4 * rows, width), lambda g, order: (g, 0)),
            ),
            out_shape=out,
            compiler_params=pltpu.CompilerParams(vmem_limit_bytes=24 * 1024 * 1024),
            name="move_large",
        )(order, field, field, field, field)


class Plain:
    groups = 1

    def __init__(self):
        self.order = jnp.arange(lax.axis_size("ctx"), dtype=jnp.int32)

    def gather(self, block, fills, use):
        whole = lax.all_gather(block, "ctx", axis=0, tiled=True)
        return [whole], [fill() for fill in fills], [use(0, whole)]

    def scatter(self, make, fills):
        total = lax.psum_scatter(make(0), "ctx", scatter_dimension=0, tiled=True)
        return total, [fill() for fill in fills]

    def to_whole(self, small):
        return small

    def from_whole(self, small):
        return small

    def move(self, field, back):
        return field


def local(
    layer_input,
    out_grad,
    seq_lengths,
    block_deal,
    expert_routes,
    attn_gain,
    query_gain,
    key_gain,
    ffn_gain,
    w_query,
    w_key,
    w_value,
    w_out,
    w_router,
    w_gate,
    w_up,
    w_down,
):
    ws_count = lax.axis_size("ws")
    ctx_count = lax.axis_size("ctx")
    c = lax.axis_index("ctx")
    w = lax.axis_index("ws")
    tokens, width = layer_input.shape[2:]
    heads = width // HD
    parts = ctx_count // heads
    head = c // parts
    part = c % parts
    own_part = c // heads
    slot_rows = tokens // SLOTS
    half_block = slot_rows // 2
    rows = w_query.shape[0]
    experts = w_router.shape[1]
    span = ctx_count * tokens
    part_span = span // parts

    net = Line() if ctx_count == 16 else Plain()

    starts = block_deal.reshape(ctx_count, 1, 2, 1) * (half_block * ws_count)
    in_block = jnp.arange(half_block, dtype=jnp.int32)
    pair_pos = starts + (
        jnp.arange(ws_count, dtype=jnp.int32)[None, :, None, None] * half_block + in_block
    )
    pos_slot = net.from_whole(pair_pos.reshape(ctx_count, tokens)).reshape(span)
    live_slot = pos_slot < seq_lengths[w]
    own_pos = lax.dynamic_index_in_dim(
        (starts + w * half_block + in_block)[:, 0], c, 0, keepdims=False
    ).reshape(1, slot_rows)
    live_own = (own_pos < seq_lengths[:, None]).reshape(tokens, 1)

    x = layer_input.reshape(tokens, width).astype(HIGH)
    x_scale = inv_rms(x)
    attn_in = (x * x_scale * attn_gain).astype(LOW)
    own_qkv = jnp.stack([w_query, w_key, w_value]).astype(LOW)
    by_head = own_qkv.reshape(3, rows, heads, HD).transpose(2, 1, 0, 3).reshape(heads, rows, 3 * HD)
    if parts > 1:
        by_head = jnp.repeat(by_head, parts, axis=0)
    router_rows = jnp.broadcast_to(w_router.astype(LOW), (ctx_count, rows, experts))
    named = (
        expert_routes.reshape(tokens, 1, -1) == jnp.arange(experts, dtype=jnp.int32)[None, :, None]
    )
    named = jnp.any(named, axis=2).T.astype(LOW).reshape(ctx_count, 1, tokens)
    head_width = 3 * HD + HD * -(-experts // HD)
    sent = jnp.concatenate(
        [
            jnp.concatenate(
                [by_head, router_rows, jnp.zeros((ctx_count, rows, head_width - 3 * HD - experts), LOW)],
                axis=2,
            ),
            jnp.pad(named, ((0, 0), (0, 15), (0, head_width - tokens))),
        ],
        axis=1,
    )
    came = lax.all_to_all(sent, "ctx", 0, 0, tiled=True)
    def after(field, event):
        return lax.optimization_barrier((field, event))[0]

    own_gate, own_up, own_down = (field[0].astype(LOW) for field in (w_gate, w_up, w_down))

    def first_fill():
        return came, own_gate, own_up, own_down

    slot_own = swap_ws(attn_in.reshape(SLOTS, slot_rows, width)).reshape(tokens, width)
    state = {}

    def second_fill():
        state["gate"] = other_ws(after(own_gate, slot_own))
        return state["gate"], rope_tables(pos_slot)

    def project(g, rows_in):
        if g == 0:
            head_rows = came[None, :, :rows]
            both = whole_ws(head_rows, other_ws(after(head_rows, state["gate"])))
            state["head"] = both.transpose(1, 0, 2, 3).reshape(width, head_width)
        field = dot(rows_in, state["head"][:, : 3 * HD])
        if g == net.groups - 1:
            came_up = other_ws(after(own_up, state["head"]))
            field, state["up"] = lax.optimization_barrier((field, came_up))
        return field

    slot_groups, ((came, *_), (came_gate, (cosine, sine))), qkv = net.gather(
        slot_own, [first_fill, second_fill], project
    )
    w_head_all = state["head"]
    w_head = w_head_all[:, : 3 * HD]
    r_weight = w_head_all[:, 3 * HD : 3 * HD + experts]
    routed = net.from_whole(came[:, rows, :tokens].astype(HIGH)).reshape(span, 1) > 0.5
    came_up = state["up"]
    o_weight = lax.all_gather(after(w_out.astype(LOW), qkv[0]), ("ctx", "ws"), axis=0, tiled=True)
    grad_own = jnp.where(live_own, out_grad.reshape(tokens, width), 0).astype(LOW)
    grad_all = lax.all_gather(after(grad_own, qkv[0]), "ctx", axis=0, tiled=True)
    slot_in = jnp.concatenate(slot_groups, axis=0)
    qkv = jnp.concatenate(qkv, axis=0)

    q_pre, k_pre = qkv[:, :HD], qkv[:, HD : 2 * HD]
    v_low = qkv[:, 2 * HD :].astype(LOW)

    def sum_heads(first, second):
        both = jnp.concatenate(
            [first.reshape(ctx_count, tokens), second.reshape(ctx_count, tokens)], axis=1
        )
        both = net.from_whole(sum_ctx(net.to_whole(both))) * (1.0 / (parts * width))
        return both[:, :tokens].reshape(span, 1), both[:, tokens:].reshape(span, 1)

    q_mean, k_mean = sum_heads(jnp.sum(q_pre * q_pre, axis=1), jnp.sum(k_pre * k_pre, axis=1))
    q_scale = lax.rsqrt(q_mean + NORM_EPS)
    k_scale = lax.rsqrt(k_mean + NORM_EPS)
    q_hat = q_pre * q_scale
    k_hat = k_pre * k_scale
    q_gain = lax.dynamic_slice_in_dim(query_gain, head * HD, HD, 0)
    k_gain = lax.dynamic_slice_in_dim(key_gain, head * HD, HD, 0)
    q_low = rotate(q_hat * q_gain, cosine, sine).astype(LOW)
    k_low = rotate(k_hat * k_gain, cosine, sine).astype(LOW)

    def of_part(field):
        if parts == 1:
            return field
        return lax.dynamic_slice_in_dim(field, part * part_span, part_span, 0)

    q_part = of_part(q_low)
    pos_query = of_part(pos_slot)
    score_scale = HD ** (-0.5)
    visible = (pos_slot[None, :] <= pos_query[:, None]) & live_slot[None, :]
    scores = jnp.where(visible, dot(q_part, k_low, ((1,), (1,))) * score_scale, MASK_FLOOR)
    row_max = jnp.max(scores, axis=1, keepdims=True)
    expo = jnp.exp(scores - row_max)
    row_sum = jnp.sum(expo, axis=1, keepdims=True)
    attn_head = dot((expo / row_sum).astype(LOW), v_low)
    log_total = row_max + jnp.log(row_sum)
    attn_head_low, came_down = lax.optimization_barrier(
        (attn_head.astype(LOW), other_ws(after(own_down, came_up)))
    )

    attn_whole = net.move(attn_head_low, True)
    out_chunks = attn_whole.reshape(heads, tokens, HD)
    if parts > 1:
        out_chunks = lax.dynamic_update_slice_in_dim(
            jnp.zeros((ctx_count, tokens, HD), LOW), out_chunks, part * heads, 0
        )
    came = lax.all_to_all(out_chunks, "ctx", 0, 0, tiled=True)
    came, g_weight, u_weight = lax.optimization_barrier(
        (came, whole_ws(own_gate, came_gate), whole_ws(own_up, came_up))
    )
    if parts > 1:
        came = lax.dynamic_index_in_dim(
            came.reshape(heads, parts, tokens, HD), own_part, 1, keepdims=False
        )
    attn_rows = came.transpose(1, 0, 2).reshape(ws_count, slot_rows, width)
    attn_low = swap_ws(attn_rows).reshape(tokens, width)

    mid = x + dot(attn_low, o_weight)
    mid_scale = inv_rms(mid)
    ffn_in = (mid * mid_scale * ffn_gain).astype(LOW)
    def group(field, g):
        size = span // net.groups
        return lax.slice_in_dim(field, g * size, (g + 1) * size, axis=0)

    half = net.groups // 2

    grad_plane = net.move(grad_all, False)

    d_weight = whole_ws(own_down, came_down)
    grad_plane = after(grad_plane, ffn_in)

    def raw_first():
        return [dot(group(grad_plane, g), d_weight, ((1,), (1,))) for g in range(half)]

    def raw_second():
        return [dot(group(grad_plane, g), d_weight, ((1,), (1,))) for g in range(half, net.groups)]

    def expert(g, rows_in):
        router_prob = jax.nn.softmax(dot(rows_in, r_weight), axis=-1)
        prob_own = lax.dynamic_slice_in_dim(router_prob, c, 1, 1)
        gate = jnp.where(group(routed, g), prob_own, 0.0)
        return prob_own, gate, dot(rows_in, g_weight), dot(rows_in, u_weight)

    plane_groups, raw, forward = net.gather(ffn_in, [raw_first, raw_second], expert)
    raw = raw[0] + raw[1]
    kept = []
    for g in range(net.groups):
        prob_own, gate, gate_pre, up_pre = forward[g]
        d_hidden_raw = raw[g]
        sigma = jax.nn.sigmoid(gate_pre)
        act = gate_pre * sigma
        hidden = (act * up_pre).astype(LOW)
        d_gate = jnp.sum(hidden.astype(HIGH) * d_hidden_raw, axis=1, keepdims=True)
        d_gate = jnp.where(group(routed, g), d_gate, 0.0)
        d_hidden = gate * d_hidden_raw
        d_gate_low = (d_hidden * up_pre * (sigma * (1.0 + gate_pre * (1.0 - sigma)))).astype(LOW)
        d_up_low = (d_hidden * act).astype(LOW)
        hidden_gated = (gate * hidden.astype(HIGH)).astype(LOW)
        kept.append((prob_own, gate, hidden, hidden_gated, d_gate, d_gate_low, d_up_low))
    prob_own, gate, hidden, hidden_gated, d_gate, d_gate_low, d_up_low = (
        jnp.concatenate(fields, axis=0) for fields in zip(*kept)
    )
    plane_in = jnp.concatenate(plane_groups, axis=0)

    def grad_rows(left, right, device):
        count = left.shape[1] // ws_count
        return dot(lax.dynamic_slice_in_dim(left, device * count, count, 1), right, ((0,), (0,)))

    def away(left, right):
        return grad_rows(left, right, 1 - w).astype(LOW)

    def own(left, right, came):
        return (grad_rows(left, right, w) + came.astype(HIGH))[None]

    prob_sum = net.from_whole(sum_ctx(net.to_whole((prob_own * d_gate).reshape(ctx_count, tokens))))
    prob_sum, down_away = lax.optimization_barrier((prob_sum, away(hidden_gated, grad_plane)))
    down_came = other_ws(down_away)
    d_log = (prob_own * (d_gate - prob_sum.reshape(span, 1))).astype(LOW)
    r_column = lax.dynamic_slice_in_dim(r_weight, c, 1, 1).reshape(1, width).astype(HIGH)

    def copies_back(g):
        made = (
            dot(kept[g][5], g_weight, ((1,), (1,)))
            + dot(kept[g][6], u_weight, ((1,), (1,)))
            + group(d_log, g).astype(HIGH) * r_column
        ).astype(LOW)
        return made

    def results():
        produced = dot(hidden, d_weight).astype(LOW).astype(HIGH)
        return net.move((gate * produced).astype(LOW), True)

    d_ffn, ((gated, down_came), gate_away) = net.scatter(
        copies_back, [lambda: (results(), down_came), lambda: away(plane_in, d_gate_low)]
    )
    d_ffn = d_ffn.astype(HIGH)
    mixture = lax.psum_scatter(gated, "ctx", scatter_dimension=0, tiled=True)
    layer_out = (mid + mixture.astype(HIGH)).astype(LOW)

    router_column = jnp.sum(plane_in.astype(HIGH) * d_log.astype(HIGH), axis=0)

    mid_hat = mid * mid_scale
    ffn_gain_part = jnp.sum(d_ffn * mid_hat, axis=0)
    d_mid = grad_own.astype(HIGH) + rms_back(mid, mid_scale, d_ffn * ffn_gain)
    d_mid_low = d_mid.astype(LOW)

    d_attn = dot(d_mid_low, o_weight, ((1,), (1,))).astype(LOW)
    d_attn_rows = swap_ws(d_attn.reshape(SLOTS, slot_rows, width)).reshape(tokens, heads, HD)
    gate_came = other_ws(after(gate_away, d_attn_rows))
    in_chunks = d_attn_rows.transpose(1, 0, 2)
    if parts > 1:
        in_chunks = lax.dynamic_update_slice(
            jnp.zeros((heads, parts, tokens, HD), LOW), in_chunks[:, None], (0, own_part, 0, 0)
        ).reshape(ctx_count, tokens, HD)
    d_attn_head = lax.all_to_all(in_chunks, "ctx", 0, 0, tiled=True)
    d_attn_head, up_away = lax.optimization_barrier((d_attn_head, away(plane_in, d_up_low)))
    up_came = other_ws(up_away)
    if parts > 1:
        d_attn_head = lax.dynamic_slice_in_dim(d_attn_head, part * heads, heads, 0)
    d_attn_head = net.move(d_attn_head.reshape(part_span, HD), False)

    slot_d_mid = lax.all_gather(
        swap_ws(d_mid_low.reshape(SLOTS, slot_rows, width)).reshape(tokens, width),
        "ctx",
        axis=0,
        tiled=True,
    )
    delta = jnp.sum(d_attn_head.astype(HIGH) * attn_head, axis=1, keepdims=True)
    prob = jnp.exp(
        jnp.where(visible, dot(q_part, k_low, ((1,), (1,))) * score_scale, MASK_FLOOR) - log_total
    )
    d_prob = dot(d_attn_head, v_low, ((1,), (1,)))
    d_score = (prob * (d_prob - delta)).astype(LOW)
    d_q_part = (dot(d_score, k_low) * score_scale).astype(LOW)
    d_k_rot = (dot(d_score, q_part, ((0,), (0,))) * score_scale).astype(LOW)
    d_v_low = dot(prob.astype(LOW), d_attn_head, ((0,), (0,))).astype(LOW)
    d_q_rot = d_q_part
    if parts > 1:
        d_q_rot = lax.dynamic_update_slice_in_dim(
            jnp.zeros((span, HD), LOW), d_q_part, part * part_span, 0
        )
    d_q_norm = rotate(d_q_rot.astype(HIGH), cosine, -sine)
    d_k_norm = rotate(d_k_rot.astype(HIGH), cosine, -sine)
    gain_parts = jnp.stack([jnp.sum(d_q_norm * q_hat, axis=0), jnp.sum(d_k_norm * k_hat, axis=0)])
    d_q_hat = d_q_norm * q_gain
    d_k_hat = d_k_norm * k_gain
    q_dot, k_dot = sum_heads(jnp.sum(d_q_hat * q_hat, axis=1), jnp.sum(d_k_hat * k_hat, axis=1))
    q_dot, gate_came = lax.optimization_barrier((q_dot, gate_came))
    d_q_low = (q_scale * (d_q_hat - q_hat * q_dot)).astype(LOW)
    d_k_low = (k_scale * (d_k_hat - k_hat * k_dot)).astype(LOW)
    d_qkv = jnp.concatenate([d_q_low, d_k_low, d_v_low], axis=1)

    head_grad = dot(slot_in, d_qkv, ((0,), (0,))).astype(LOW)
    head_grad, d_qkv = lax.optimization_barrier((head_grad, d_qkv))
    head_grad = head_grad.reshape(ctx_count, ws_count, rows, 3 * HD).transpose(1, 0, 2, 3)
    head_grad = swap_ws(head_grad)

    def make_d_in(g):
        made = dot(group(d_qkv, g), w_head, ((1,), (1,))).astype(LOW)
        if g == 2:
            state["down"] = own(hidden_gated, grad_plane, down_came)
            return lax.optimization_barrier((made, state["down"]))[0]
        if g == 1:
            state["gate"] = own(plane_in, d_gate_low, gate_came)
            return lax.optimization_barrier((made, state["gate"]))[0]
        if g == 0:
            state["sum"] = jnp.sum(head_grad.astype(HIGH), axis=0).astype(LOW)
            state["up"] = own(plane_in, d_up_low, up_came)
            made, state["sum"], _ = lax.optimization_barrier((made, state["sum"], state["up"]))
        return made

    def out_grad_rows():
        out_rows = dot(attn_whole, of_part(slot_d_mid), ((0,), (0,)))
        if parts > 1:
            out_rows = lax.psum_scatter(
                out_rows, "ctx", scatter_dimension=0, axis_index_groups=groups, tiled=True
            )
        out_rows = out_rows.reshape(ws_count, rows, width)
        mine = lax.dynamic_index_in_dim(out_rows, w, 0, keepdims=False)
        sent = lax.dynamic_index_in_dim(out_rows, 1 - w, 0, keepdims=False).astype(LOW)
        return mine, sent

    groups = [[h * parts + i for i in range(parts)] for h in range(heads)]
    d_in_sum, ((out_mine, out_sent), col_grad) = net.scatter(
        make_d_in,
        [out_grad_rows, lambda: lax.all_to_all(state["sum"], "ctx", 0, 0, tiled=True)],
    )
    if net.groups == 1:
        state["down"] = own(hidden_gated, grad_plane, down_came)
        state["gate"] = own(plane_in, d_gate_low, gate_came)
    grad_w_out = out_mine + other_ws(out_sent).astype(HIGH)
    d_in = swap_ws(d_in_sum.reshape(ws_count, slot_rows, width)).reshape(tokens, width)
    grad_input = d_mid + rms_back(x, x_scale, d_in.astype(HIGH) * attn_gain)

    small = jnp.stack([ffn_gain_part, router_column]).reshape(2, ctx_count, ws_count, rows)
    small = lax.all_to_all(
        small.transpose(1, 2, 0, 3).reshape(ctx_count, 2 * ws_count * rows), "ctx", 0, 0, tiled=True
    )
    small = jnp.sum(swap_ws(after(small, col_grad).reshape(ctx_count, ws_count, 2, rows).transpose(1, 2, 0, 3)), axis=0)
    grad_ffn_gain = jnp.sum(small[0], axis=0)
    grad_w_router = small[1].T

    col_grad = col_grad.astype(HIGH)
    if parts > 1:
        col_grad = jnp.sum(col_grad.reshape(heads, parts, rows, 3 * HD), axis=1)
    grads_qkv = col_grad.reshape(heads, rows, 3, HD).transpose(2, 1, 0, 3).reshape(3, rows, width)
    own_gain = lax.dynamic_slice_in_dim(attn_gain, (c * ws_count + w) * rows, rows, 0)
    grad_attn_gain = jnp.sum(grads_qkv * own_qkv.astype(HIGH), axis=(0, 2)) / own_gain

    if parts > 1:
        gain_parts = lax.psum_scatter(
            gain_parts, "ctx", scatter_dimension=1, axis_index_groups=groups, tiled=True
        )
    gain_rows = gain_parts.reshape(2, ws_count, rows).transpose(1, 0, 2)
    grad_qk_gain = jnp.sum(swap_ws(gain_rows), axis=0)

    return (
        layer_out.reshape(1, 1, tokens, width),
        grad_input.reshape(1, 1, tokens, width),
        grad_attn_gain,
        grad_qk_gain[0],
        grad_qk_gain[1],
        grad_ffn_gain,
        grads_qkv[0],
        grads_qkv[1],
        grads_qkv[2],
        grad_w_out,
        grad_w_router,
        state["gate"],
        state["up"],
        state["down"],
    )


def solution(mesh):
    rows = P("ctx", "ws", None, None)
    master = P(("ctx", "ws"), None)
    expert = P("ctx", "ws", None)
    gain = P(("ctx", "ws"))
    return jax.shard_map(
        local,
        mesh=mesh,
        in_specs=(rows, rows, P(), P(), rows) + (P(),) * 4 + (master,) * 5 + (expert,) * 3,
        out_specs=(rows, rows) + (gain,) * 4 + (master,) * 5 + (expert,) * 3,
        check_vma=False,
    )
```

time: 1260 us -> 850 us (0.67)
  waiting for transfers between devices: 679 us -> 234 us
  blocking collectives: 189 us -> 0 us
  starting transfers between devices: 38.4 us -> 142 us
  other arithmetic: 86.3 us -> 137 us
  local copies, waits for them, and re-layouts: 24.4 us -> 71 us
    all_gather x9 -> x3, waiting for transfers between devices: 357 us -> 2.17 us  [the longest x1 2.15 us: local(): lax.all_gather(after(w_out.astype(LOW), qkv[0]), ('ctx', 'ws'), axis=0, t...]
    reduce_scatter x6 -> x1, waiting for transfers between devices: 206 us -> 0.02 us  [local(): mixture = lax.psum_scatter(gated, 'ctx', scatter_dimension=0, tiled=True)]
    all_gather x3 -> x0, blocking collectives: 163 us -> none  [the longest x1 73.7 us: local(): lax.all_gather(jnp.stack([ffn_gain_part, router_column]), ('ctx', 'ws'),...]
    ppermute x8 -> x72, waiting for transfers between devices: 59 us -> 190 us  [the longest x56 85.1 us: send(): return lax.ppermute(field, 'ctx', pairs)]
    ppermute x8 -> x72, starting transfers between devices: 10.3 us -> 99.4 us  [the longest x56 83.4 us: send(): return lax.ppermute(field, 'ctx', pairs)]
    unnamed x173 -> x348, local copies, waits for them, and re-layouts: 12.1 us -> 47.3 us
    all_to_all x1 -> x0, blocking collectives: 26.3 us -> none  [local(): came = lax.all_to_all(out_chunks, 'ctx', 0, 0, tiled=True)]
    select_n x0 -> x18, other arithmetic: none -> 18.3 us  [the longest x4 12.3 us: whole_ws(): jnp.where(first, half, came)]
  transfers between devices with their start and end apart: 38 -> 93, of which waited for: 32 -> 39; matrix products, arithmetic and copies ran while one was open for 20% -> 43% of each run, Pallas kernels for 0% -> 1%
where the time goes in v2:
time: 850 us; the launch traced here: 839 us
  waiting for transfers between devices  234 us (28%)
  matrix products  232 us (27%)
  starting transfers between devices  142 us (17%)
  other arithmetic  137 us (16%)
  local copies, waits for them, and re-layouts  71 us (8%)
  between operations  17.3 us (2%)
    dot_general x49, matrix products, dot(): lax.dot_general(left, right, (dims, ((), ())), preferred_element_type=HIGH)  232 us
    ppermute x56, waiting for transfers between devices, send(): return lax.ppermute(field, 'ctx', pairs)  85.1 us
    ppermute x56, starting transfers between devices, send(): return lax.ppermute(field, 'ctx', pairs)  83.4 us
    ppermute x8, waiting for transfers between devices, other_ws(): return lax.ppermute(field, 'ws', [(0, 1), (1, 0)])  71.7 us
    unnamed x348, local copies, waits for them, and re-layouts  47.3 us
    ppermute x8, waiting for transfers between devices, pair_ws(): came = lax.ppermute(away, 'ws', [(0, 1), (1, 0)])  32.8 us
    ppermute x12, starting transfers between devices, sum_ctx(): lax.ppermute(field, 'ctx', [(i, i ^ step) for i in range(count)])  18.6 us
    convert_element_type x15, other arithmetic, add(): return total.astype(LOW)  18.5 us
  transfers between devices with their start and end apart: 93, of which 39 were waited for; matrix products, arithmetic and copies ran while one was open for 43% of the time, Pallas kernels for 1%

profile of v2, /device:TPU:0, one launch (start us, length us, event | category | flops | bytes accessed | tf_op | source)
XLA Modules:
  0.0 839.3 jit_solution(11917527423113492351)
XLA Ops:
  53.8 8.7 %collective-permute-done.3 = bf16[128,2048]{1,0:T(8,128)(2,1)} collective-permute-done((bf16[128,2048]{1,0:T(8,128)(2,1)}, bf16[128,2048]{1,0:T(8,128)(2,1)}, u32[]{:S(2)}, u32[]{:S(2)}) %collective-permute-start.3) | collective-permute-done | bytes 524320 | tf_op jit(solution)/shard_map/ppermute | solution.py:103
  73.5 11.9 %collective-permute-done.8 = bf16[1024,1024]{1,0:T(8,128)(2,1)} collective-permute-done((bf16[1024,1024]{1,0:T(8,128)(2,1)}, bf16[1024,1024]{1,0:T(8,128)(2,1)}, u32[]{:S(2)}, u32[]{:S(2)}) %collective-permute-start.8) | collective-permute-done | bytes 2097184 | tf_op jit(solution)/shard_map/ppermute | solution.py:60
  94.4 16.0 %collective-permute-done.13 = bf16[1,16,64,512]{3,2,1,0:T(8,128)(2,1)} collective-permute-done((bf16[1,16,64,512]{3,2,1,0:T(8,128)(2,1)}, bf16[1,16,64,512]{3,2,1,0:T(8,128)(2,1)}, u32[]{:S(2)}, u32[]{:S(2)}) %collective-permute-start.13) | collective-permute-done | bytes 1048608 | tf_op jit(solution)/shard_map/ppermute | solution.py:60
  131.6 13.2 %collective-permute-done.14 = bf16[128,2048]{1,0:T(8,128)(2,1)S(1)} collective-permute-done((bf16[128,2048]{1,0:T(8,128)(2,1)S(1)}, bf16[128,2048]{1,0:T(8,128)(2,1)S(1)}, u32[]{:S(2)}, u32[]{:S(2)}) %collective-permute-start.14) | collective-permute-done | bytes 524320 | tf_op jit(solution)/shard_map/ppermute | solution.py:103
  157.2 17.7 %collective-permute-done.17 = bf16[1024,1024]{1,0:T(8,128)(2,1)} collective-permute-done((bf16[1024,1024]{1,0:T(8,128)(2,1)}, bf16[1024,1024]{1,0:T(8,128)(2,1)}, u32[]{:S(2)}, u32[]{:S(2)}) %collective-permute-start.17) | collective-permute-done | bytes 2097184 | tf_op jit(solution)/shard_map/ppermute | solution.py:60
  195.0 8.7 %fusion.186 = (f32[2048]{0:T(1024)S(1)}, f32[2048,2048]{0,1:T(8,128)}) fusion(bf16[2048,64]{1,0:T(8,128)(2,1)S(1)} %get-tuple-element.331, bf16[2048,64]{1,0:T(8,128)(2,1)S(1)} %get-tuple-element.332, bf16[2048,64]{1,0:T(8,128)(2,1)S(1)} %get-tuple-element.318, bf16[2048,64]{1,0:T(8,128)(2,1)S(1)} %get-tuple-element.317, ...), kind=kOutput, calls=%fused_computation.472 | convolution fusion | flops 1096808448 | bytes 17844224 | tf_op jit(solution)/shard_map/dot_general | solution.py:22
  203.7 8.4 fusion
  212.1 10.0 %fusion.187 = (bf16[2048,128]{1,0:T(8,128)(2,1)}, f32[2048,128]{1,0:T(8,128)}) fusion(f32[2048,384]{1,0:T(8,128)S(1)} %constant_dynamic-update-slice_fusion, f32[2048,2048]{0,1:T(8,128)} %get-tuple-element.375, f32[2048]{0:T(1024)S(1)} %fusion, f32[2048]{0:T(1024)S(1)} %get-tuple-element.374), kind=kOutput, calls=%fused_computation.473 | convolution fusion | flops 1086586880 | bytes 18890752 | tf_op jit(solution)/shard_map/dot_general | solution.py:22
  222.1 26.1 %collective-permute-done.22 = bf16[512,2048]{1,0:T(8,128)(2,1)} collective-permute-done((bf16[512,2048]{1,0:T(8,128)(2,1)}, bf16[512,2048]{1,0:T(8,128)(2,1)}, u32[]{:S(2)}, u32[]{:S(2)}) %collective-permute-start.22) | collective-permute-done | bytes 2097184 | tf_op jit(solution)/shard_map/ppermute | solution.py:60
  262.3 13.6 %all-to-all-done.1 = bf16[16,128,128]{2,1,0:T(8,128)(2,1)S(1)} async-done(((bf16[16,128,128]{2,1,0:T(8,128)(2,1)}), bf16[16,128,128]{2,1,0:T(8,128)(2,1)S(1)}, u32[]{:S(2)}, u32[]{:S(2)}) %all-to-all-start.1) | async-done | bytes 524320 | tf_op jit(solution)/shard_map/all_to_all | solution.py:418
  329.4 10.1 %collective-permute-done.27 = bf16[128,2048]{1,0:T(8,128)(2,1)S(1)} collective-permute-done((bf16[128,2048]{1,0:T(8,128)(2,1)S(1)}, bf16[128,2048]{1,0:T(8,128)(2,1)S(1)}, u32[]{:S(2)}, u32[]{:S(2)}) %collective-permute-start.27) | collective-permute-done | bytes 524320 | tf_op jit(solution)/shard_map/ppermute | solution.py:103
  462.1 10.0 %collective-permute-done.43 = bf16[128,2048]{1,0:T(8,128)(2,1)S(1)} collective-permute-done((bf16[128,2048]{1,0:T(8,128)(2,1)S(1)}, bf16[128,2048]{1,0:T(8,128)(2,1)S(1)}, u32[]{:S(2)}, u32[]{:S(2)}) %collective-permute-start.43) | collective-permute-done | bytes 524320 | tf_op jit(solution)/shard_map/ppermute | solution.py:103
  479.5 11.5 %collective-permute-done.47 = bf16[128,2048]{1,0:T(8,128)(2,1)S(1)} collective-permute-done((bf16[128,2048]{1,0:T(8,128)(2,1)S(1)}, bf16[128,2048]{1,0:T(8,128)(2,1)S(1)}, u32[]{:S(2)}, u32[]{:S(2)}) %collective-permute-start.47) | collective-permute-done | bytes 524320 | tf_op jit(solution)/shard_map/ppermute | solution.py:103
  498.8 14.0 %multiply_convert_fusion.1.in0.in1.in2.in3 = bf16[2048,2048]{1,0:T(8,128)(2,1)S(1)} fusion(f32[2048]{0:T(1024)S(1)} %bitcast.399, bf16[512,1024]{1,0:T(8,128)(2,1)} %copy-done.85, bf16[512,1024]{1,0:T(8,128)(2,1)S(1)} %copy-done.51, bf16[512,1024]{1,0:T(8,128)(2,1)S(1)} %copy-done.49, bf16[512,1024]{1,0:T(8,128)(2,1)S(1)} %copy-done.47, ...), kind=kOutput, calls=%fused_computation.3 | convolution fusion | flops 8631877632 | bytes 16785408 | tf_op jit(solution)/shard_map/dot_general | solution.py:22
  531.8 7.8 fusion.79
  573.4 9.7 %fusion.60 = f32[512,2048]{1,0:T(8,128)} fusion(bf16[2048,2048]{1,0:T(8,128)(2,1)} %copy-done.2, bf16[2048,1024]{1,0:T(8,128)(2,1)S(1)} %copy-done.46, s32[]{:T(128)S(6)} %select_n.418), kind=kOutput, calls=%fused_computation.104 | convolution fusion | flops 4294967296 | bytes 14680068 | tf_op jit(solution)/shard_map/dot_general | solution.py:22
  606.8 8.5 %fusion.82 = bf16[1024,1024]{1,0:T(8,128)(2,1)} fusion(bf16[2048,2048]{1,0:T(8,128)(2,1)} %constant_dynamic-update-slice_fusion.4, s32[]{:T(128)S(6)} %select_n.413, bf16[512,1024]{1,0:T(8,128)(2,1)} %get-tuple-element.304, bf16[512,1024]{1,0:T(8,128)(2,1)S(1)} %copy-done.95, bf16[512,1024]{1,0:T(8,128)(2,1)S(1)} %copy-done.90, ...), kind=kOutput, calls=%fused_computation.149 | convolution fusion | flops 4312793088 | bytes 10485764 | tf_op jit(solution)/shard_map/dot_general | solution.py:22
  631.8 10.0 %multiply_convert_fusion = bf16[2048,2048]{0,1:T(8,128)(2,1)} fusion(f32[2048,2048]{0,1:T(8,128)} %get-tuple-element.375, bf16[2048,128]{1,0:T(8,128)(2,1)} %move_small.3, f32[2048]{0:T(1024)S(1)} %multiply_reduce_fusion.6, f32[2048]{0:T(1024)S(1)} %log_add_fusion, f32[2048,384]{1,0:T(8,128)S(1)} %copy-done.7), kind=kOutput, calls=%fused_computation.1 | convolution fusion | flops 1090519040 | bytes 26230784 | tf_op jit(solution)/shard_map/dot_general | solution.py:22
  667.4 9.1 %fusion.25 = bf16[2048,128]{1,0:T(8,128)(2,1)S(1)} fusion(bf16[2048,128]{1,0:T(8,128)(2,1)} %move_small.3, f32[2048,2048]{0,1:T(8,128)} %get-tuple-element.375, f32[2048]{0:T(1024)S(1)} %log_add_fusion), kind=kOutput, calls=%fused_computation.62 | convolution fusion | flops 1082392576 | bytes 17833984 | tf_op jit(solution)/shard_map/dot_general | solution.py:22
  685.6 8.0 convolution_convert_fusion.5
  700.6 9.3 %add_bitcast_fusion.1 = f32[1,1024,1024]{2,1,0:T(8,128)} fusion(bf16[1024,1024]{1,0:T(8,128)(2,1)} %collective-permute-done.62, bf16[2048,2048]{1,0:T(8,128)(2,1)S(1)} %bitcast.334, s32[]{:T(128)S(6)} %select_n.419, bf16[512,1024]{1,0:T(8,128)(2,1)} %get-tuple-element.303, bf16[512,1024]{1,0:T(8,128)(2,1)S(1)} %copy-done.100, ...), kind=kOutput, calls=%fused_computation.26 | convolution fusion | flops 4313841664 | bytes 14680068 | tf_op jit(solution)/shard_map/dot_general | solution.py:22
  715.3 25.1 %collective-permute-done.70 = bf16[16,64,384]{2,1,0:T(8,128)(2,1)S(1)} collective-permute-done((bf16[16,64,384]{2,1,0:T(8,128)(2,1)S(1)}, bf16[16,64,384]{2,1,0:T(8,128)(2,1)S(1)}, u32[]{:S(2)}, u32[]{:S(2)}) %collective-permute-start.70) | collective-permute-done | bytes 786464 | tf_op jit(solution)/shard_map/ppermute | solution.py:47
  749.1 7.3 add_bitcast_fusion
  794.9 11.0 %collective-permute-start.77 = (bf16[128,2048]{1,0:T(8,128)(2,1)}, bf16[128,2048]{1,0:T(8,128)(2,1)}, u32[]{:S(2)}, u32[]{:S(2)}) collective-permute-start(bf16[128,2048]{1,0:T(8,128)(2,1)} %get-tuple-element.337), channel_id=1, source_target_pairs={{0,8},{2,10},{4,12},{6,14},{8,16},{10,18},{12,20},{14,22},{16,24},... | collective-permute-start | bytes 1572872 | tf_op jit(solution)/shard_map/ppermute | solution.py:103
  (796 shorter events, 536.3 us)
Async XLA Ops:
  21.1 44.3 %all-to-all-start = ((bf16[16,80,512]{2,1,0:T(8,128)(2,1)}), bf16[16,80,512]{2,1,0:T(8,128)(2,1)S(1)}, u32[]{:S(2)}, u32[]{:S(2)}) async-start(bf16[16,80,512]{2,1,0:T(8,128)(2,1)} %pad_maximum_fusion.11), calls=%async_computation | async-start | bytes 2621440 | tf_op jit(solution)/shard_map/all_to_all | solution.py:332
  27.0 256.4 %all-gather.6.cloned.1.call-start = ((), (), s32[]{:S(2)}) async-start(), calls=%async_computation.7 | async-start | bytes 8912896 | tf_op jit(solution)/shard_map/all_gather | solution.py:369
  37.1 48.3 %collective-permute-start.8 = (bf16[1024,1024]{1,0:T(8,128)(2,1)}, bf16[1024,1024]{1,0:T(8,128)(2,1)}, u32[]{:S(2)}, u32[]{:S(2)}) collective-permute-start(bf16[1024,1024]{1,0:T(8,128)(2,1)} %get-tuple-element.136), channel_id=1, source_target_pairs={{0,1},{1,0},{2,3},{3,2},{4,5},{5,4},{6,7},{7,6},{8,9},{9,8},{10,11... | collective-permute-start | bytes 6291464 | tf_op jit(solution)/shard_map/ppermute | solution.py:60
  85.4 25.0 %collective-permute-start.13 = (bf16[1,16,64,512]{3,2,1,0:T(8,128)(2,1)}, bf16[1,16,64,512]{3,2,1,0:T(8,128)(2,1)}, u32[]{:S(2)}, u32[]{:S(2)}) collective-permute-start(bf16[1,16,64,512]{3,2,1,0:T(8,128)(2,1)} %slice_bitcast_fusion), channel_id=1, source_target_pairs={{0,1},{1,0},{2,3},{3,2},{4,5},{5,4},{6,7},{7,6},{8,9},{9,8},{10,11... | collective-permute-start | bytes 3145736 | tf_op jit(solution)/shard_map/ppermute | solution.py:60
  88.2 29.2 %collective-permute-start.11 = (bf16[128,2048]{1,0:T(8,128)(2,1)}, bf16[128,2048]{1,0:T(8,128)(2,1)S(1)}, u32[]{:S(2)}, u32[]{:S(2)}) collective-permute-start(bf16[128,2048]{1,0:T(8,128)(2,1)} %collective-permute-done.6), channel_id=1, source_target_pairs={{8,0},{10,2},{12,4},{14,6},{9,1},{11,3},{13,5},{15,7}} | collective-permute-start | bytes 1572872 | tf_op jit(solution)/shard_map/ppermute | solution.py:103
  89.5 28.7 %collective-permute-start.10 = (bf16[128,2048]{1,0:T(8,128)(2,1)}, bf16[128,2048]{1,0:T(8,128)(2,1)S(1)}, u32[]{:S(2)}, u32[]{:S(2)}) collective-permute-start(bf16[128,2048]{1,0:T(8,128)(2,1)} %collective-permute-done.5), channel_id=1, source_target_pairs={{16,24},{18,26},{20,28},{22,30},{17,25},{19,27},{21,29},{23,31}} | collective-permute-start | bytes 1572872 | tf_op jit(solution)/shard_map/ppermute | solution.py:103
  91.5 27.5 %collective-permute-start.12 = (bf16[256,2048]{1,0:T(8,128)(2,1)S(1)}, bf16[256,2048]{1,0:T(8,128)(2,1)}, u32[]{:S(2)}, u32[]{:S(2)}) collective-permute-start(bf16[256,2048]{1,0:T(8,128)(2,1)S(1)} %pad_maximum_fusion.13), channel_id=1, source_target_pairs={{0,2},{2,0},{4,6},{6,4},{8,10},{10,8},{12,14},{14,12},{16,18},{18,... | collective-permute-start | bytes 3145736 | tf_op jit(solution)/shard_map/ppermute | solution.py:103
  119.0 174.6 %all-gather.4.cloned.1.call-start = ((), (), s32[]{:S(2)}) async-start(), calls=%async_computation.6 | async-start | bytes 8650752 | tf_op jit(solution)/shard_map/all_gather | solution.py:367
  126.8 48.1 %collective-permute-start.17 = (bf16[1024,1024]{1,0:T(8,128)(2,1)}, bf16[1024,1024]{1,0:T(8,128)(2,1)}, u32[]{:S(2)}, u32[]{:S(2)}) collective-permute-start(bf16[1024,1024]{1,0:T(8,128)(2,1)} %get-tuple-element.152), channel_id=1, source_target_pairs={{0,1},{1,0},{2,3},{3,2},{4,5},{5,4},{6,7},{7,6},{8,9},{9,8},{10,11... | collective-permute-start | bytes 6291464 | tf_op jit(solution)/shard_map/ppermute | solution.py:60
  192.5 55.7 %collective-permute-start.22 = (bf16[512,2048]{1,0:T(8,128)(2,1)}, bf16[512,2048]{1,0:T(8,128)(2,1)}, u32[]{:S(2)}, u32[]{:S(2)}) collective-permute-start(bf16[512,2048]{1,0:T(8,128)(2,1)} %convert_bitcast_fusion), channel_id=1, source_target_pairs={{0,1},{1,0},{2,3},{3,2},{4,5},{5,4},{6,7},{7,6},{8,9},{9,8},{10,11... | collective-permute-start | bytes 6291464 | tf_op jit(solution)/shard_map/ppermute | solution.py:60
  250.1 25.8 %all-to-all-start.1 = ((bf16[16,128,128]{2,1,0:T(8,128)(2,1)}), bf16[16,128,128]{2,1,0:T(8,128)(2,1)S(1)}, u32[]{:S(2)}, u32[]{:S(2)}) async-start(bf16[16,128,128]{2,1,0:T(8,128)(2,1)} %bitcast.336), calls=%async_computation.1 | async-start | bytes 1048576 | tf_op jit(solution)/shard_map/all_to_all | solution.py:418
  253.7 521.0 %all-gather.8.cloned.1.call-start = ((), (), s32[]{:S(2)}) async-start(), calls=%async_computation.9 | async-start | bytes 8912896 | tf_op jit(solution)/shard_map/all_gather | solution.py:533
  454.4 65.3 %collective-permute-start.53 = (bf16[512,2048]{1,0:T(8,128)(2,1)}, bf16[512,2048]{1,0:T(8,128)(2,1)}, u32[]{:S(2)}, u32[]{:S(2)}) collective-permute-start(bf16[512,2048]{1,0:T(8,128)(2,1)} %convolution_convert_fusion.4), channel_id=1, source_target_pairs={{0,1},{1,0},{2,3},{3,2},{4,5},{5,4},{6,7},{7,6},{8,9},{9,8},{10,11... | collective-permute-start | bytes 6291464 | tf_op jit(solution)/shard_map/ppermute | solution.py:60
  492.4 27.3 %collective-permute-start.51 = (bf16[128,2048]{1,0:T(8,128)(2,1)}, bf16[128,2048]{1,0:T(8,128)(2,1)}, u32[]{:S(2)}, u32[]{:S(2)}) collective-permute-start(bf16[128,2048]{1,0:T(8,128)(2,1)} %slice.350), channel_id=1, source_target_pairs={{0,4},{2,6},{4,0},{6,2},{8,12},{10,14},{12,8},{14,10},{16,20},{18,... | collective-permute-start | bytes 1572872 | tf_op jit(solution)/shard_map/ppermute | solution.py:103
  494.1 25.6 %collective-permute-start.50 = (bf16[128,2048]{1,0:T(8,128)(2,1)}, bf16[128,2048]{1,0:T(8,128)(2,1)}, u32[]{:S(2)}, u32[]{:S(2)}) collective-permute-start(bf16[128,2048]{1,0:T(8,128)(2,1)} %get-tuple-element.329), channel_id=1, source_target_pairs={{16,8},{18,10},{20,12},{22,14},{24,16},{26,18},{28,20},{30,22},{17... | collective-permute-start | bytes 1572872 | tf_op jit(solution)/shard_map/ppermute | solution.py:103
  495.6 24.1 %collective-permute-start.49 = (bf16[128,2048]{1,0:T(8,128)(2,1)}, bf16[128,2048]{1,0:T(8,128)(2,1)}, u32[]{:S(2)}, u32[]{:S(2)}) collective-permute-start(bf16[128,2048]{1,0:T(8,128)(2,1)} %get-tuple-element.330), channel_id=1, source_target_pairs={{0,8},{2,10},{4,12},{6,14},{8,16},{10,18},{12,20},{14,22},{1,9},{3... | collective-permute-start | bytes 1572872 | tf_op jit(solution)/shard_map/ppermute | solution.py:103
  602.5 25.7 %all-to-all-start.2 = ((bf16[16,128,128]{2,1,0:T(8,128)(2,1)}), bf16[16,128,128]{2,1,0:T(8,128)(2,1)}, u32[]{:S(2)}, u32[]{:S(2)}) async-start(bf16[16,128,128]{2,1,0:T(8,128)(2,1)} %copy.89), calls=%async_computation.3 | async-start | bytes 1048576 | tf_op jit(solution)/shard_map/all_to_all | solution.py:526
  606.8 222.4 %reduce-scatter.2.cloned.1.call-start = ((), (), s32[]{:S(2)}) async-start(), calls=%async_computation.8 | async-start | bytes 8912896 | tf_op jit(solution)/shard_map/reduce_scatter | solution.py:508
  621.3 62.0 %collective-permute-start.62 = (bf16[1024,1024]{1,0:T(8,128)(2,1)}, bf16[1024,1024]{1,0:T(8,128)(2,1)}, u32[]{:S(2)}, u32[]{:S(2)}) collective-permute-start(bf16[1024,1024]{1,0:T(8,128)(2,1)} %fusion.79), channel_id=1, source_target_pairs={{0,1},{1,0},{2,3},{3,2},{4,5},{5,4},{6,7},{7,6},{8,9},{9,8},{10,11... | collective-permute-start | bytes 6291464 | tf_op jit(solution)/shard_map/ppermute | solution.py:60
  676.4 72.6 %collective-permute-start.71 = (bf16[1024,1024]{1,0:T(8,128)(2,1)}, bf16[1024,1024]{1,0:T(8,128)(2,1)}, u32[]{:S(2)}, u32[]{:S(2)}) collective-permute-start(bf16[1024,1024]{1,0:T(8,128)(2,1)} %fusion.82), channel_id=1, source_target_pairs={{0,1},{1,0},{2,3},{3,2},{4,5},{5,4},{6,7},{7,6},{8,9},{9,8},{10,11... | collective-permute-start | bytes 6291464 | tf_op jit(solution)/shard_map/ppermute | solution.py:60
  693.9 46.4 %collective-permute-start.70 = (bf16[16,64,384]{2,1,0:T(8,128)(2,1)S(1)}, bf16[16,64,384]{2,1,0:T(8,128)(2,1)S(1)}, u32[]{:S(2)}, u32[]{:S(2)}) collective-permute-start(bf16[16,64,384]{2,1,0:T(8,128)(2,1)S(1)} %dynamic-slice_bitcast_fusion), channel_id=1, source_target_pairs={{0,1},{1,0},{2,3},{3,2},{4,5},{5,4},{6,7},{7,6},{8,9},{9,8},{10,11... | collective-permute-start | bytes 2359304 | tf_op jit(solution)/shard_map/ppermute | solution.py:47
  709.9 31.5 %collective-permute-start.65 = (bf16[256,2048]{1,0:T(8,128)(2,1)S(1)}, bf16[256,2048]{1,0:T(8,128)(2,1)S(1)}, u32[]{:S(2)}, u32[]{:S(2)}) collective-permute-start(bf16[256,2048]{1,0:T(8,128)(2,1)S(1)} %slice.303), channel_id=1, source_target_pairs={{0,2},{2,0},{4,6},{6,4},{8,10},{10,8},{12,14},{14,12},{16,18},{18,... | collective-permute-start | bytes 3145736 | tf_op jit(solution)/shard_map/ppermute | solution.py:103
  710.7 30.7 %collective-permute-start.64 = (bf16[128,2048]{1,0:T(8,128)(2,1)S(1)}, bf16[128,2048]{1,0:T(8,128)(2,1)S(1)}, u32[]{:S(2)}, u32[]{:S(2)}) collective-permute-start(bf16[128,2048]{1,0:T(8,128)(2,1)S(1)} %slice.363), channel_id=1, source_target_pairs={{0,4},{2,6},{4,0},{6,2},{8,12},{10,14},{12,8},{14,10},{16,20},{18,... | collective-permute-start | bytes 1572872 | tf_op jit(solution)/shard_map/ppermute | solution.py:103
  756.4 50.9 %all-to-all-start.3 = ((bf16[16,64,384]{2,1,0:T(8,128)(2,1)}), bf16[16,64,384]{2,1,0:T(8,128)(2,1)}, u32[]{:S(2)}, u32[]{:S(2)}) async-start(bf16[16,64,384]{2,1,0:T(8,128)(2,1)} %fusion.98), calls=%async_computation.4 | async-start | bytes 1572864 | tf_op jit(solution)/shard_map/all_to_all | solution.py:597
  (225 other events, 3270.2 us)
Sparse Core Ops, SparseCore 0:
  119.2 78.7 all-gather.5
  200.9 92.7 all-gather.3
  552.7 84.7 all-gather.7
  641.4 107.9 reduce-scatter.1

commit v3 on v2

--- a/solution.py
+++ b/solution.py
@@ -105,42 +105,40 @@
     def gather(self, block, fills, use):
         send, z = self.send, self.z
         bar = lax.optimization_barrier
+
+        def pair(near, side):
+            return jnp.concatenate([near, side], axis=0)
+
         side0, up1, down1, filled0 = bar(
             (send(block, dy=1), send(block, 1), send(block, -1), fills[0]())
         )
         near1 = jnp.where(z == 0, down1, up1)
-        pair0 = jnp.concatenate([block, side0], axis=0)
         side1, up2, down2, core0, filled1 = bar(
             (
                 send(near1, dy=1),
                 send(up1, 1, least=1),
                 send(down1, -1, most=2),
-                send(pair0, dk=1),
+                send(pair(block, side0), dk=1),
                 fills[1](),
             )
         )
         near2 = jnp.where(z == 0, down2, jnp.where(z == 3, up2, down1))
-        pair1 = jnp.concatenate([near1, side1], axis=0)
-        group0 = jnp.concatenate([pair0, core0], axis=0)
         side2, up3, down3, core1, used0 = bar(
             (
                 send(near2, dy=1),
                 send(up2, 1, least=2),
                 send(down2, -1, most=1),
-                send(pair1, dk=1),
-                use(0, group0),
+                send(pair(near1, side1), dk=1),
+                use(0, (block, side0, core0)),
             )
         )
         near3 = jnp.where(z == 0, down3, jnp.where(z == 1, down2, jnp.where(z == 2, up2, up3)))
-        pair2 = jnp.concatenate([near2, side2], axis=0)
-        group1 = jnp.concatenate([pair1, core1], axis=0)
-        side3, core2, used1 = bar((send(near3, dy=1), send(pair2, dk=1), use(1, group1)))
-        pair3 = jnp.concatenate([near3, side3], axis=0)
-        group2 = jnp.concatenate([pair2, core2], axis=0)
-        core3, used2 = bar((send(pair3, dk=1), use(2, group2)))
-        group3 = jnp.concatenate([pair3, core3], axis=0)
-        used3 = use(3, group3)
-        return [group0, group1, group2, group3], [filled0, filled1], [used0, used1, used2, used3]
+        side3, core2, used1 = bar(
+            (send(near3, dy=1), send(pair(near2, side2), dk=1), use(1, (near1, side1, core1), used0))
+        )
+        core3, used2 = bar((send(pair(near3, side3), dk=1), use(2, (near2, side2, core2), used1)))
+        used3 = use(3, (near3, side3, core3), used2)
+        return [filled0, filled1], used3
 
     def scatter(self, make, fills):
         send, z = self.send, self.z
@@ -240,7 +238,7 @@
 
     def gather(self, block, fills, use):
         whole = lax.all_gather(block, "ctx", axis=0, tiled=True)
-        return [whole], [fill() for fill in fills], [use(0, whole)]
+        return [fill() for fill in fills], use(0, (whole,))
 
     def scatter(self, make, fills):
         total = lax.psum_scatter(make(0), "ctx", scatter_dimension=0, tiled=True)
@@ -254,6 +252,276 @@
 
     def move(self, field, back):
         return field
+
+
+def kernel_params(mib):
+    return pltpu.CompilerParams(vmem_limit_bytes=mib * 1024 * 1024)
+
+
+def cost(matmuls, reads):
+    return pl.CostEstimate(flops=2 * matmuls, bytes_accessed=reads, transcendentals=0)
+
+
+def attend(q, k, v, pos_query, pos_key):
+    queries, keys = q.shape[0], k.shape[0]
+    block = 256 if keys <= 2048 else 128
+
+    def body(q_ref, k_ref, v_ref, pq_ref, pk_ref, out_ref, low_ref, log_ref):
+        scores = dot(q_ref[...], k_ref[...], ((1,), (1,))) * HD ** (-0.5)
+        scores = jnp.where(pk_ref[...] <= pq_ref[...], scores, MASK_FLOOR)
+        row_max = jnp.max(scores, axis=1, keepdims=True)
+        expo = jnp.exp(scores - row_max)
+        row_sum = jnp.sum(expo, axis=1, keepdims=True)
+        out = dot((expo * (1.0 / row_sum)).astype(LOW), v_ref[...])
+        out_ref[...] = out
+        low_ref[...] = out.astype(LOW)
+        log_ref[...] = row_max + jnp.log(row_sum)
+
+    rows = pl.BlockSpec((block, HD), lambda i: (i, 0))
+    whole = pl.BlockSpec((keys, HD), lambda i: (0, 0))
+    column = pl.BlockSpec((block, 1), lambda i: (i, 0))
+    return pl.pallas_call(
+        body,
+        grid=(queries // block,),
+        in_specs=[rows, whole, whole, column, pl.BlockSpec((1, keys), lambda i: (0, 0))],
+        out_specs=[rows, rows, column],
+        out_shape=[
+            jax.ShapeDtypeStruct((queries, HD), HIGH),
+            jax.ShapeDtypeStruct((queries, HD), LOW),
+            jax.ShapeDtypeStruct((queries, 1), HIGH),
+        ],
+        compiler_params=kernel_params(48),
+        cost_estimate=cost(8 * queries * keys * HD, 8 * keys * HD),
+        name="attend",
+    )(q, k, v, pos_query.reshape(queries, 1), pos_key.reshape(1, keys))
+
+
+def attend_back(q, k, v, d_out, log_total, delta, pos_query, pos_key):
+    queries, keys = q.shape[0], k.shape[0]
+    block = 256 if keys <= 2048 else 128
+    steps = queries // block
+    scale = HD ** (-0.5)
+
+    def body(q_ref, k_ref, v_ref, do_ref, log_ref, delta_ref, pq_ref, pk_ref, dq_ref, dk_ref, dv_ref, dk_sum, dv_sum):
+        step = pl.program_id(0)
+
+        @pl.when(step == 0)
+        def _():
+            dk_sum[...] = jnp.zeros_like(dk_sum)
+            dv_sum[...] = jnp.zeros_like(dv_sum)
+
+        q_rows, k_rows, do_rows = q_ref[...], k_ref[...], do_ref[...]
+        scores = dot(k_rows, q_rows, ((1,), (1,))) * scale
+        scores = jnp.where(pk_ref[...] <= pq_ref[...], scores, MASK_FLOOR)
+        prob = jnp.exp(scores - log_ref[...])
+        d_prob = dot(v_ref[...], do_rows, ((1,), (1,)))
+        d_score = (prob * (d_prob - delta_ref[...])).astype(LOW)
+        dv_sum[...] += dot(prob.astype(LOW), do_rows)
+        dk_sum[...] += dot(d_score, q_rows)
+        dq_ref[...] = (dot(d_score, k_rows, ((0,), (0,))) * scale).astype(LOW)
+
+        @pl.when(step == steps - 1)
+        def _():
+            dk_ref[...] = (dk_sum[...] * scale).astype(LOW)
+            dv_ref[...] = dv_sum[...].astype(LOW)
+
+    rows = pl.BlockSpec((block, HD), lambda i: (i, 0))
+    whole = pl.BlockSpec((keys, HD), lambda i: (0, 0))
+    row = pl.BlockSpec((1, block), lambda i: (0, i))
+    column = pl.BlockSpec((keys, 1), lambda i: (0, 0))
+    return pl.pallas_call(
+        body,
+        grid=(steps,),
+        in_specs=[rows, whole, whole, rows, row, row, row, column],
+        out_specs=[rows, whole, whole],
+        out_shape=[
+            jax.ShapeDtypeStruct((queries, HD), LOW),
+            jax.ShapeDtypeStruct((keys, HD), LOW),
+            jax.ShapeDtypeStruct((keys, HD), LOW),
+        ],
+        scratch_shapes=[pltpu.VMEM((keys, HD), HIGH), pltpu.VMEM((keys, HD), HIGH)],
+        compiler_params=kernel_params(56),
+        cost_estimate=cost(12 * queries * keys * HD, 8 * keys * HD),
+        name="attend_back",
+    )(
+        q,
+        k,
+        v,
+        d_out,
+        log_total.reshape(1, queries),
+        delta.reshape(1, queries),
+        pos_query.reshape(1, queries),
+        pos_key.reshape(keys, 1),
+    )
+
+
+def in_place(body, g, last, prefetch, operands, **kernel):
+    outs = kernel.pop("outs")
+    specs = kernel.pop("in_specs")
+    count = len(operands)
+    last = list(last) if last is not None else []
+
+    def called(*refs):
+        body(*refs[: prefetch + count], *refs[prefetch + count + len(last) :])
+
+    return pl.pallas_call(
+        called,
+        grid_spec=pltpu.PrefetchScalarGridSpec(
+            num_scalar_prefetch=prefetch,
+            grid=kernel.pop("grid"),
+            in_specs=specs + [pl.BlockSpec(memory_space=pl.ANY)] * len(last),
+            out_specs=kernel.pop("out_specs"),
+            scratch_shapes=kernel.pop("scratch_shapes", ()),
+        ),
+        out_shape=outs,
+        input_output_aliases={prefetch + count + i: i for i in range(len(last))},
+        **kernel,
+    )
+
+
+def fixed(rows, columns, g=0):
+    return pl.BlockSpec((rows, columns), lambda j, *info: (g, 0))
+
+
+def project_group(g, pieces, last, groups, w_all):
+    count, width = 4 * pieces[0].shape[0], pieces[0].shape[1]
+    third = count // 4
+
+    def body(near_ref, side_ref, core_ref, w_ref, rows_ref, qk_ref, v_ref):
+        rows_ref[:third, :] = near_ref[...]
+        rows_ref[third : 2 * third, :] = side_ref[...]
+        rows_ref[2 * third :, :] = core_ref[...]
+        field = dot(rows_ref[...], w_ref[...])
+        qk_ref[...] = field[:, : 2 * HD]
+        v_ref[...] = field[:, 2 * HD :].astype(LOW)
+
+    operands = [*pieces, w_all]
+    return in_place(
+        body,
+        g,
+        last,
+        0,
+        operands,
+        grid=(1,),
+        in_specs=[fixed(third, width), fixed(third, width), fixed(2 * third, width), fixed(width, 3 * HD)],
+        out_specs=[fixed(count, width, g), fixed(count, 2 * HD, g), fixed(count, HD, g)],
+        outs=[
+            jax.ShapeDtypeStruct((groups * count, width), LOW),
+            jax.ShapeDtypeStruct((groups * count, 2 * HD), HIGH),
+            jax.ShapeDtypeStruct((groups * count, HD), LOW),
+        ],
+        compiler_params=kernel_params(58),
+        cost_estimate=cost(count * width * 3 * HD, 6 * count * width),
+        name="project_group",
+    )(*operands, *(last or ()))
+
+
+def expert_group(g, pieces, last, groups, grad_all, info, routed, g_weight, u_weight, d_weight, r_wide, experts):
+    count, width = 4 * pieces[0].shape[0], pieces[0].shape[1]
+    hidden_width = g_weight.shape[1]
+    chunk = 256
+    block = count // 4
+
+    def body(info_ref, near_ref, side_ref, core_ref, grad0, grad1, grad2, grad3, routed_ref, wg_ref, wu_ref, wd_ref, wr_ref, rows_ref, grad_ref, hid_ref, gated_ref, dg_ref, du_ref, sum_ref, prob_ref, gate_s):
+        @pl.when(pl.program_id(0) == 0)
+        def _():
+            rows_ref[:block, :] = near_ref[...]
+            rows_ref[block : 2 * block, :] = side_ref[...]
+            rows_ref[2 * block :, :] = core_ref[...]
+            for i, ref in enumerate((grad0, grad1, grad2, grad3)):
+                grad_ref[i * block : (i + 1) * block, :] = ref[...]
+            lane = lax.broadcasted_iota(jnp.int32, (count, r_wide.shape[1]), 1)
+            logits = jnp.where(lane < experts, dot(rows_ref[...], wr_ref[...]), MASK_FLOOR)
+            expo = jnp.exp(logits - jnp.max(logits, axis=1, keepdims=True))
+            prob = expo / jnp.sum(expo, axis=1, keepdims=True)
+            own = jnp.sum(jnp.where(lane == info_ref[16], prob, 0.0), axis=1, keepdims=True)
+            gate = own * routed_ref[...]
+            gate_s[...] = jnp.broadcast_to(gate, gate_s.shape)
+            prob_ref[...] = jnp.where(lane[:, :HD] == 0, own, gate)
+            sum_ref[...] = jnp.zeros_like(sum_ref)
+
+        rows = rows_ref[...]
+        gate_pre = dot(rows, wg_ref[...])
+        up_pre = dot(rows, wu_ref[...])
+        raw = dot(grad_ref[...], wd_ref[...], ((1,), (1,)))
+        sigma = 1.0 / (1.0 + jnp.exp(-gate_pre))
+        act = gate_pre * sigma
+        hidden = (act * up_pre).astype(LOW)
+        wide = hidden.astype(HIGH)
+        product = wide * raw
+        total = product[:, :HD]
+        for i in range(1, chunk // HD):
+            total = total + product[:, i * HD : (i + 1) * HD]
+        sum_ref[...] += total
+        gate = gate_s[:, :1]
+        d_hidden = gate * raw
+        hid_ref[...] = hidden
+        gated_ref[...] = (gate * wide).astype(LOW)
+        dg_ref[...] = (d_hidden * up_pre * (sigma * (1.0 + gate_pre * (1.0 - sigma)))).astype(LOW)
+        du_ref[...] = (d_hidden * act).astype(LOW)
+
+    by_column = pl.BlockSpec((width, chunk), lambda j, info: (0, j))
+    out_chunk = pl.BlockSpec((count, chunk), lambda j, info: (g, j))
+    operands = [*pieces, *[grad_all] * 4, routed, g_weight, u_weight, d_weight, r_wide]
+    full = groups * count
+    return in_place(
+        body,
+        g,
+        last,
+        1,
+        operands,
+        grid=(hidden_width // chunk,),
+        in_specs=[fixed(block, width), fixed(block, width), fixed(2 * block, width)]
+        + [
+            pl.BlockSpec((block, width), lambda j, info, i=i: (info[4 * g + i], 0))
+            for i in range(4)
+        ]
+        + [
+            fixed(count, 1, g),
+            by_column,
+            by_column,
+            pl.BlockSpec((chunk, width), lambda j, info: (j, 0)),
+            fixed(width, r_wide.shape[1]),
+        ],
+        out_specs=[fixed(count, width, g)] * 2 + [out_chunk] * 4 + [fixed(count, HD, g)] * 2,
+        outs=[jax.ShapeDtypeStruct((full, width), LOW)] * 2
+        + [jax.ShapeDtypeStruct((full, hidden_width), LOW)] * 4
+        + [jax.ShapeDtypeStruct((full, HD), HIGH)] * 2,
+        scratch_shapes=(pltpu.VMEM((count, HD), HIGH),),
+        compiler_params=kernel_params(56),
+        cost_estimate=cost(3 * count * width * hidden_width, 8 * width * hidden_width),
+        name="expert_group",
+    )(info, *operands, *(last or ()))
+
+
+def copies_group(g, d_gate, d_up, g_weight, u_weight, d_log, r_row, groups):
+    count, hidden_width = d_gate.shape[0] // groups, d_gate.shape[1]
+    width = g_weight.shape[0]
+    chunk = 512
+
+    def body(dg_ref, du_ref, wg_ref, wu_ref, log_ref, r_ref, out_ref):
+        made = dot(dg_ref[...], wg_ref[...], ((1,), (1,)))
+        made = made + dot(du_ref[...], wu_ref[...], ((1,), (1,)))
+        out_ref[...] = (made + log_ref[...] * r_ref[...]).astype(LOW)
+
+    by_row = pl.BlockSpec((chunk, hidden_width), lambda j: (j, 0))
+    return pl.pallas_call(
+        body,
+        grid=(width // chunk,),
+        in_specs=[
+            fixed(count, hidden_width, g),
+            fixed(count, hidden_width, g),
+            by_row,
+            by_row,
+            fixed(count, 1, g),
+            pl.BlockSpec((1, chunk), lambda j: (0, j)),
+        ],
+        out_specs=pl.BlockSpec((count, chunk), lambda j: (0, j)),
+        out_shape=jax.ShapeDtypeStruct((count, width), LOW),
+        compiler_params=kernel_params(32),
+        cost_estimate=cost(2 * count * width * hidden_width, 4 * width * hidden_width),
+        name="copies_group",
+    )(d_gate, d_up, g_weight, u_weight, d_log, r_row)
 
 
 def local(
@@ -341,37 +609,47 @@
     slot_own = swap_ws(attn_in.reshape(SLOTS, slot_rows, width)).reshape(tokens, width)
     state = {}
 
+    halves = [own_gate[: own_gate.shape[0] // 2], own_gate[own_gate.shape[0] // 2 :]]
+    halves += [own_up[: own_up.shape[0] // 2], own_up[own_up.shape[0] // 2 :]]
+
     def second_fill():
-        state["gate"] = other_ws(after(own_gate, slot_own))
-        return state["gate"], rope_tables(pos_slot)
-
-    def project(g, rows_in):
+        state["came"] = [other_ws(after(halves[0], slot_own))]
+        return state["came"][0], rope_tables(pos_slot)
+
+    def send_half(i, event):
+        state["came"].append(other_ws(after(halves[i], event)))
+
+    def project(g, pieces, last=None):
         if g == 0:
             head_rows = came[None, :, :rows]
-            both = whole_ws(head_rows, other_ws(after(head_rows, state["gate"])))
+            both = whole_ws(head_rows, other_ws(after(head_rows, state["came"][0])))
             state["head"] = both.transpose(1, 0, 2, 3).reshape(width, head_width)
-        field = dot(rows_in, state["head"][:, : 3 * HD])
+            send_half(1, state["head"])
+        if net.groups == 1:
+            field = dot(pieces[0], state["head"][:, : 3 * HD])
+            out = [pieces[0], field[:, : 2 * HD], field[:, 2 * HD :].astype(LOW)]
+        else:
+            out = list(project_group(g, pieces, last, net.groups, state["head"]))
+        if g == min(1, net.groups - 1):
+            out[0], state["came"][1] = lax.optimization_barrier((out[0], state["came"][1]))
+            send_half(2, state["came"][1])
         if g == net.groups - 1:
-            came_up = other_ws(after(own_up, state["head"]))
-            field, state["up"] = lax.optimization_barrier((field, came_up))
-        return field
-
-    slot_groups, ((came, *_), (came_gate, (cosine, sine))), qkv = net.gather(
+            out[0], state["came"][2] = lax.optimization_barrier((out[0], state["came"][2]))
+            send_half(3, state["came"][2])
+        return out
+
+    ((came, *_), (first_half, (cosine, sine))), (slot_in, qk_pre, v_low) = net.gather(
         slot_own, [first_fill, second_fill], project
     )
     w_head_all = state["head"]
     w_head = w_head_all[:, : 3 * HD]
-    r_weight = w_head_all[:, 3 * HD : 3 * HD + experts]
+    r_wide = w_head_all[:, 3 * HD :]
+    r_weight = r_wide[:, :experts]
     routed = net.from_whole(came[:, rows, :tokens].astype(HIGH)).reshape(span, 1) > 0.5
-    came_up = state["up"]
-    o_weight = lax.all_gather(after(w_out.astype(LOW), qkv[0]), ("ctx", "ws"), axis=0, tiled=True)
+    o_weight = lax.all_gather(after(w_out.astype(LOW), first_half), ("ctx", "ws"), axis=0, tiled=True)
     grad_own = jnp.where(live_own, out_grad.reshape(tokens, width), 0).astype(LOW)
-    grad_all = lax.all_gather(after(grad_own, qkv[0]), "ctx", axis=0, tiled=True)
-    slot_in = jnp.concatenate(slot_groups, axis=0)
-    qkv = jnp.concatenate(qkv, axis=0)
-
-    q_pre, k_pre = qkv[:, :HD], qkv[:, HD : 2 * HD]
-    v_low = qkv[:, 2 * HD :].astype(LOW)
+    grad_all = lax.all_gather(after(grad_own, first_half), "ctx", axis=0, tiled=True)
+    q_pre, k_pre = qk_pre[:, :HD], qk_pre[:, HD:]
 
     def sum_heads(first, second):
         both = jnp.concatenate(
@@ -397,17 +675,8 @@
 
     q_part = of_part(q_low)
     pos_query = of_part(pos_slot)
-    score_scale = HD ** (-0.5)
-    visible = (pos_slot[None, :] <= pos_query[:, None]) & live_slot[None, :]
-    scores = jnp.where(visible, dot(q_part, k_low, ((1,), (1,))) * score_scale, MASK_FLOOR)
-    row_max = jnp.max(scores, axis=1, keepdims=True)
-    expo = jnp.exp(scores - row_max)
-    row_sum = jnp.sum(expo, axis=1, keepdims=True)
-    attn_head = dot((expo / row_sum).astype(LOW), v_low)
-    log_total = row_max + jnp.log(row_sum)
-    attn_head_low, came_down = lax.optimization_barrier(
-        (attn_head.astype(LOW), other_ws(after(own_down, came_up)))
-    )
+    pos_key = jnp.where(live_slot, pos_slot, jnp.int32(2**30))
+    attn_head, attn_head_low, log_total = attend(q_part, k_low, v_low, pos_query, pos_key)
 
     attn_whole = net.move(attn_head_low, True)
     out_chunks = attn_whole.reshape(heads, tokens, HD)
@@ -416,15 +685,18 @@
             jnp.zeros((ctx_count, tokens, HD), LOW), out_chunks, part * heads, 0
         )
     came = lax.all_to_all(out_chunks, "ctx", 0, 0, tiled=True)
-    came, g_weight, u_weight = lax.optimization_barrier(
-        (came, whole_ws(own_gate, came_gate), whole_ws(own_up, came_up))
-    )
+    came, last_half = lax.optimization_barrier((came, state["came"][3]))
+    came_gate = jnp.concatenate([first_half, state["came"][1]], axis=0)
+    came_up = jnp.concatenate([state["came"][2], last_half], axis=0)
+    g_weight, u_weight = whole_ws(own_gate, came_gate), whole_ws(own_up, came_up)
     if parts > 1:
         came = lax.dynamic_index_in_dim(
             came.reshape(heads, parts, tokens, HD), own_part, 1, keepdims=False
         )
     attn_rows = came.transpose(1, 0, 2).reshape(ws_count, slot_rows, width)
     attn_low = swap_ws(attn_rows).reshape(tokens, width)
+    half_down = own_down.shape[0] // 2
+    down_first = other_ws(after(own_down[:half_down], attn_low))
 
     mid = x + dot(attn_low, o_weight)
     mid_scale = inv_rms(mid)
@@ -433,45 +705,63 @@
         size = span // net.groups
         return lax.slice_in_dim(field, g * size, (g + 1) * size, axis=0)
 
-    half = net.groups // 2
-
-    grad_plane = net.move(grad_all, False)
-
-    d_weight = whole_ws(own_down, came_down)
-    grad_plane = after(grad_plane, ffn_in)
-
-    def raw_first():
-        return [dot(group(grad_plane, g), d_weight, ((1,), (1,))) for g in range(half)]
-
-    def raw_second():
-        return [dot(group(grad_plane, g), d_weight, ((1,), (1,))) for g in range(half, net.groups)]
-
-    def expert(g, rows_in):
+    def expert_plain(rows_in):
         router_prob = jax.nn.softmax(dot(rows_in, r_weight), axis=-1)
         prob_own = lax.dynamic_slice_in_dim(router_prob, c, 1, 1)
-        gate = jnp.where(group(routed, g), prob_own, 0.0)
-        return prob_own, gate, dot(rows_in, g_weight), dot(rows_in, u_weight)
-
-    plane_groups, raw, forward = net.gather(ffn_in, [raw_first, raw_second], expert)
-    raw = raw[0] + raw[1]
-    kept = []
-    for g in range(net.groups):
-        prob_own, gate, gate_pre, up_pre = forward[g]
-        d_hidden_raw = raw[g]
+        gate = jnp.where(routed, prob_own, 0.0)
+        gate_pre, up_pre = dot(rows_in, g_weight), dot(rows_in, u_weight)
+        raw = dot(grad_all, state["d"], ((1,), (1,)))
         sigma = jax.nn.sigmoid(gate_pre)
         act = gate_pre * sigma
         hidden = (act * up_pre).astype(LOW)
-        d_gate = jnp.sum(hidden.astype(HIGH) * d_hidden_raw, axis=1, keepdims=True)
-        d_gate = jnp.where(group(routed, g), d_gate, 0.0)
-        d_hidden = gate * d_hidden_raw
+        wide = hidden.astype(HIGH)
+        d_gate = jnp.where(routed, jnp.sum(wide * raw, axis=1, keepdims=True), 0.0)
+        d_hidden = gate * raw
         d_gate_low = (d_hidden * up_pre * (sigma * (1.0 + gate_pre * (1.0 - sigma)))).astype(LOW)
         d_up_low = (d_hidden * act).astype(LOW)
-        hidden_gated = (gate * hidden.astype(HIGH)).astype(LOW)
-        kept.append((prob_own, gate, hidden, hidden_gated, d_gate, d_gate_low, d_up_low))
-    prob_own, gate, hidden, hidden_gated, d_gate, d_gate_low, d_up_low = (
-        jnp.concatenate(fields, axis=0) for fields in zip(*kept)
-    )
-    plane_in = jnp.concatenate(plane_groups, axis=0)
+        return prob_own, gate, hidden, (gate * wide).astype(LOW), d_gate, d_gate_low, d_up_low
+
+    info = jnp.concatenate([net.order[:16], c.astype(jnp.int32)[None]])
+
+    def expert(g, pieces, last=None):
+        if g == 0:
+            came_down = jnp.concatenate([state["first"], state["second"]], axis=0)
+            state["d"] = whole_ws(own_down, after(came_down, pieces[-1]))
+        if net.groups == 1:
+            return (pieces[0], *expert_plain(pieces[0]))
+        return expert_group(
+            g,
+            pieces,
+            last,
+            net.groups,
+            grad_all,
+            info,
+            mask,
+            g_weight,
+            u_weight,
+            state["d"],
+            r_wide,
+            experts,
+        )
+
+    mask = routed.astype(HIGH)
+    def fill_first():
+        state["first"] = down_first
+        return down_first
+
+    def fill_second():
+        state["second"] = other_ws(after(own_down[half_down:], down_first))
+        return state["second"]
+
+    _, kept = net.gather(ffn_in, [fill_first, fill_second], expert)
+    d_weight = state["d"]
+    if net.groups == 1:
+        plane_in, prob_own, gate, hidden, hidden_gated, d_gate, d_gate_low, d_up_low = kept
+        grad_plane = grad_all
+    else:
+        plane_in, grad_plane, hidden, hidden_gated, d_gate_low, d_up_low, sums, prob = kept
+        d_gate = mask * jnp.sum(sums, axis=1, keepdims=True)
+        prob_own, gate = prob[:, :1], prob[:, 1:2]
 
     def grad_rows(left, right, device):
         count = left.shape[1] // ws_count
@@ -481,34 +771,56 @@
         return grad_rows(left, right, 1 - w).astype(LOW)
 
     def own(left, right, came):
+        right, came = lax.optimization_barrier((right, came))
         return (grad_rows(left, right, w) + came.astype(HIGH))[None]
 
     prob_sum = net.from_whole(sum_ctx(net.to_whole((prob_own * d_gate).reshape(ctx_count, tokens))))
     prob_sum, down_away = lax.optimization_barrier((prob_sum, away(hidden_gated, grad_plane)))
-    down_came = other_ws(down_away)
+
+    def cut(field):
+        return field[: field.shape[0] // 2], field[field.shape[0] // 2 :]
+
+    down_cut = cut(down_away)
+    down_came = [other_ws(down_cut[0])]
     d_log = (prob_own * (d_gate - prob_sum.reshape(span, 1))).astype(LOW)
     r_column = lax.dynamic_slice_in_dim(r_weight, c, 1, 1).reshape(1, width).astype(HIGH)
 
     def copies_back(g):
-        made = (
-            dot(kept[g][5], g_weight, ((1,), (1,)))
-            + dot(kept[g][6], u_weight, ((1,), (1,)))
-            + group(d_log, g).astype(HIGH) * r_column
+        if net.groups > 1:
+            log_column = d_log.astype(HIGH)
+            made = copies_group(
+                g, d_gate_low, d_up_low, g_weight, u_weight, log_column, r_column, net.groups
+            )
+            if g == 0:
+                made, down_came[0] = lax.optimization_barrier((made, down_came[0]))
+            return made
+        return (
+            dot(d_gate_low, g_weight, ((1,), (1,)))
+            + dot(d_up_low, u_weight, ((1,), (1,)))
+            + d_log.astype(HIGH) * r_column
         ).astype(LOW)
-        return made
 
     def results():
         produced = dot(hidden, d_weight).astype(LOW).astype(HIGH)
         return net.move((gate * produced).astype(LOW), True)
 
-    d_ffn, ((gated, down_came), gate_away) = net.scatter(
-        copies_back, [lambda: (results(), down_came), lambda: away(plane_in, d_gate_low)]
-    )
+    def fill_gate():
+        down_came.append(other_ws(after(down_cut[1], down_came[0])))
+        gate_away = away(plane_in, d_gate_low)
+        return gate_away, down_came[1]
+
+    def fill_results():
+        first = other_ws(after(cut(state["gate_away"])[0], down_came[1]))
+        return results(), first
+
+    def fill_both():
+        state["gate_away"], down_came[1] = lax.optimization_barrier(fill_gate())
+        return down_came[1]
+
+    d_ffn, (_, (gated, gate_first)) = net.scatter(copies_back, [fill_both, fill_results])
+    down_came = jnp.concatenate(down_came, axis=0)
     d_ffn = d_ffn.astype(HIGH)
-    mixture = lax.psum_scatter(gated, "ctx", scatter_dimension=0, tiled=True)
-    layer_out = (mid + mixture.astype(HIGH)).astype(LOW)
-
-    router_column = jnp.sum(plane_in.astype(HIGH) * d_log.astype(HIGH), axis=0)
+
 
     mid_hat = mid * mid_scale
     ffn_gain_part = jnp.sum(d_ffn * mid_hat, axis=0)
@@ -517,15 +829,17 @@
 
     d_attn = dot(d_mid_low, o_weight, ((1,), (1,))).astype(LOW)
     d_attn_rows = swap_ws(d_attn.reshape(SLOTS, slot_rows, width)).reshape(tokens, heads, HD)
-    gate_came = other_ws(after(gate_away, d_attn_rows))
+    gate_second = other_ws(after(cut(state["gate_away"])[1], d_attn_rows))
     in_chunks = d_attn_rows.transpose(1, 0, 2)
     if parts > 1:
         in_chunks = lax.dynamic_update_slice(
             jnp.zeros((heads, parts, tokens, HD), LOW), in_chunks[:, None], (0, own_part, 0, 0)
         ).reshape(ctx_count, tokens, HD)
     d_attn_head = lax.all_to_all(in_chunks, "ctx", 0, 0, tiled=True)
-    d_attn_head, up_away = lax.optimization_barrier((d_attn_head, away(plane_in, d_up_low)))
-    up_came = other_ws(up_away)
+    d_attn_head, gate_second, up_away = lax.optimization_barrier(
+        (d_attn_head, gate_second, away(plane_in, after(d_up_low, d_attn_rows)))
+    )
+    gate_came = jnp.concatenate([gate_first, gate_second], axis=0)
     if parts > 1:
         d_attn_head = lax.dynamic_slice_in_dim(d_attn_head, part * heads, heads, 0)
     d_attn_head = net.move(d_attn_head.reshape(part_span, HD), False)
@@ -536,15 +850,15 @@
         axis=0,
         tiled=True,
     )
+    mixture = lax.psum_scatter(
+        after(gated, slot_d_mid), "ctx", scatter_dimension=0, tiled=True
+    )
+    layer_out = (mid + mixture.astype(HIGH)).astype(LOW)
+
     delta = jnp.sum(d_attn_head.astype(HIGH) * attn_head, axis=1, keepdims=True)
-    prob = jnp.exp(
-        jnp.where(visible, dot(q_part, k_low, ((1,), (1,))) * score_scale, MASK_FLOOR) - log_total
-    )
-    d_prob = dot(d_attn_head, v_low, ((1,), (1,)))
-    d_score = (prob * (d_prob - delta)).astype(LOW)
-    d_q_part = (dot(d_score, k_low) * score_scale).astype(LOW)
-    d_k_rot = (dot(d_score, q_part, ((0,), (0,))) * score_scale).astype(LOW)
-    d_v_low = dot(prob.astype(LOW), d_attn_head, ((0,), (0,))).astype(LOW)
+    d_q_part, d_k_rot, d_v_low = attend_back(
+        q_part, k_low, v_low, d_attn_head, log_total, delta, pos_query, pos_key
+    )
     d_q_rot = d_q_part
     if parts > 1:
         d_q_rot = lax.dynamic_update_slice_in_dim(
@@ -556,28 +870,29 @@
     d_q_hat = d_q_norm * q_gain
     d_k_hat = d_k_norm * k_gain
     q_dot, k_dot = sum_heads(jnp.sum(d_q_hat * q_hat, axis=1), jnp.sum(d_k_hat * k_hat, axis=1))
-    q_dot, gate_came = lax.optimization_barrier((q_dot, gate_came))
     d_q_low = (q_scale * (d_q_hat - q_hat * q_dot)).astype(LOW)
     d_k_low = (k_scale * (d_k_hat - k_hat * k_dot)).astype(LOW)
     d_qkv = jnp.concatenate([d_q_low, d_k_low, d_v_low], axis=1)
 
-    head_grad = dot(slot_in, d_qkv, ((0,), (0,))).astype(LOW)
-    head_grad, d_qkv = lax.optimization_barrier((head_grad, d_qkv))
-    head_grad = head_grad.reshape(ctx_count, ws_count, rows, 3 * HD).transpose(1, 0, 2, 3)
-    head_grad = swap_ws(head_grad)
+    def head_grads():
+        field = dot(slot_in, d_qkv, ((0,), (0,))).astype(LOW)
+        return field.reshape(ctx_count, ws_count, rows, 3 * HD).transpose(1, 0, 2, 3)
+
+    up_cut = cut(up_away)
+    up_first = other_ws(after(up_cut[0], d_v_low))
 
     def make_d_in(g):
         made = dot(group(d_qkv, g), w_head, ((1,), (1,))).astype(LOW)
-        if g == 2:
+        if g == min(2, net.groups - 1):
+            made, head_grad, state["up"] = lax.optimization_barrier((made, head_grads(), up_first))
+            state["head_grad"] = swap_ws(after(head_grad, state["up"]))
+        if g == min(1, net.groups - 1):
             state["down"] = own(hidden_gated, grad_plane, down_came)
-            return lax.optimization_barrier((made, state["down"]))[0]
-        if g == 1:
+            made, _ = lax.optimization_barrier((made, state["down"]))
+        if g == 0:
+            state["sum"] = jnp.sum(state["head_grad"].astype(HIGH), axis=0).astype(LOW)
             state["gate"] = own(plane_in, d_gate_low, gate_came)
-            return lax.optimization_barrier((made, state["gate"]))[0]
-        if g == 0:
-            state["sum"] = jnp.sum(head_grad.astype(HIGH), axis=0).astype(LOW)
-            state["up"] = own(plane_in, d_up_low, up_came)
-            made, state["sum"], _ = lax.optimization_barrier((made, state["sum"], state["up"]))
+            made, state["sum"], _ = lax.optimization_barrier((made, state["sum"], state["gate"]))
         return made
 
     def out_grad_rows():
@@ -591,18 +906,25 @@
         sent = lax.dynamic_index_in_dim(out_rows, 1 - w, 0, keepdims=False).astype(LOW)
         return mine, sent
 
+    def fill_rows():
+        state["up_second"] = other_ws(after(up_cut[1], state["sum"]))
+        return out_grad_rows(), state["up_second"]
+
+    def fill_up():
+        came = jnp.concatenate([state["up"], state["up_second"]], axis=0)
+        grad = own(plane_in, d_up_low, came)
+        return lax.all_to_all(state["sum"], "ctx", 0, 0, tiled=True), grad
+
     groups = [[h * parts + i for i in range(parts)] for h in range(heads)]
-    d_in_sum, ((out_mine, out_sent), col_grad) = net.scatter(
+    d_in_sum, (((out_mine, out_sent), _), (col_grad, grad_w_up)) = net.scatter(
         make_d_in,
-        [out_grad_rows, lambda: lax.all_to_all(state["sum"], "ctx", 0, 0, tiled=True)],
-    )
-    if net.groups == 1:
-        state["down"] = own(hidden_gated, grad_plane, down_came)
-        state["gate"] = own(plane_in, d_gate_low, gate_came)
+        [fill_rows, fill_up],
+    )
     grad_w_out = out_mine + other_ws(out_sent).astype(HIGH)
     d_in = swap_ws(d_in_sum.reshape(ws_count, slot_rows, width)).reshape(tokens, width)
     grad_input = d_mid + rms_back(x, x_scale, d_in.astype(HIGH) * attn_gain)
 
+    router_column = jnp.sum(plane_in.astype(HIGH) * after(d_log, d_v_low).astype(HIGH), axis=0)
     small = jnp.stack([ffn_gain_part, router_column]).reshape(2, ctx_count, ws_count, rows)
     small = lax.all_to_all(
         small.transpose(1, 2, 0, 3).reshape(ctx_count, 2 * ws_count * rows), "ctx", 0, 0, tiled=True
@@ -638,7 +960,7 @@
         grad_w_out,
         grad_w_router,
         state["gate"],
-        state["up"],
+        grad_w_up,
         state["down"],
     )
 

time: 850 us -> 815 us (0.959)
  matrix products: 232 us -> 95.5 us
  Pallas kernels: 6.27 us -> 135 us
  waiting for transfers between devices: 234 us -> 204 us
  other arithmetic: 137 us -> 114 us
  local copies, waits for them, and re-layouts: 71 us -> 89 us
    dot_general x49 -> x15, matrix products: 232 us -> 95.5 us  [dot(): lax.dot_general(left, right, (dims, ((), ())), preferred_element_type=HIGH)]
    pallas_call x0 -> x14, Pallas kernels: none -> 130 us  [the longest x4 61.4 us: expert_group(): in_place(body, g, last, 1, operands, grid=(hidden_width // chunk,), in_sp...]
    convert_element_type x5, other arithmetic: 17 us -> 4.1 us  [the longest x1 2.71 us: copies_back(): log_column = d_log.astype(HIGH)]
    slice x2 -> x8, local copies, waits for them, and re-layouts: 0.07 us -> 11.8 us  [the longest x3 6.29 us: cut(): return (field[:field.shape[0] // 2], field[field.shape[0] // 2:])]
    ppermute x56, starting transfers between devices: 83.4 us -> 74.2 us  [send(): return lax.ppermute(field, 'ctx', pairs)]
    ppermute x8, waiting for transfers between devices: 32.8 us -> 23.8 us  [pair_ws(): came = lax.ppermute(away, 'ws', [(0, 1), (1, 0)])]
    unnamed x348 -> x299, local copies, waits for them, and re-layouts: 47.3 us -> 49.6 us
    ppermute x8 -> x14, waiting for transfers between devices: 71.7 us -> 71.5 us  [other_ws(): return lax.ppermute(field, 'ws', [(0, 1), (1, 0)])]
  transfers between devices with their start and end apart: 93 -> 99, of which waited for: 39 -> 28; matrix products, arithmetic and copies ran while one was open for 43% -> 29% of each run, Pallas kernels for 1% -> 14%
where the time goes in v3:
time: 815 us; the launch traced here: 803 us
  waiting for transfers between devices  204 us (25%)
  starting transfers between devices  149 us (18%)
  Pallas kernels  135 us (17%)
  other arithmetic  114 us (14%)
  matrix products  95.5 us (12%)
  local copies, waits for them, and re-layouts  89 us (11%)
  between operations  17 us (2%)
    dot_general x15, matrix products, dot(): lax.dot_general(left, right, (dims, ((), ())), preferred_element_type=HIGH)  95.5 us
    ppermute x56, waiting for transfers between devices, send(): return lax.ppermute(field, 'ctx', pairs)  88.7 us
    ppermute x56, starting transfers between devices, send(): return lax.ppermute(field, 'ctx', pairs)  74.2 us
    ppermute x14, waiting for transfers between devices, other_ws(): return lax.ppermute(field, 'ws', [(0, 1), (1, 0)])  71.5 us
    pallas_call x4, Pallas kernels, expert_group(): in_place(body, g, last, 1, operands, grid=(hidden_width // chunk,), in_sp...  61.4 us
    unnamed x299, local copies, waits for them, and re-layouts  49.6 us
    ppermute x12, starting transfers between devices, sum_ctx(): lax.ppermute(field, 'ctx', [(i, i ^ step) for i in range(count)])  25.8 us
    ppermute x8, waiting for transfers between devices, pair_ws(): came = lax.ppermute(away, 'ws', [(0, 1), (1, 0)])  23.8 us
  transfers between devices with their start and end apart: 99, of which 28 were waited for; matrix products, arithmetic and copies ran while one was open for 29% of the time, Pallas kernels for 14%

profile of v3, /device:TPU:0, one launch (start us, length us, event | category | flops | bytes accessed | tf_op | source)
XLA Modules:
  0.0 802.7 jit_solution(11067354386440846132)
XLA Ops:
  40.5 20.1 %collective-permute-done.3 = bf16[128,2048]{1,0:T(8,128)(2,1)S(1)} collective-permute-done((bf16[128,2048]{1,0:T(8,128)(2,1)S(1)}, bf16[128,2048]{1,0:T(8,128)(2,1)S(1)}, u32[]{:S(2)}, u32[]{:S(2)}) %collective-permute-start.3) | collective-permute-done | bytes 524320 | tf_op jit(solution)/shard_map/ppermute | solution.py:103
  96.2 17.7 %collective-permute-done.13 = bf16[1,16,64,512]{3,2,1,0:T(8,128)(2,1)} collective-permute-done((bf16[1,16,64,512]{3,2,1,0:T(8,128)(2,1)}, bf16[1,16,64,512]{3,2,1,0:T(8,128)(2,1)}, u32[]{:S(2)}, u32[]{:S(2)}) %collective-permute-start.13) | collective-permute-done | bytes 1048608 | tf_op jit(solution)/shard_map/ppermute | solution.py:60
  137.9 9.7 %collective-permute-done.16 = bf16[512,1024]{1,0:T(8,128)(2,1)} collective-permute-done((bf16[512,1024]{1,0:T(8,128)(2,1)}, bf16[512,1024]{1,0:T(8,128)(2,1)}, u32[]{:S(2)}, u32[]{:S(2)}) %collective-permute-start.16) | collective-permute-done | bytes 1048608 | tf_op jit(solution)/shard_map/ppermute | solution.py:60
  190.8 10.7 %attend.1 = (f32[2048,128]{1,0:T(8,128)S(1)}, bf16[2048,128]{1,0:T(8,128)(2,1)S(1)}, f32[2048,1]{1,0:T(8,128)S(1)}) custom-call(bf16[2048,128]{1,0:T(8,128)(2,1)S(1)} %get-tuple-element.510.q_ref, bf16[2048,128]{1,0:T(8,128)(2,1)S(1)} %get-tuple-element.511.k_ref, bf16[2048,128]{1,0:T(8,128)(2,1)S(1)} %copy-done.11, s32[2048,1]{1,0:T(8,128)S(1)} %copy.119.pq_ref, ...), custom_call_target="tpu_custom_call" | custom-call | flops 8589934592 | bytes 2097152 | tf_op jit(solution)/shard_map/attend/pallas_call | solution.py:283
  220.5 10.6 %all-to-all-done.1 = bf16[16,128,128]{2,1,0:T(8,128)(2,1)S(1)} async-done(((bf16[16,128,128]{2,1,0:T(8,128)(2,1)}), bf16[16,128,128]{2,1,0:T(8,128)(2,1)S(1)}, u32[]{:S(2)}, u32[]{:S(2)}) %all-to-all-start.1) | async-done | bytes 524320 | tf_op jit(solution)/shard_map/all_to_all | solution.py:687
  258.5 8.7 %collective-permute-done.28 = bf16[256,2048]{1,0:T(8,128)(2,1)} collective-permute-done((bf16[256,2048]{1,0:T(8,128)(2,1)}, bf16[256,2048]{1,0:T(8,128)(2,1)}, u32[]{:S(2)}, u32[]{:S(2)}) %collective-permute-start.28) | collective-permute-done | bytes 1048608 | tf_op jit(solution)/shard_map/ppermute | solution.py:60
  267.8 10.3 %collective-permute-done.27 = bf16[128,2048]{1,0:T(8,128)(2,1)S(1)} collective-permute-done((bf16[128,2048]{1,0:T(8,128)(2,1)S(1)}, bf16[128,2048]{1,0:T(8,128)(2,1)S(1)}, u32[]{:S(2)}, u32[]{:S(2)}) %collective-permute-start.27) | collective-permute-done | bytes 524320 | tf_op jit(solution)/shard_map/ppermute | solution.py:103
  308.4 15.6 %expert_group.4 = (bf16[2048,2048]{1,0:T(8,128)(2,1)}, bf16[2048,2048]{1,0:T(8,128)(2,1)}, bf16[2048,1024]{1,0:T(8,128)(2,1)}, bf16[2048,1024]{1,0:T(8,128)(2,1)...) custom-call(s32[17]{0:T(128)} %pad_add_fusion.refs_0_, ...), custom_call_target="tpu_custom_call" | custom-call | flops 6442450944 | bytes 16777216 | tf_op jit(solution)/shard_map/expert_group/pallas_call | solution.py:467
  327.2 15.1 %expert_group.5 = (bf16[2048,2048]{1,0:T(8,128)(2,1)}, bf16[2048,2048]{1,0:T(8,128)(2,1)}, bf16[2048,1024]{1,0:T(8,128)(2,1)}, bf16[2048,1024]{1,0:T(8,128)(2,1)...) custom-call(s32[17]{0:T(128)} %pad_add_fusion.refs_0_, ...), custom_call_target="tpu_custom_call", output_to_operand_aliasing={{0}: (13, {}), {1}: (14, {}), {2}: (15, {}), {3}: (16, {}),... | custom-call | flops 6442450944 | bytes 16777216 | tf_op jit(solution)/shard_map/expert_group/pallas_call | solution.py:467
  343.4 15.2 %expert_group.6 = (bf16[2048,2048]{1,0:T(8,128)(2,1)}, bf16[2048,2048]{1,0:T(8,128)(2,1)}, bf16[2048,1024]{1,0:T(8,128)(2,1)}, bf16[2048,1024]{1,0:T(8,128)(2,1)...) custom-call(s32[17]{0:T(128)} %pad_add_fusion.refs_0_, ...), custom_call_target="tpu_custom_call", output_to_operand_aliasing={{0}: (13, {}), {1}: (14, {}), {2}: (15, {}), {3}: (16, {}),... | custom-call | flops 6442450944 | bytes 16777216 | tf_op jit(solution)/shard_map/expert_group/pallas_call | solution.py:467
  359.6 15.4 %expert_group.7 = (bf16[2048,2048]{1,0:T(8,128)(2,1)}, bf16[2048,2048]{1,0:T(8,128)(2,1)}, bf16[2048,1024]{1,0:T(8,128)(2,1)}, bf16[2048,1024]{1,0:T(8,128)(2,1)...) custom-call(s32[17]{0:T(128)} %pad_add_fusion.refs_0_, ...), custom_call_target="tpu_custom_call", output_to_operand_aliasing={{0}: (13, {}), {1}: (14, {}), {2}: (15, {}), {3}: (16, {}),... | custom-call | flops 6442450944 | bytes 16777216 | tf_op jit(solution)/shard_map/expert_group/pallas_call | solution.py:467
  394.6 9.9 %convolution_convert_fusion.4 = bf16[512,2048]{1,0:T(8,128)(2,1)} fusion(bf16[2048,2048]{1,0:T(8,128)(2,1)} %get-tuple-element.382, bf16[2048,1024]{1,0:T(8,128)(2,1)} %get-tuple-element.337, s32[]{:T(128)S(6)} %select_n.387), kind=kOutput, calls=%fused_computation.21 | convolution fusion | flops 4296015872 | bytes 12582916 | tf_op jit(solution)/shard_map/dot_general | solution.py:22
  480.3 10.0 %collective-permute-done.57 = bf16[256,2048]{1,0:T(8,128)(2,1)S(1)} collective-permute-done((bf16[256,2048]{1,0:T(8,128)(2,1)S(1)}, bf16[256,2048]{1,0:T(8,128)(2,1)S(1)}, u32[]{:S(2)}, u32[]{:S(2)}) %collective-permute-start.57) | collective-permute-done | bytes 1048608 | tf_op jit(solution)/shard_map/ppermute | solution.py:60
  504.9 9.4 %multiply_convert_fusion.in0.in1.in2.in3 = bf16[2048,2048]{1,0:T(8,128)(2,1)S(1)} fusion(f32[2048]{0:T(1024)S(1)} %get-tuple-element.428, bf16[2048,1024]{1,0:T(8,128)(2,1)S(1)} %copy-done.27, bf16[512,2048]{1,0:T(8,128)(2,1)S(1)} %copy-done.50, bf16[512,2048]{1,0:T(8,128)(2,1)S(1)} %copy-done.48), kind=kOutput, calls=%fused_computation.1 | convolution fusion | flops 8615100416 | bytes 16785408 | tf_op jit(solution)/shard_map/dot_general | solution.py:22
  531.2 7.0 convolution_convert_fusion.6
  551.1 10.9 %add_bitcast_fusion.2 = f32[1,512,2048]{2,1,0:T(8,128)} fusion(bf16[512,2048]{1,0:T(8,128)(2,1)S(1)} %pad_maximum_fusion.4, bf16[2048,2048]{1,0:T(8,128)(2,1)} %get-tuple-element.382, bf16[2048,1024]{1,0:T(8,128)(2,1)} %get-tuple-element.337, s32[]{:T(128)S(6)} %select_n.399), kind=kOutput, calls=%fused_computation.7 | convolution fusion | flops 4297064448 | bytes 16777220 | tf_op jit(solution)/shard_map/dot_general | solution.py:22
  562.1 9.4 %fusion.15 = bf16[1024,1024]{1,0:T(8,128)(2,1)} fusion(bf16[2048,1024]{1,0:T(8,128)(2,1)} %get-tuple-element.407.du_ref, bf16[2048,2048]{1,0:T(8,128)(2,1)} %get-tuple-element.352, s32[]{:T(128)S(6)} %select_n.390), kind=kOutput, calls=%fused_computation.47 | convolution fusion | flops 4296015872 | bytes 10485764 | tf_op jit(solution)/shard_map/dot_general | solution.py:22
  580.3 17.3 %attend_back.1 = (bf16[2048,128]{1,0:T(8,128)(2,1)}, bf16[2048,128]{1,0:T(8,128)(2,1)}, bf16[2048,128]{1,0:T(8,128)(2,1)}) custom-call(bf16[2048,128]{1,0:T(8,128)(2,1)} %copy-done.19, bf16[2048,128]{1,0:T(8,128)(2,1)} %copy-done.20, bf16[2048,128]{1,0:T(8,128)(2,1)} %get-tuple-element.255.v_ref, bf16[2048,128]{1,0:T(8,128)(2,1)} %move_small.3.do_ref, ...), custom_call_target="tpu_custom_call" | custom-call | flops 12884901888 | bytes 2097152 | tf_op jit(solution)/shard_map/attend_back/pallas_call | solution.py:332
  628.0 8.3 %add_bitcast_fusion.1 = f32[1,1024,1024]{2,1,0:T(8,128)} fusion(bf16[1024,1024]{1,0:T(8,128)(2,1)S(1)} %pad_maximum_fusion.5, bf16[2048,1024]{1,0:T(8,128)(2,1)S(1)} %copy-done.6, bf16[2048,2048]{1,0:T(8,128)(2,1)} %get-tuple-element.352, s32[]{:T(128)S(6)} %select_n.403), kind=kOutput, calls=%fused_computation.6 | convolution fusion | flops 4297064448 | bytes 14680068 | tf_op jit(solution)/shard_map/dot_general | solution.py:22
  649.8 8.7 %convolution_convert_fusion.5 = bf16[2048,384]{1,0:T(8,128)(2,1)S(1)} fusion(bf16[2048,2048]{1,0:T(8,128)(2,1)} %get-tuple-element.376, bf16[2048,128]{1,0:T(8,128)(2,1)S(1)} %copy-done.115, bf16[2048,128]{1,0:T(8,128)(2,1)S(1)} %copy-done.90, bf16[2048,128]{1,0:T(8,128)(2,1)S(1)} %copy-done.88), kind=kOutput, calls=%fused_computation.22 | convolution fusion | flops 3226730496 | bytes 11534336 | tf_op jit(solution)/shard_map/dot_general | solution.py:22
  663.5 13.7 %collective-permute-done.77 = bf16[16,64,384]{2,1,0:T(8,128)(2,1)S(1)} collective-permute-done((bf16[16,64,384]{2,1,0:T(8,128)(2,1)S(1)}, bf16[16,64,384]{2,1,0:T(8,128)(2,1)S(1)}, u32[]{:S(2)}, u32[]{:S(2)}) %collective-permute-start.77) | collective-permute-done | bytes 786464 | tf_op jit(solution)/shard_map/ppermute | solution.py:47
  692.1 9.8 %collective-permute-done.82 = bf16[512,1024]{1,0:T(8,128)(2,1)} collective-permute-done((bf16[512,1024]{1,0:T(8,128)(2,1)}, bf16[512,1024]{1,0:T(8,128)(2,1)}, u32[]{:S(2)}, u32[]{:S(2)}) %collective-permute-start.82) | collective-permute-done | bytes 1048608 | tf_op jit(solution)/shard_map/ppermute | solution.py:60
  722.3 20.6 %collective-permute-done.78 = bf16[128,2048]{1,0:T(8,128)(2,1)S(1)} collective-permute-done((bf16[128,2048]{1,0:T(8,128)(2,1)S(1)}, bf16[128,2048]{1,0:T(8,128)(2,1)S(1)}, u32[]{:S(2)}, u32[]{:S(2)}) %collective-permute-start.78) | collective-permute-done | bytes 524320 | tf_op jit(solution)/shard_map/ppermute | solution.py:103
  762.9 14.5 %collective-permute-done.84 = bf16[128,2048]{1,0:T(8,128)(2,1)S(1)} collective-permute-done((bf16[128,2048]{1,0:T(8,128)(2,1)}, bf16[128,2048]{1,0:T(8,128)(2,1)S(1)}, u32[]{:S(2)}, u32[]{:S(2)}) %collective-permute-start.84) | collective-permute-done | bytes 524320 | tf_op jit(solution)/shard_map/ppermute | solution.py:103
  (734 shorter events, 487.0 us)
Async XLA Ops:
  19.2 43.0 %all-to-all-start = ((bf16[16,80,512]{2,1,0:T(8,128)(2,1)}), bf16[16,80,512]{2,1,0:T(8,128)(2,1)S(1)}, u32[]{:S(2)}, u32[]{:S(2)}) async-start(bf16[16,80,512]{2,1,0:T(8,128)(2,1)} %pad_maximum_fusion.8), calls=%async_computation | async-start | bytes 2621440 | tf_op jit(solution)/shard_map/all_to_all | solution.py:600
  25.2 218.1 %all-gather.4.cloned.1.call-start = ((), (), s32[]{:S(2)}) async-start(), calls=%async_computation.6 | async-start | bytes 8650752 | tf_op jit(solution)/shard_map/all_gather | solution.py:649
  30.6 30.0 %collective-permute-start.3 = (bf16[128,2048]{1,0:T(8,128)(2,1)S(1)}, bf16[128,2048]{1,0:T(8,128)(2,1)S(1)}, u32[]{:S(2)}, u32[]{:S(2)}) collective-permute-start(bf16[128,2048]{1,0:T(8,128)(2,1)S(1)} %bitcast.308), channel_id=1, source_target_pairs={{8,0},{10,2},{12,4},{14,6},{16,8},{18,10},{20,12},{22,14},{24,16},... | collective-permute-start | bytes 1572872 | tf_op jit(solution)/shard_map/ppermute | solution.py:103
  31.9 28.7 %collective-permute-start.2 = (bf16[128,2048]{1,0:T(8,128)(2,1)S(1)}, bf16[128,2048]{1,0:T(8,128)(2,1)S(1)}, u32[]{:S(2)}, u32[]{:S(2)}) collective-permute-start(bf16[128,2048]{1,0:T(8,128)(2,1)S(1)} %bitcast.309), channel_id=1, source_target_pairs={{0,8},{2,10},{4,12},{6,14},{8,16},{10,18},{12,20},{14,22},{16,24},... | collective-permute-start | bytes 1572872 | tf_op jit(solution)/shard_map/ppermute | solution.py:103
  40.0 34.7 %collective-permute-start.8 = (bf16[512,1024]{1,0:T(8,128)(2,1)}, bf16[512,1024]{1,0:T(8,128)(2,1)}, u32[]{:S(2)}, u32[]{:S(2)}) collective-permute-start(bf16[512,1024]{1,0:T(8,128)(2,1)} %get-tuple-element.219), channel_id=1, source_target_pairs={{0,1},{1,0},{2,3},{3,2},{4,5},{5,4},{6,7},{7,6},{8,9},{9,8},{10,11... | collective-permute-start | bytes 3145736 | tf_op jit(solution)/shard_map/ppermute | solution.py:60
  86.4 222.1 %all-gather.6.cloned.1.call-start = ((), (), s32[]{:S(2)}) async-start(), calls=%async_computation.7 | async-start | bytes 8912896 | tf_op jit(solution)/shard_map/all_gather | solution.py:651
  89.3 33.1 %collective-permute-start.11 = (bf16[128,2048]{1,0:T(8,128)(2,1)}, bf16[128,2048]{1,0:T(8,128)(2,1)S(1)}, u32[]{:S(2)}, u32[]{:S(2)}) collective-permute-start(bf16[128,2048]{1,0:T(8,128)(2,1)} %collective-permute-done.6), channel_id=1, source_target_pairs={{8,0},{10,2},{12,4},{14,6},{9,1},{11,3},{13,5},{15,7}} | collective-permute-start | bytes 1572872 | tf_op jit(solution)/shard_map/ppermute | solution.py:103
  90.6 31.8 %collective-permute-start.10 = (bf16[128,2048]{1,0:T(8,128)(2,1)S(1)}, bf16[128,2048]{1,0:T(8,128)(2,1)}, u32[]{:S(2)}, u32[]{:S(2)}) collective-permute-start(bf16[128,2048]{1,0:T(8,128)(2,1)S(1)} %collective-permute-done.5), channel_id=1, source_target_pairs={{16,24},{18,26},{20,28},{22,30},{17,25},{19,27},{21,29},{23,31}} | collective-permute-start | bytes 1572872 | tf_op jit(solution)/shard_map/ppermute | solution.py:103
  93.4 29.0 %collective-permute-start.12 = (bf16[256,2048]{1,0:T(8,128)(2,1)S(1)}, bf16[256,2048]{1,0:T(8,128)(2,1)S(1)}, u32[]{:S(2)}, u32[]{:S(2)}) collective-permute-start(bf16[256,2048]{1,0:T(8,128)(2,1)S(1)} %pad_maximum_fusion.10), channel_id=1, source_target_pairs={{0,2},{2,0},{4,6},{6,4},{8,10},{10,8},{12,14},{14,12},{16,18},{18,... | collective-permute-start | bytes 3145736 | tf_op jit(solution)/shard_map/ppermute | solution.py:103
  117.0 30.7 %collective-permute-start.16 = (bf16[512,1024]{1,0:T(8,128)(2,1)}, bf16[512,1024]{1,0:T(8,128)(2,1)}, u32[]{:S(2)}, u32[]{:S(2)}) collective-permute-start(bf16[512,1024]{1,0:T(8,128)(2,1)} %get-tuple-element.236), channel_id=1, source_target_pairs={{0,1},{1,0},{2,3},{3,2},{4,5},{5,4},{6,7},{7,6},{8,9},{9,8},{10,11... | collective-permute-start | bytes 3145736 | tf_op jit(solution)/shard_map/ppermute | solution.py:60
  151.1 35.9 %collective-permute-start.22 = (bf16[512,1024]{1,0:T(8,128)(2,1)}, bf16[512,1024]{1,0:T(8,128)(2,1)}, u32[]{:S(2)}, u32[]{:S(2)}) collective-permute-start(bf16[512,1024]{1,0:T(8,128)(2,1)} %get-tuple-element.259), channel_id=1, source_target_pairs={{0,1},{1,0},{2,3},{3,2},{4,5},{5,4},{6,7},{7,6},{8,9},{9,8},{10,11... | collective-permute-start | bytes 3145736 | tf_op jit(solution)/shard_map/ppermute | solution.py:60
  187.0 44.1 %collective-permute-start.23 = (bf16[512,1024]{1,0:T(8,128)(2,1)}, bf16[512,1024]{1,0:T(8,128)(2,1)}, u32[]{:S(2)}, u32[]{:S(2)}) collective-permute-start(bf16[512,1024]{1,0:T(8,128)(2,1)} %get-tuple-element.261), channel_id=1, source_target_pairs={{0,1},{1,0},{2,3},{3,2},{4,5},{5,4},{6,7},{7,6},{8,9},{9,8},{10,11... | collective-permute-start | bytes 3145736 | tf_op jit(solution)/shard_map/ppermute | solution.py:60
  212.7 431.1 %all-gather.8.cloned.1.call-start = ((), (), s32[]{:S(2)}) async-start(), calls=%async_computation.8 | async-start | bytes 8912896 | tf_op jit(solution)/shard_map/all_gather | solution.py:847
  249.5 28.6 %collective-permute-start.27 = (bf16[128,2048]{1,0:T(8,128)(2,1)S(1)}, bf16[128,2048]{1,0:T(8,128)(2,1)S(1)}, u32[]{:S(2)}, u32[]{:S(2)}) collective-permute-start(bf16[128,2048]{1,0:T(8,128)(2,1)S(1)} %multiply_convert_fusion.4.refs_1_), channel_id=1, source_target_pairs={{8,0},{10,2},{12,4},{14,6},{16,8},{18,10},{20,12},{22,14},{24,16},... | collective-permute-start | bytes 1572872 | tf_op jit(solution)/shard_map/ppermute | solution.py:103
  430.3 35.0 %collective-permute-start.52 = (bf16[256,2048]{1,0:T(8,128)(2,1)}, bf16[256,2048]{1,0:T(8,128)(2,1)}, u32[]{:S(2)}, u32[]{:S(2)}) collective-permute-start(bf16[256,2048]{1,0:T(8,128)(2,1)} %get-tuple-element.462), channel_id=1, source_target_pairs={{0,1},{1,0},{2,3},{3,2},{4,5},{5,4},{6,7},{7,6},{8,9},{9,8},{10,11... | collective-permute-start | bytes 3145736 | tf_op jit(solution)/shard_map/ppermute | solution.py:60
  603.9 83.6 %all-to-all-start.4 = ((f32[16,1,256]{2,1,0:T(1,128)}), f32[16,1,256]{2,1,0:T(1,128)S(1)}, u32[]{:S(2)}, u32[]{:S(2)}) async-start(f32[16,1,256]{2,1,0:T(1,128)} %all_to_all.27), calls=%async_computation.5 | async-start | bytes 32768 | tf_op jit(solution)/shard_map/all_to_all | solution.py:929
  609.8 182.4 %reduce-scatter.2.cloned.1.call-start = ((), (), s32[]{:S(2)}) async-start(), calls=%async_computation.9 | async-start | bytes 8912896 | tf_op jit(solution)/shard_map/reduce_scatter | solution.py:853
  615.3 70.8 %collective-permute-start.87 = (f32[2,64]{1,0:T(2,128)S(1)}, f32[2,64]{1,0:T(2,128)S(1)}, u32[]{:S(2)}, u32[]{:S(2)}) collective-permute-start(f32[2,64]{1,0:T(2,128)S(1)} %bitcast.356), channel_id=1, source_target_pairs={{0,1},{1,0},{2,3},{3,2},{4,5},{5,4},{6,7},{7,6},{8,9},{9,8},{10,11... | collective-permute-start | bytes 1544 | tf_op jit(solution)/shard_map/ppermute | solution.py:47
  624.3 34.1 %collective-permute-start.70 = (bf16[512,1024]{1,0:T(8,128)(2,1)}, bf16[512,1024]{1,0:T(8,128)(2,1)}, u32[]{:S(2)}, u32[]{:S(2)}) collective-permute-start(bf16[512,1024]{1,0:T(8,128)(2,1)} %get-tuple-element.378), channel_id=1, source_target_pairs={{0,1},{1,0},{2,3},{3,2},{4,5},{5,4},{6,7},{7,6},{8,9},{9,8},{10,11... | collective-permute-start | bytes 3145736 | tf_op jit(solution)/shard_map/ppermute | solution.py:60
  687.5 75.4 %all-to-all-start.3 = ((bf16[16,64,384]{2,1,0:T(8,128)(2,1)}), bf16[16,64,384]{2,1,0:T(8,128)(2,1)}, u32[]{:S(2)}, u32[]{:S(2)}) async-start(bf16[16,64,384]{2,1,0:T(8,128)(2,1)} %fusion.35), calls=%async_computation.4 | async-start | bytes 1572864 | tf_op jit(solution)/shard_map/all_to_all | solution.py:916
  709.2 33.7 %collective-permute-start.81 = (bf16[256,2048]{1,0:T(8,128)(2,1)S(1)}, bf16[256,2048]{1,0:T(8,128)(2,1)S(1)}, u32[]{:S(2)}, u32[]{:S(2)}) collective-permute-start(bf16[256,2048]{1,0:T(8,128)(2,1)S(1)} %slice.320), channel_id=1, source_target_pairs={{0,2},{2,0},{4,6},{6,4},{8,10},{10,8},{12,14},{14,12},{16,18},{18,... | collective-permute-start | bytes 3145736 | tf_op jit(solution)/shard_map/ppermute | solution.py:103
  711.9 31.0 %collective-permute-start.78 = (bf16[128,2048]{1,0:T(8,128)(2,1)S(1)}, bf16[128,2048]{1,0:T(8,128)(2,1)S(1)}, u32[]{:S(2)}, u32[]{:S(2)}) collective-permute-start(bf16[128,2048]{1,0:T(8,128)(2,1)S(1)} %get-tuple-element.454), channel_id=1, source_target_pairs={{0,8},{2,10},{4,12},{6,14},{8,16},{10,18},{12,20},{14,22},{1,9},{3... | collective-permute-start | bytes 1572872 | tf_op jit(solution)/shard_map/ppermute | solution.py:103
  748.8 28.6 %collective-permute-start.84 = (bf16[128,2048]{1,0:T(8,128)(2,1)}, bf16[128,2048]{1,0:T(8,128)(2,1)S(1)}, u32[]{:S(2)}, u32[]{:S(2)}) collective-permute-start(bf16[128,2048]{1,0:T(8,128)(2,1)} %get-tuple-element.478), channel_id=1, source_target_pairs={{8,0},{10,2},{12,4},{14,6},{16,8},{18,10},{20,12},{22,14},{24,16},... | collective-permute-start | bytes 1572872 | tf_op jit(solution)/shard_map/ppermute | solution.py:103
  750.1 28.1 %collective-permute-start.83 = (bf16[128,2048]{1,0:T(8,128)(2,1)}, bf16[128,2048]{1,0:T(8,128)(2,1)}, u32[]{:S(2)}, u32[]{:S(2)}) collective-permute-start(bf16[128,2048]{1,0:T(8,128)(2,1)} %get-tuple-element.479), channel_id=1, source_target_pairs={{0,8},{2,10},{4,12},{6,14},{8,16},{10,18},{12,20},{14,22},{16,24},... | collective-permute-start | bytes 1572872 | tf_op jit(solution)/shard_map/ppermute | solution.py:103
  (217 other events, 2660.2 us)
Sparse Core Ops, SparseCore 0:
  86.5 98.2 all-gather.3
  186.9 90.1 all-gather.5
  528.7 73.7 all-gather.7
  643.9 139.2 reduce-scatter.1
